TPU v7x, 32 devices: a whole 2x2x4 slice. The times are simulated.
32 devices in a mesh: ctx: 8 (over y, x, core), head: 4 (over z).
Axes of the slice: x: 2, y: 2, z: 4, core: 2. Of those that a mesh axis runs over, the one named last changes fastest.
Arguments:
- queries: bfloat16 [8192, 8192], P('ctx', 'head'), may hold values from -6 to 6
- key_rows: bfloat16 [8192, 8192], P('ctx', 'head'), may hold values from -6 to 6
- values: bfloat16 [8192, 8192], P('ctx', 'head'), may hold values from -32 to 32, as said below
- gate_input: bfloat16 [8192, 8192], P('ctx', 'head'), may hold values from -6 to 6
- norm_gain: float32 [8192], P('head'), may hold values from 0.1 to 1.9
- session_of: int32 [8], replicated, may hold values from 0 to 1, as said below
Outputs:
- attended: bfloat16 [8192, 8192], P('ctx', 'head')
Inputs may be any that keep to these rules, and one draw needn't show every extreme that they name: `session_of`: session numbers never fall along the blocks; one session holds exactly 6 consecutive blocks and the other the remaining 8 - 6. `values`: values are of order one to some tens.
All inputs are finite; a program needn't handle non-finite values.
Results may differ from a plain program's by a relative error of at most 0.0049.
Values sent between devices are 32-bit elements; how exact they have to be, the bound alone decides.
No kernel may reach another device: no remote copies, remote signals or barrier semaphores. Data moves between devices by JAX's collectives and lax.ppermute only.
A program may use at most 128 MiB of HBM per device.

v0:
```python
import jax
import jax.numpy as jnp
from jax import lax
from jax.sharding import PartitionSpec as P

HEADS = 64
HEAD_DIM = 128


def entering(part, axis, combine, identity):
    place = lax.axis_index(axis)
    gathered = jax.tree.map(lambda a: lax.all_gather(a, axis), part)
    state = jax.tree.map(lambda a, e: jnp.zeros_like(a) + jnp.asarray(e, a.dtype), part, identity)

    def one(lap, state):
        return combine(
            state, jax.tree.map(lambda a: lax.dynamic_index_in_dim(a, lap, 0, False), gathered)
        )

    return lax.fori_loop(0, place, one, state)


def on_device(queries, key_rows, values, gate_input, norm_gain, session_of):
    tokens_here = queries.shape[0]
    width = queries.shape[1]
    heads_here = width // HEAD_DIM

    def split_heads(matrix):
        return jnp.swapaxes(matrix.reshape(tokens_here, heads_here, HEAD_DIM), 0, 1)

    query_heads = split_heads(queries)
    key_heads = split_heads(key_rows)
    value_heads = split_heads(values)
    states = jnp.einsum("htd,hte->hde", key_heads, value_heads, preferred_element_type=jnp.float32)
    position = lax.axis_index("ctx")
    mine = session_of[position]
    before = session_of[jnp.maximum(position - 1, 0)]
    first = jnp.where(jnp.logical_or(position == 0, before != mine), 1.0, 0.0).astype(jnp.float32)

    def combine(earlier, later):
        return (later[0] + (1.0 - later[1]) * earlier[0], jnp.maximum(earlier[1], later[1]))

    identity = (jnp.zeros_like(states), jnp.zeros((), jnp.float32))
    carried, _ = entering((states, first), "ctx", combine, identity)
    prefix = carried * (1.0 - first)
    prefix = prefix.astype(jnp.bfloat16)
    places = jnp.arange(tokens_here)
    causal = places[:, None] >= places[None, :]

    def one_head(args):
        query_one, key_one, value_one, prefix_one = args
        scores = jnp.einsum("td,sd->ts", query_one, key_one, preferred_element_type=jnp.float32)
        scores = jnp.where(causal, scores, 0.0).astype(jnp.bfloat16)
        inner = jnp.dot(scores, value_one, preferred_element_type=jnp.float32)
        return inner + jnp.dot(query_one, prefix_one, preferred_element_type=jnp.float32)

    mixed = lax.map(one_head, (query_heads, key_heads, value_heads, prefix))
    mixed = jnp.swapaxes(mixed, 0, 1).reshape(tokens_here, width)
    partial_power = jnp.sum(mixed * mixed, axis=1)
    total_power = lax.psum(partial_power, "head")
    factor = lax.rsqrt(total_power / (HEADS * HEAD_DIM) + 1e-06)
    gated = (
        mixed
        * factor[:, None]
        * norm_gain[None, :]
        * jax.nn.sigmoid(gate_input.astype(jnp.float32))
    )
    return gated.astype(jnp.bfloat16)


def solution(mesh):
    return jax.shard_map(
        on_device,
        mesh=mesh,
        in_specs=(
            P("ctx", "head"),
            P("ctx", "head"),
            P("ctx", "head"),
            P("ctx", "head"),
            P("head"),
            P(),
        ),
        out_specs=P("ctx", "head"),
        check_vma=False,
    )
```

profile of v0, /device:TPU:7, one launch (start us, length us, event | category | flops | bytes accessed | tf_op | source)
XLA Modules:
  0.0 200.9 jit_solution(6904517233811465321)
XLA Ops:
  6.5 6.4 %copy.18 = bf16[1024,2048]{0,1:T(8,128)(2,1)} copy(bf16[1024,2048]{1,0:T(8,128)(2,1)} %param.11) | data formatting | bytes 8388608 | tf_op args[1]
  12.9 6.4 %copy.19 = bf16[1024,2048]{0,1:T(8,128)(2,1)} copy(bf16[1024,2048]{1,0:T(8,128)(2,1)} %param.12) | data formatting | bytes 8388608 | tf_op args[2]
  19.4 5.8 %fusion.28 = f32[16,128,128]{2,1,0:T(8,128)} fusion(bf16[16,1024,128]{1,2,0:T(8,128)(2,1)} %bitcast.73, bf16[16,1024,128]{1,2,0:T(8,128)(2,1)} %bitcast.75), kind=kOutput, calls=%fused_computation.30 | convolution fusion | flops 536870912 | bytes 9437184 | tf_op jit(solution)/shard_map/htd,hte->hde/dot_general | solution.py:34
  28.5 11.3 %all-reduce = f32[8]{0:T(128)S(1)} all-reduce(f32[8]{0:T(128)S(1)} %dynamic-update-slice), channel_id=1, replica_groups=mesh['ctx'=8,'head'=4] {'ctx'}, use_global_device_ids=true, to_apply=%add | all-reduce | flops 8 | bytes 64
  39.8 6.4 %copy.17 = bf16[1024,2048]{0,1:T(8,128)(2,1)} copy(bf16[1024,2048]{1,0:T(8,128)(2,1)} %param.10) | data formatting | bytes 8388608 | tf_op args[0]
  46.2 34.3 %all-gather.3.cloned.1.call-done = f32[128,128,128]{2,1,0:T(8,128)} async-done(((f32[16,128,128]{2,1,0:T(8,128)}), f32[128,128,128]{2,1,0:T(8,128)}) %all-gather.3.cloned.1.call-update) | async-done | bytes 8388624 | tf_op jit(solution)/shard_map/all_gather | solution.py:12
  80.6 19.7 %while.23 = (s32[]{:T(128)}, f32[16,128,128]{2,1,0:T(8,128)S(1)}, s32[]{:T(128)}, f32[8,16,128,128]{3,2,1,0:T(8,128)}, f32[8]{0:T(128)S(1)}, /*index=5*/s32[]{:T(128)}, s32[]{:T(128)}, s32[]{:T(128)}, f32[1]{0:T(128)}) while((s32[]{:T(128)}, f32[16,128,128]{2,1,0:T(8,128)S(1)}, s32[]{:T(128)}, f32[8,16,128,128]{3,2,1,0:T(8,128)}, ...), condition=%wide.region_1.2_spmd, body=%wide.region_0.1_spmd.sunk | while | flops 524294 | bytes 3145887 | solution.py:20
  100.4 72.7 %while.24 = (s32[]{:T(128)}, f32[16,1024,128]{2,1,0:T(8,128)}, bf16[16,1024,128]{1,2,0:T(8,128)(2,1)}, bf16[16,1024,128]{1,2,0:T(8,128)(2,1)}, bf16[16,1024,128]...) while((s32[]{:T(128)}, f32[16,1024,128]{2,1,0:T(8,128)}, ...), condition=%wide.region_3.4_spmd.clone, body=%wide.region_2.3_spmd.clone.sunk | while | flops 573702144 | bytes 2657357 | solution.py:57
  100.4 2.5 %fusion.44 = f32[1024,128]{1,0:T(8,128)S(1)} fusion(bf16[16,1024,128]{1,2,0:T(8,128)(2,1)} %get-tuple-element.252, s32[]{:T(128)} %get-tuple-element.241, bf16[16,1024,128]{1,2,0:T(8,128)(2,1)} %get-tuple-element.251, bf16[16,1024,128]{1,2,0:T(8,128)(2,1)} %get-tuple-element.250), kind=kOutput, calls=%fused_computation.4.clone.1 | convolution fusion | flops 540016640 | bytes 1312256 | tf_op jit(solution)/shard_map/while/body/eval_jaxpr/dot_general | solution.py:54
  102.9 2.1 %fusion.45 = f32[16,1024,128]{2,1,0:T(8,128)} fusion(f32[16,1024,128]{2,1,0:T(8,128)} %get-tuple-element.242, s32[]{:T(128)} %get-tuple-element.241, f32[1024,128]{1,0:T(8,128)S(1)} %fusion.44, bf16[16,1024,128]{1,2,0:T(8,128)(2,1)} %get-tuple-element.250, bf16[16,128,128]{2,1,0:T(8,128)(2,1)S(1)} %get-tuple-element.253), kind=kOutput, calls=%fused_computation.7.clone.1 | convolution fusion | flops 33685504 | bytes 1345024 | tf_op jit(solution)/shard_map/while/body/eval_jaxpr/dot_general | solution.py:55
  105.0 2.5 %fusion.44 = f32[1024,128]{1,0:T(8,128)S(1)} fusion(bf16[16,1024,128]{1,2,0:T(8,128)(2,1)} %get-tuple-element.252, s32[]{:T(128)} %get-tuple-element.241, bf16[16,1024,128]{1,2,0:T(8,128)(2,1)} %get-tuple-element.251, bf16[16,1024,128]{1,2,0:T(8,128)(2,1)} %get-tuple-element.250), kind=kOutput, calls=%fused_computation.4.clone.1 | convolution fusion | flops 540016640 | bytes 1312256 | tf_op jit(solution)/shard_map/while/body/eval_jaxpr/dot_general | solution.py:54
  107.5 2.1 %fusion.45 = f32[16,1024,128]{2,1,0:T(8,128)} fusion(f32[16,1024,128]{2,1,0:T(8,128)} %get-tuple-element.242, s32[]{:T(128)} %get-tuple-element.241, f32[1024,128]{1,0:T(8,128)S(1)} %fusion.44, bf16[16,1024,128]{1,2,0:T(8,128)(2,1)} %get-tuple-element.250, bf16[16,128,128]{2,1,0:T(8,128)(2,1)S(1)} %get-tuple-element.253), kind=kOutput, calls=%fused_computation.7.clone.1 | convolution fusion | flops 33685504 | bytes 1345024 | tf_op jit(solution)/shard_map/while/body/eval_jaxpr/dot_general | solution.py:55
  109.5 2.5 %fusion.44 = f32[1024,128]{1,0:T(8,128)S(1)} fusion(bf16[16,1024,128]{1,2,0:T(8,128)(2,1)} %get-tuple-element.252, s32[]{:T(128)} %get-tuple-element.241, bf16[16,1024,128]{1,2,0:T(8,128)(2,1)} %get-tuple-element.251, bf16[16,1024,128]{1,2,0:T(8,128)(2,1)} %get-tuple-element.250), kind=kOutput, calls=%fused_computation.4.clone.1 | convolution fusion | flops 540016640 | bytes 1312256 | tf_op jit(solution)/shard_map/while/body/eval_jaxpr/dot_general | solution.py:54
  114.1 2.5 %fusion.44 = f32[1024,128]{1,0:T(8,128)S(1)} fusion(bf16[16,1024,128]{1,2,0:T(8,128)(2,1)} %get-tuple-element.252, s32[]{:T(128)} %get-tuple-element.241, bf16[16,1024,128]{1,2,0:T(8,128)(2,1)} %get-tuple-element.251, bf16[16,1024,128]{1,2,0:T(8,128)(2,1)} %get-tuple-element.250), kind=kOutput, calls=%fused_computation.4.clone.1 | convolution fusion | flops 540016640 | bytes 1312256 | tf_op jit(solution)/shard_map/while/body/eval_jaxpr/dot_general | solution.py:54
  118.6 2.5 %fusion.44 = f32[1024,128]{1,0:T(8,128)S(1)} fusion(bf16[16,1024,128]{1,2,0:T(8,128)(2,1)} %get-tuple-element.252, s32[]{:T(128)} %get-tuple-element.241, bf16[16,1024,128]{1,2,0:T(8,128)(2,1)} %get-tuple-element.251, bf16[16,1024,128]{1,2,0:T(8,128)(2,1)} %get-tuple-element.250), kind=kOutput, calls=%fused_computation.4.clone.1 | convolution fusion | flops 540016640 | bytes 1312256 | tf_op jit(solution)/shard_map/while/body/eval_jaxpr/dot_general | solution.py:54
  123.2 2.5 %fusion.44 = f32[1024,128]{1,0:T(8,128)S(1)} fusion(bf16[16,1024,128]{1,2,0:T(8,128)(2,1)} %get-tuple-element.252, s32[]{:T(128)} %get-tuple-element.241, bf16[16,1024,128]{1,2,0:T(8,128)(2,1)} %get-tuple-element.251, bf16[16,1024,128]{1,2,0:T(8,128)(2,1)} %get-tuple-element.250), kind=kOutput, calls=%fused_computation.4.clone.1 | convolution fusion | flops 540016640 | bytes 1312256 | tf_op jit(solution)/shard_map/while/body/eval_jaxpr/dot_general | solution.py:54
  127.7 2.5 %fusion.44 = f32[1024,128]{1,0:T(8,128)S(1)} fusion(bf16[16,1024,128]{1,2,0:T(8,128)(2,1)} %get-tuple-element.252, s32[]{:T(128)} %get-tuple-element.241, bf16[16,1024,128]{1,2,0:T(8,128)(2,1)} %get-tuple-element.251, bf16[16,1024,128]{1,2,0:T(8,128)(2,1)} %get-tuple-element.250), kind=kOutput, calls=%fused_computation.4.clone.1 | convolution fusion | flops 540016640 | bytes 1312256 | tf_op jit(solution)/shard_map/while/body/eval_jaxpr/dot_general | solution.py:54
  132.2 2.5 %fusion.44 = f32[1024,128]{1,0:T(8,128)S(1)} fusion(bf16[16,1024,128]{1,2,0:T(8,128)(2,1)} %get-tuple-element.252, s32[]{:T(128)} %get-tuple-element.241, bf16[16,1024,128]{1,2,0:T(8,128)(2,1)} %get-tuple-element.251, bf16[16,1024,128]{1,2,0:T(8,128)(2,1)} %get-tuple-element.250), kind=kOutput, calls=%fused_computation.4.clone.1 | convolution fusion | flops 540016640 | bytes 1312256 | tf_op jit(solution)/shard_map/while/body/eval_jaxpr/dot_general | solution.py:54
  136.7 2.5 %fusion.44 = f32[1024,128]{1,0:T(8,128)S(1)} fusion(bf16[16,1024,128]{1,2,0:T(8,128)(2,1)} %get-tuple-element.252, s32[]{:T(128)} %get-tuple-element.241, bf16[16,1024,128]{1,2,0:T(8,128)(2,1)} %get-tuple-element.251, bf16[16,1024,128]{1,2,0:T(8,128)(2,1)} %get-tuple-element.250), kind=kOutput, calls=%fused_computation.4.clone.1 | convolution fusion | flops 540016640 | bytes 1312256 | tf_op jit(solution)/shard_map/while/body/eval_jaxpr/dot_general | solution.py:54
  139.2 2.0 %fusion.45 = f32[16,1024,128]{2,1,0:T(8,128)} fusion(f32[16,1024,128]{2,1,0:T(8,128)} %get-tuple-element.242, s32[]{:T(128)} %get-tuple-element.241, f32[1024,128]{1,0:T(8,128)S(1)} %fusion.44, bf16[16,1024,128]{1,2,0:T(8,128)(2,1)} %get-tuple-element.250, bf16[16,128,128]{2,1,0:T(8,128)(2,1)S(1)} %get-tuple-element.253), kind=kOutput, calls=%fused_computation.7.clone.1 | convolution fusion | flops 33685504 | bytes 1345024 | tf_op jit(solution)/shard_map/while/body/eval_jaxpr/dot_general | solution.py:55
  141.3 2.5 %fusion.44 = f32[1024,128]{1,0:T(8,128)S(1)} fusion(bf16[16,1024,128]{1,2,0:T(8,128)(2,1)} %get-tuple-element.252, s32[]{:T(128)} %get-tuple-element.241, bf16[16,1024,128]{1,2,0:T(8,128)(2,1)} %get-tuple-element.251, bf16[16,1024,128]{1,2,0:T(8,128)(2,1)} %get-tuple-element.250), kind=kOutput, calls=%fused_computation.4.clone.1 | convolution fusion | flops 540016640 | bytes 1312256 | tf_op jit(solution)/shard_map/while/body/eval_jaxpr/dot_general | solution.py:54
  143.8 2.0 %fusion.45 = f32[16,1024,128]{2,1,0:T(8,128)} fusion(f32[16,1024,128]{2,1,0:T(8,128)} %get-tuple-element.242, s32[]{:T(128)} %get-tuple-element.241, f32[1024,128]{1,0:T(8,128)S(1)} %fusion.44, bf16[16,1024,128]{1,2,0:T(8,128)(2,1)} %get-tuple-element.250, bf16[16,128,128]{2,1,0:T(8,128)(2,1)S(1)} %get-tuple-element.253), kind=kOutput, calls=%fused_computation.7.clone.1 | convolution fusion | flops 33685504 | bytes 1345024 | tf_op jit(solution)/shard_map/while/body/eval_jaxpr/dot_general | solution.py:55
  145.8 2.5 %fusion.44 = f32[1024,128]{1,0:T(8,128)S(1)} fusion(bf16[16,1024,128]{1,2,0:T(8,128)(2,1)} %get-tuple-element.252, s32[]{:T(128)} %get-tuple-element.241, bf16[16,1024,128]{1,2,0:T(8,128)(2,1)} %get-tuple-element.251, bf16[16,1024,128]{1,2,0:T(8,128)(2,1)} %get-tuple-element.250), kind=kOutput, calls=%fused_computation.4.clone.1 | convolution fusion | flops 540016640 | bytes 1312256 | tf_op jit(solution)/shard_map/while/body/eval_jaxpr/dot_general | solution.py:54
  150.4 2.5 %fusion.44 = f32[1024,128]{1,0:T(8,128)S(1)} fusion(bf16[16,1024,128]{1,2,0:T(8,128)(2,1)} %get-tuple-element.252, s32[]{:T(128)} %get-tuple-element.241, bf16[16,1024,128]{1,2,0:T(8,128)(2,1)} %get-tuple-element.251, bf16[16,1024,128]{1,2,0:T(8,128)(2,1)} %get-tuple-element.250), kind=kOutput, calls=%fused_computation.4.clone.1 | convolution fusion | flops 540016640 | bytes 1312256 | tf_op jit(solution)/shard_map/while/body/eval_jaxpr/dot_general | solution.py:54
  154.9 2.5 %fusion.44 = f32[1024,128]{1,0:T(8,128)S(1)} fusion(bf16[16,1024,128]{1,2,0:T(8,128)(2,1)} %get-tuple-element.252, s32[]{:T(128)} %get-tuple-element.241, bf16[16,1024,128]{1,2,0:T(8,128)(2,1)} %get-tuple-element.251, bf16[16,1024,128]{1,2,0:T(8,128)(2,1)} %get-tuple-element.250), kind=kOutput, calls=%fused_computation.4.clone.1 | convolution fusion | flops 540016640 | bytes 1312256 | tf_op jit(solution)/shard_map/while/body/eval_jaxpr/dot_general | solution.py:54
  157.4 2.0 %fusion.45 = f32[16,1024,128]{2,1,0:T(8,128)} fusion(f32[16,1024,128]{2,1,0:T(8,128)} %get-tuple-element.242, s32[]{:T(128)} %get-tuple-element.241, f32[1024,128]{1,0:T(8,128)S(1)} %fusion.44, bf16[16,1024,128]{1,2,0:T(8,128)(2,1)} %get-tuple-element.250, bf16[16,128,128]{2,1,0:T(8,128)(2,1)S(1)} %get-tuple-element.253), kind=kOutput, calls=%fused_computation.7.clone.1 | convolution fusion | flops 33685504 | bytes 1345024 | tf_op jit(solution)/shard_map/while/body/eval_jaxpr/dot_general | solution.py:55
  159.4 2.5 %fusion.44 = f32[1024,128]{1,0:T(8,128)S(1)} fusion(bf16[16,1024,128]{1,2,0:T(8,128)(2,1)} %get-tuple-element.252, s32[]{:T(128)} %get-tuple-element.241, bf16[16,1024,128]{1,2,0:T(8,128)(2,1)} %get-tuple-element.251, bf16[16,1024,128]{1,2,0:T(8,128)(2,1)} %get-tuple-element.250), kind=kOutput, calls=%fused_computation.4.clone.1 | convolution fusion | flops 540016640 | bytes 1312256 | tf_op jit(solution)/shard_map/while/body/eval_jaxpr/dot_general | solution.py:54
  164.0 2.5 %fusion.44 = f32[1024,128]{1,0:T(8,128)S(1)} fusion(bf16[16,1024,128]{1,2,0:T(8,128)(2,1)} %get-tuple-element.252, s32[]{:T(128)} %get-tuple-element.241, bf16[16,1024,128]{1,2,0:T(8,128)(2,1)} %get-tuple-element.251, bf16[16,1024,128]{1,2,0:T(8,128)(2,1)} %get-tuple-element.250), kind=kOutput, calls=%fused_computation.4.clone.1 | convolution fusion | flops 540016640 | bytes 1312256 | tf_op jit(solution)/shard_map/while/body/eval_jaxpr/dot_general | solution.py:54
  168.5 2.5 %fusion.44 = f32[1024,128]{1,0:T(8,128)S(1)} fusion(bf16[16,1024,128]{1,2,0:T(8,128)(2,1)} %get-tuple-element.252, s32[]{:T(128)} %get-tuple-element.241, bf16[16,1024,128]{1,2,0:T(8,128)(2,1)} %get-tuple-element.251, bf16[16,1024,128]{1,2,0:T(8,128)(2,1)} %get-tuple-element.250), kind=kOutput, calls=%fused_computation.4.clone.1 | convolution fusion | flops 540016640 | bytes 1312256 | tf_op jit(solution)/shard_map/while/body/eval_jaxpr/dot_general | solution.py:54
  173.0 4.0 %fusion.26 = f32[1024]{0:T(1024)S(1)} fusion(f32[16,1024,128]{2,1,0:T(8,128)} %get-tuple-element.87), kind=kLoop, calls=%fused_computation.26 | loop fusion | flops 4193280 | bytes 8392704 | tf_op jit(solution)/shard_map/reduce_sum | solution.py:59
  177.1 9.7 %psum.7 = f32[1024]{0:T(1024)S(1)} all-reduce(f32[1024]{0:T(1024)S(1)} %fusion.26), channel_id=1, replica_groups=mesh['ctx'=8,'head'=4] {'head'}, use_global_device_ids=true, to_apply=%region_5.6 | all-reduce | flops 1024 | bytes 8192 | tf_op jit(solution)/shard_map/psum | solution.py:60
  186.8 7.3 %fusion.25 = bf16[1024,2048]{1,0:T(8,128)(2,1)} fusion(bf16[1024,2048]{1,0:T(8,128)(2,1)} %param.13, f32[2048]{0:T(1024)S(1)} %copy-done, f32[1024]{0:T(1024)S(1)} %add_rsqrt_fusion, f32[16,1024,128]{2,1,0:T(8,128)} %get-tuple-element.87), kind=kLoop, calls=%fused_computation.24 | loop fusion | flops 16777216 | bytes 16789504 | tf_op jit(solution)/shard_map/convert_element_type | solution.py:68
  (41 shorter events, 39.9 us)
Async XLA Ops:
  6.5 73.9 %all-gather.3.cloned.1.call-start = ((), (), s32[]{:S(2)}) async-start(), calls=%async_computation | async-start | bytes 9437184 | tf_op jit(solution)/shard_map/all_gather | solution.py:12
  19.4 5.9 %copy-start.1 = (s32[8]{0:T(128)S(1)}, s32[8]{0:T(128)}, u32[]{:S(2)}) copy-start(s32[8]{0:T(128)} %param.15) | copy-start | bytes 100
  19.4 7.8 %copy-start.2 = (u32[32]{0:T(128)S(1)}, u32[32]{0:T(128)}, u32[]{:S(2)}) copy-start(u32[32]{0:T(128)} %constant.62) | copy-start | bytes 388
  173.0 13.8 %copy-start = (f32[2048]{0:T(1024)S(1)}, f32[2048]{0:T(1024)}, u32[]{:S(2)}) copy-start(f32[2048]{0:T(1024)} %param.14) | copy-start | bytes 24580
Sparse Core Ops, SparseCore 0:
  25.3 55.1 all-gather.2
where the time goes:
time: 203 us; the launch traced here: 201 us
  matrix products  78.4 us (39%)
  waiting for transfers between devices  34.3 us (17%)
  local copies, waits for them, and re-layouts  25.3 us (12%)
  other arithmetic  22.9 us (11%)
  blocking collectives  21.1 us (10%)
  between operations  14.7 us (7%)
  loops' own time  4.21 us (2%)
    dot_general x16, matrix products, one_head(): inner = jnp.dot(scores, value_one, preferred_element_type=jnp.float32)  40.1 us
    all_gather x1, waiting for transfers between devices, entering(): gathered = jax.tree.map(lambda a: lax.all_gather(a, axis), part)  34.3 us
    dot_general x16, matrix products, one_head(): jnp.dot(query_one, prefix_one, preferred_element_type=jnp.float32)  32.5 us
    unnamed x12, local copies, waits for them, and re-layouts  20.6 us
    add x7, other arithmetic, combine(): later[0] + (1.0 - later[1]) * earlier[0]  11.4 us
    unnamed x1, blocking collectives  11.3 us
    psum x1, blocking collectives, on_device(): total_power = lax.psum(partial_power, 'head')  9.72 us
    convert_element_type x1, other arithmetic, on_device(): return gated.astype(jnp.bfloat16)  7.31 us
  transfers between devices with their start and end apart: 1, of which 1 were waited for; matrix products, arithmetic and copies ran while one was open for 4% of the time, Pallas kernels for 0%

commit v1 on v0

v1 whole, which is shorter than its diff:
```python
import jax
import jax.numpy as jnp
from jax import lax
from jax.experimental import pallas as pl
from jax.experimental.pallas import tpu as pltpu
from jax.sharding import PartitionSpec as P

HEAD_DIM = 128
PAIR = 2 * HEAD_DIM
CHUNK = 256
MIB = 1024 * 1024
F32 = jnp.float32
BF16 = jnp.bfloat16


def params(mib):
    return pltpu.CompilerParams(vmem_limit_bytes=mib * MIB)


def dot_tn(a, b):
    return lax.dot_general(a, b, (((0,), (0,)), ((), ())), preferred_element_type=F32)


def dot_nt(a, b):
    return lax.dot_general(a, b, (((1,), (1,)), ((), ())), preferred_element_type=F32)


def dot_nn(a, b):
    return lax.dot_general(a, b, (((1,), (0,)), ((), ())), preferred_element_type=F32)


def states_kernel(first_ref, key_ref, value_ref, state_ref):
    for h in range(key_ref.shape[1] // HEAD_DIM):
        cols = slice(h * HEAD_DIM, (h + 1) * HEAD_DIM)
        state_ref[cols, :] = dot_tn(key_ref[:, cols], value_ref[:, cols])


def half_states(first, key_rows, values):
    tokens, width = key_rows.shape
    steps = width // 2 // PAIR
    block = pl.BlockSpec((tokens, PAIR), lambda i, first_ref: (0, first_ref[0] * steps + i))
    return pl.pallas_call(
        states_kernel,
        grid_spec=pltpu.PrefetchScalarGridSpec(
            num_scalar_prefetch=1,
            grid=(steps,),
            in_specs=[block, block],
            out_specs=pl.BlockSpec((PAIR, HEAD_DIM), lambda i, first_ref: (i, 0)),
        ),
        out_shape=jax.ShapeDtypeStruct((width // 2, HEAD_DIM), F32),
        compiler_params=params(16),
        cost_estimate=pl.CostEstimate(
            flops=tokens * width * HEAD_DIM, bytes_accessed=2 * tokens * width, transcendentals=0
        ),
        name="states",
    )(first, key_rows, values)


def inner_kernel(query_ref, key_ref, value_ref, inner_ref):
    tokens = query_ref.shape[0]
    rows_at = lax.broadcasted_iota(jnp.int32, (CHUNK, CHUNK), 0)
    cols_at = lax.broadcasted_iota(jnp.int32, (CHUNK, CHUNK), 1)
    causal = rows_at >= cols_at
    for h in range(query_ref.shape[1] // HEAD_DIM):
        cols = slice(h * HEAD_DIM, (h + 1) * HEAD_DIM)
        before = None
        for c in range(tokens // CHUNK):
            rows = slice(c * CHUNK, (c + 1) * CHUNK)
            query, key, value = query_ref[rows, cols], key_ref[rows, cols], value_ref[rows, cols]
            scores = jnp.where(causal, dot_nt(query, key), 0.0).astype(BF16)
            out = dot_nn(scores, value)
            if before is not None:
                out += dot_nn(query, before.astype(BF16))
            inner_ref[rows, cols] = out
            if c + 1 < tokens // CHUNK:
                state = dot_tn(key, value)
                before = state if before is None else before + state


def inner_part(queries, key_rows, values, part, parts):
    tokens, width = queries.shape
    steps = width // parts // PAIR
    block = pl.BlockSpec((tokens, PAIR), lambda i: (0, part * steps + i))
    return pl.pallas_call(
        inner_kernel,
        grid=(steps,),
        in_specs=[block, block, block],
        out_specs=pl.BlockSpec((tokens, PAIR), lambda i: (0, i)),
        out_shape=jax.ShapeDtypeStruct((tokens, width // parts), F32),
        compiler_params=params(24),
        cost_estimate=pl.CostEstimate(
            flops=tokens * width // parts * 6 * CHUNK,
            bytes_accessed=10 * tokens * width // parts,
            transcendentals=0,
        ),
        name="inner",
    )(queries, key_rows, values)


def mixed_kernel(query_ref, inner_ref, prefix_ref, mixed_ref, power_ref, total_ref):
    step = pl.program_id(0)
    squares = None
    for h in range(query_ref.shape[1] // HEAD_DIM):
        cols = slice(h * HEAD_DIM, (h + 1) * HEAD_DIM)
        mixed = inner_ref[:, cols] + dot_nn(query_ref[:, cols], prefix_ref[cols, :].astype(BF16))
        mixed_ref[:, cols] = mixed
        square = mixed * mixed
        squares = square if squares is None else squares + square

    @pl.when(step == 0)
    def _():
        total_ref[...] = squares

    @pl.when(step > 0)
    def _():
        total_ref[...] += squares

    @pl.when(step == pl.num_programs(0) - 1)
    def _():
        power_ref[...] = jnp.sum(jnp.transpose(total_ref[...]), axis=0, keepdims=True)


def mix(queries, inner, prefix):
    tokens, width = queries.shape
    block = pl.BlockSpec((tokens, PAIR), lambda i: (0, i))
    return pl.pallas_call(
        mixed_kernel,
        grid=(width // PAIR,),
        in_specs=[block, block, pl.BlockSpec((PAIR, HEAD_DIM), lambda i: (i, 0))],
        out_specs=[block, pl.BlockSpec((1, tokens), lambda i: (0, 0))],
        out_shape=[
            jax.ShapeDtypeStruct((tokens, width), F32),
            jax.ShapeDtypeStruct((1, tokens), F32),
        ],
        scratch_shapes=[pltpu.VMEM((tokens, HEAD_DIM), F32)],
        compiler_params=params(24),
        cost_estimate=pl.CostEstimate(
            flops=2 * tokens * width * HEAD_DIM, bytes_accessed=10 * tokens * width, transcendentals=0
        ),
        name="mix",
    )(queries, inner, prefix)


def gate_kernel(mixed_ref, gate_ref, gain_ref, gated_ref):
    gate = gate_ref[...].astype(F32)
    gated_ref[...] = mixed_ref[...] * gain_ref[...] * jax.nn.sigmoid(gate)


def gate(mixed, gate_input, norm_gain):
    tokens, width = mixed.shape
    block = pl.BlockSpec((tokens, PAIR), lambda i: (0, i))
    return pl.pallas_call(
        gate_kernel,
        grid=(width // PAIR,),
        in_specs=[block, block, pl.BlockSpec((1, PAIR), lambda i: (0, i))],
        out_specs=block,
        out_shape=jax.ShapeDtypeStruct((tokens, width), F32),
        compiler_params=params(24),
        cost_estimate=pl.CostEstimate(
            flops=8 * tokens * width, bytes_accessed=10 * tokens * width, transcendentals=tokens * width
        ),
        name="gate",
    )(mixed, gate_input, norm_gain.reshape(1, width))


def scale_kernel(features, gated_ref, power_ref, out_ref):
    power = jnp.broadcast_to(power_ref[...], (HEAD_DIM, power_ref.shape[1]))
    factor = lax.rsqrt(jnp.transpose(power) / features + 1e-06)
    for h in range(gated_ref.shape[1] // HEAD_DIM):
        cols = slice(h * HEAD_DIM, (h + 1) * HEAD_DIM)
        out_ref[:, cols] = (gated_ref[:, cols] * factor).astype(BF16)


def scale(gated, power, features):
    tokens, width = gated.shape
    rows = tokens // 8
    block = pl.BlockSpec((rows, width), lambda i: (i, 0))
    return pl.pallas_call(
        lambda *refs: scale_kernel(features, *refs),
        grid=(tokens // rows,),
        in_specs=[block, pl.BlockSpec((1, rows), lambda i: (0, i))],
        out_specs=block,
        out_shape=jax.ShapeDtypeStruct((tokens, width), BF16),
        compiler_params=params(24),
        cost_estimate=pl.CostEstimate(
            flops=2 * tokens * width, bytes_accessed=6 * tokens * width, transcendentals=0
        ),
        name="scale",
    )(gated, power)


def swap(count, bit):
    return [(i, i ^ bit) for i in range(count)]


def chip_prefix(keep, send, session_of, blocks):
    place = lax.axis_index("ctx")
    core = place % 2
    chip = place // 2

    def flag(condition):
        return jnp.where(condition, 1.0, 0.0).astype(F32)

    def first_of(c):
        return session_of[2 * c]

    def last_of(c):
        return session_of[2 * c + 1]

    def need(dest, source):
        return flag(jnp.logical_and(source < dest, first_of(dest) == last_of(source)))

    whole = flag(first_of(chip) == last_of(chip))
    got = lax.ppermute(send, "ctx", swap(blocks, 1))
    own_weight = jnp.where(core == 0, whole, 1.0)
    got_weight = jnp.where(core == 0, 1.0, whole)
    chip_sum = own_weight * keep + got_weight * got
    return core, chip, need, whole, got, chip_sum


def on_device(blocks, features, queries, key_rows, values, gate_input, norm_gain, session_of):
    tokens, width = queries.shape
    place = lax.axis_index("ctx")
    core = place % 2
    as_index = core.astype(jnp.int32).reshape(1)
    send = half_states(1 - as_index, key_rows, values)
    keep = half_states(as_index, key_rows, values)
    core, chip, need, whole, got, chip_sum = chip_prefix(keep, send, session_of, blocks)
    inner = inner_part(queries, key_rows, values, 0, 1)

    if blocks == 8:
        first_step = [(i, i ^ (2 if i % 2 == 0 else 4)) for i in range(blocks)]
        second_step = [(i, i ^ (4 if i % 2 == 0 else 2)) for i in range(blocks)]
        partner = jnp.where(core == 0, chip ^ 1, chip ^ 2)
        dest = jnp.where(core == 0, chip ^ 2, chip ^ 1)
        there = lax.ppermute(chip_sum, "ctx", first_step)
        onward = need(dest, chip) * chip_sum + need(dest, partner) * there
        mine = need(chip, partner) * there
        prefix = mine + lax.ppermute(onward, "ctx", second_step)
    else:
        total = chip_sum
        prefix = jnp.zeros_like(chip_sum)
        bit = 1
        while 2 * bit < blocks:
            there = lax.ppermute(total, "ctx", swap(blocks, 2 * bit))
            partner = chip ^ bit
            lower = partner < chip
            last_here = chip | (bit - 1)
            last_there = partner | (bit - 1)
            same_group_end = session_of[2 * last_here + 1] == session_of[2 * last_there + 1]
            reaches = session_of[2 * last_there + 1] == session_of[2 * chip]
            prefix = prefix + jnp.where(jnp.logical_and(lower, reaches), 1.0, 0.0) * there
            joined = jnp.where(same_group_end, 1.0, 0.0)
            total = jnp.where(lower, total + joined * there, joined * total + there)
            bit *= 2

    back = prefix + jnp.where(core == 0, 1.0, 0.0) * keep
    other = lax.ppermute(back, "ctx", swap(blocks, 1))
    mine = jnp.where(core == 0, 1.0, whole) * (prefix + jnp.where(core == 0, 0.0, 1.0) * got)
    other = jnp.where(core == 0, 1.0, whole) * other
    low = jnp.where(core == 0, mine, other)
    high = jnp.where(core == 0, other, mine)
    prefix = jnp.concatenate([low, high], axis=0).astype(BF16)

    mixed, power = mix(queries, inner, prefix)
    count = features // width
    bit = 1
    while bit < count:
        power = power + lax.ppermute(power, "head", swap(count, bit))
        bit *= 2
    gated = gate(mixed, gate_input, norm_gain)
    return scale(gated, power, features)


def solution(mesh):
    blocks = mesh.shape["ctx"]

    def whole(queries, key_rows, values, gate_input, norm_gain, session_of):
        features = queries.shape[1]
        return jax.shard_map(
            lambda *args: on_device(blocks, features, *args),
            mesh=mesh,
            in_specs=(
                P("ctx", "head"),
                P("ctx", "head"),
                P("ctx", "head"),
                P("ctx", "head"),
                P("head"),
                P(),
            ),
            out_specs=P("ctx", "head"),
            check_vma=False,
        )(queries, key_rows, values, gate_input, norm_gain, session_of)

    return whole
```

time: 203 us -> 72.6 us (0.36)
  the two profiles are of different devices: /device:TPU:7 before, /device:TPU:0 now
where the time goes in v1:
time: 72.6 us; the launch traced here: 72.2 us
  Pallas kernels  27.8 us (38%)
  local copies, waits for them, and re-layouts  16 us (22%)
  waiting for transfers between devices  12 us (17%)
  starting transfers between devices  10.5 us (14%)
  between operations  5.33 us (7%)
    unnamed x20, local copies, waits for them, and re-layouts  15.3 us
    pallas_call x1, Pallas kernels, inner_part(): pl.pallas_call(inner_kernel, grid=(steps,), in_specs=[block, block, block...  11.6 us
    ppermute x1, waiting for transfers between devices, on_device(): prefix = mine + lax.ppermute(onward, 'ctx', second_step)  5.77 us
    ppermute x2, starting transfers between devices, on_device(): power = power + lax.ppermute(power, 'head', swap(count, bit))  5.18 us
    pallas_call x1, Pallas kernels, mix(): pl.pallas_call(mixed_kernel, grid=(width // PAIR,), in_specs=[block, bloc...  4.82 us
    ppermute x1, waiting for transfers between devices, on_device(): there = lax.ppermute(chip_sum, 'ctx', first_step)  4.65 us
    pallas_call x2, Pallas kernels, half_states(): pl.pallas_call(states_kernel, grid_spec=pltpu.PrefetchScalarGridSpec(num_...  4.06 us
    pallas_call x1, Pallas kernels, scale(): pl.pallas_call(lambda *refs: scale_kernel(features, *refs), grid=(tokens...  4.02 us
  transfers between devices with their start and end apart: 6, of which 3 were waited for; matrix products, arithmetic and copies ran while one was open for 1% of the time, Pallas kernels for 23%

profile of v1, /device:TPU:0, one launch (start us, length us, event | category | flops | bytes accessed | tf_op | source)
XLA Modules:
  0.0 72.2 jit_solution(277117608265576506)
XLA Ops:
  0.0 2.2 %copy-done = bf16[1024,2048]{1,0:T(8,128)(2,1)S(1)} copy-done((bf16[1024,2048]{1,0:T(8,128)(2,1)S(1)}, bf16[1024,2048]{1,0:T(8,128)(2,1)}, u32[]{:S(2)}) %copy-start) | copy-done | bytes 4194328
  2.2 2.2 %copy-done.3 = bf16[1024,2048]{1,0:T(8,128)(2,1)S(1)} copy-done((bf16[1024,2048]{1,0:T(8,128)(2,1)S(1)}, bf16[1024,2048]{1,0:T(8,128)(2,1)}, u32[]{:S(2)}) %copy-start.3) | copy-done | bytes 4194328
  4.4 2.0 %states.3 = f32[1024,128]{1,0:T(8,128)S(1)} custom-call(s32[1]{0:T(128)S(6)} %sub.8.first_ref, bf16[1024,2048]{1,0:T(8,128)(2,1)S(1)} %copy-done, bf16[1024,2048]{1,0:T(8,128)(2,1)S(1)} %copy-done.3), custom_call_target="tpu_custom_call" | custom-call | flops 268435456 | bytes 4194304 | tf_op jit(solution)/shard_map/states/pallas_call | solution.py:42
  6.4 0.5 collective-permute-start
  6.9 0.7 fusion
  8.9 0.0 copy-start.1
  8.9 2.2 %copy-done.1 = bf16[1024,2048]{1,0:T(8,128)(2,1)S(1)} copy-done((bf16[1024,2048]{1,0:T(8,128)(2,1)S(1)}, bf16[1024,2048]{1,0:T(8,128)(2,1)}, u32[]{:S(2)}) %copy-start.1) | copy-done | bytes 4194328
  11.1 2.2 %copy-done.4 = bf16[1024,2048]{1,0:T(8,128)(2,1)S(1)} copy-done((bf16[1024,2048]{1,0:T(8,128)(2,1)S(1)}, bf16[1024,2048]{1,0:T(8,128)(2,1)}, u32[]{:S(2)}) %copy-start.4) | copy-done | bytes 4194328
  13.3 2.0 %states.2 = f32[1024,128]{1,0:T(8,128)S(1)} custom-call(s32[1]{0:T(128)} %bitcast.2.first_ref, bf16[1024,2048]{1,0:T(8,128)(2,1)S(1)} %copy-done.1, bf16[1024,2048]{1,0:T(8,128)(2,1)S(1)} %copy-done.4), custom_call_target="tpu_custom_call" | custom-call | flops 268435456 | bytes 4194304 | tf_op jit(solution)/shard_map/states/pallas_call | solution.py:42
  15.3 0.1 multiply_add_fusion.3
  15.4 2.6 %collective-permute-start.1 = (f32[1024,128]{1,0:T(8,128)S(1)}, f32[1024,128]{1,0:T(8,128)S(1)}, u32[]{:S(2)}, u32[]{:S(2)}) collective-permute-start(f32[1024,128]{1,0:T(8,128)S(1)} %multiply_add_fusion.3), channel_id=1, source_target_pairs={{0,8},{4,20},{8,0},{12,28},{16,24},{20,4},{24,16},{28,12},{1,9},{5... | collective-permute-start | bytes 1572872 | tf_op jit(solution)/shard_map/ppermute | solution.py:236
  20.5 4.7 %collective-permute-done.1 = f32[1024,128]{1,0:T(8,128)S(1)} collective-permute-done((f32[1024,128]{1,0:T(8,128)S(1)}, f32[1024,128]{1,0:T(8,128)S(1)}, u32[]{:S(2)}, u32[]{:S(2)}) %collective-permute-start.1) | collective-permute-done | bytes 524320 | tf_op jit(solution)/shard_map/ppermute | solution.py:236
  25.2 0.1 multiply_add_fusion.1
  25.2 2.1 %collective-permute-start.2 = (f32[1024,128]{1,0:T(8,128)S(1)}, f32[1024,128]{1,0:T(8,128)S(1)}, u32[]{:S(2)}, u32[]{:S(2)}) collective-permute-start(f32[1024,128]{1,0:T(8,128)S(1)} %multiply_add_fusion.1), channel_id=1, source_target_pairs={{0,16},{4,12},{8,24},{12,4},{16,0},{20,28},{24,8},{28,20},{1,17},{... | collective-permute-start | bytes 1572872 | tf_op jit(solution)/shard_map/ppermute | solution.py:239
  28.7 5.8 %collective-permute-done.2 = f32[1024,128]{1,0:T(8,128)S(1)} collective-permute-done((f32[1024,128]{1,0:T(8,128)S(1)}, f32[1024,128]{1,0:T(8,128)S(1)}, u32[]{:S(2)}, u32[]{:S(2)}) %collective-permute-start.2) | collective-permute-done | bytes 524320 | tf_op jit(solution)/shard_map/ppermute | solution.py:239
  34.5 0.1 multiply_add_fusion
  34.6 0.1 collective-permute-start.3
  34.7 0.0 copy-start.2
  34.7 2.2 %copy-done.2 = bf16[1024,2048]{1,0:T(8,128)(2,1)S(1)} copy-done((bf16[1024,2048]{1,0:T(8,128)(2,1)S(1)}, bf16[1024,2048]{1,0:T(8,128)(2,1)}, u32[]{:S(2)}) %copy-start.2) | copy-done | bytes 4194328
  36.9 2.2 %copy-done.5 = bf16[1024,2048]{1,0:T(8,128)(2,1)S(1)} copy-done((bf16[1024,2048]{1,0:T(8,128)(2,1)S(1)}, bf16[1024,2048]{1,0:T(8,128)(2,1)}, u32[]{:S(2)}) %copy-start.5) | copy-done | bytes 4194328
  39.1 2.2 %copy-done.6 = bf16[1024,2048]{1,0:T(8,128)(2,1)S(1)} copy-done((bf16[1024,2048]{1,0:T(8,128)(2,1)S(1)}, bf16[1024,2048]{1,0:T(8,128)(2,1)}, u32[]{:S(2)}) %copy-start.6) | copy-done | bytes 4194328
  41.2 11.6 %inner.1.inner_ref = f32[1024,2048]{1,0:T(8,128)S(1)} custom-call(bf16[1024,2048]{1,0:T(8,128)(2,1)S(1)} %copy-done.6, bf16[1024,2048]{1,0:T(8,128)(2,1)S(1)} %copy-done.2, bf16[1024,2048]{1,0:T(8,128)(2,1)S(1)} %copy-done.5), custom_call_target="tpu_custom_call" | custom-call | flops 3221225472 | bytes 20971520 | tf_op jit(solution)/shard_map/inner/pallas_call | solution.py:84
  52.8 0.2 select_convert_fusion.1
  53.0 0.1 select_convert_fusion
  53.2 0.0 copy-start.7
  53.2 0.0 copy-start.8
  53.2 4.8 %mix.1 = (f32[1024,2048]{1,0:T(8,128)S(1)}, f32[1,1024]{1,0:T(1,128)S(1)}) custom-call(bf16[1024,2048]{1,0:T(8,128)(2,1)S(1)} %copy-done.6, f32[1024,2048]{1,0:T(8,128)S(1)} %inner.1.inner_ref, bf16[2048,128]{1,0:T(8,128)(2,1)S(1)} %pad_maximum_fusion.prefix_ref), custom_call_target="tpu_custom_call" | custom-call | flops 536870912 | bytes 20971520 | tf_op jit(solution)/shard_map/mix/pallas_call | solution.py:126
  58.0 2.1 %collective-permute-start.4 = (f32[1,1024]{1,0:T(1,128)S(1)}, f32[1,1024]{1,0:T(1,128)S(1)}, u32[]{:S(2)}, u32[]{:S(2)}) collective-permute-start(f32[1,1024]{1,0:T(1,128)S(1)} %get-tuple-element.8), channel_id=1, source_target_pairs={{0,1},{1,0},{2,3},{3,2},{4,5},{5,4},{6,7},{7,6},{8,9},{9,8},{10,11... | collective-permute-start | bytes 12296 | tf_op jit(solution)/shard_map/ppermute | solution.py:269
  60.2 1.6 %collective-permute-done.4 = f32[1,1024]{1,0:T(1,128)S(1)} collective-permute-done((f32[1,1024]{1,0:T(1,128)S(1)}, f32[1,1024]{1,0:T(1,128)S(1)}, u32[]{:S(2)}, u32[]{:S(2)}) %collective-permute-start.4) | collective-permute-done | bytes 4128 | tf_op jit(solution)/shard_map/ppermute | solution.py:269
  61.7 3.0 %collective-permute-start.5 = (f32[1,1024]{1,0:T(1,128)S(1)}, f32[1,1024]{1,0:T(1,128)S(1)}, u32[]{:S(2)}, u32[]{:S(2)}) collective-permute-start(f32[1,1024]{1,0:T(1,128)S(1)} %add.67), channel_id=1, source_target_pairs={{0,2},{1,3},{2,0},{3,1},{4,6},{5,7},{6,4},{7,5},{8,10},{9,11},{10,... | collective-permute-start | bytes 12296 | tf_op jit(solution)/shard_map/ppermute | solution.py:269
  64.8 3.3 %gate.1.refs_0_ = f32[1024,2048]{1,0:T(8,128)S(1)} custom-call(f32[1024,2048]{1,0:T(8,128)S(1)} %get-tuple-element.7.mixed_ref, bf16[1024,2048]{1,0:T(8,128)(2,1)S(1)} %copy-done.7, f32[1,2048]{1,0:T(1,128)S(1)} %bitcast.6), custom_call_target="tpu_custom_call" | custom-call | flops 16777216 | bytes 20971520 | tf_op jit(solution)/shard_map/gate/pallas_call | solution.py:152
  68.2 4.0 %scale.1 = bf16[1024,2048]{1,0:T(8,128)(2,1)} custom-call(f32[1024,2048]{1,0:T(8,128)S(1)} %gate.1.refs_0_, f32[1,1024]{1,0:T(1,128)S(1)} %add.68.refs_1_), custom_call_target="tpu_custom_call" | custom-call | flops 4194304 | bytes 12582912 | tf_op jit(solution)/shard_map/scale/pallas_call | solution.py:178
  (15 shorter events, 0.1 us)
Async XLA Ops:
  0.0 2.2 %copy-start = (bf16[1024,2048]{1,0:T(8,128)(2,1)S(1)}, bf16[1024,2048]{1,0:T(8,128)(2,1)}, u32[]{:S(2)}) copy-start(bf16[1024,2048]{1,0:T(8,128)(2,1)} %key_ref.5) | copy-start | bytes 12582916
  2.2 2.2 %copy-start.3 = (bf16[1024,2048]{1,0:T(8,128)(2,1)S(1)}, bf16[1024,2048]{1,0:T(8,128)(2,1)}, u32[]{:S(2)}) copy-start(bf16[1024,2048]{1,0:T(8,128)(2,1)} %value_ref.5) | copy-start | bytes 12582916
  4.4 2.6 %copy-start.9 = (s32[8]{0:T(128)S(1)}, s32[8]{0:T(128)}, u32[]{:S(2)}) copy-start(s32[8]{0:T(128)} %param.11) | copy-start | bytes 100
  6.4 8.9 %collective-permute-start = (f32[1024,128]{1,0:T(8,128)S(1)}, f32[1024,128]{1,0:T(8,128)S(1)}, u32[]{:S(2)}, u32[]{:S(2)}) collective-permute-start(f32[1024,128]{1,0:T(8,128)S(1)} %states.3), channel_id=1, source_target_pairs={{0,4},{4,0},{8,12},{12,8},{16,20},{20,16},{24,28},{28,24},{1,5},{5... | collective-permute-start | bytes 1572872 | tf_op jit(solution)/shard_map/ppermute | solution.py:214
  8.9 2.2 %copy-start.1 = (bf16[1024,2048]{1,0:T(8,128)(2,1)S(1)}, bf16[1024,2048]{1,0:T(8,128)(2,1)}, u32[]{:S(2)}) copy-start(bf16[1024,2048]{1,0:T(8,128)(2,1)} %key_ref.5) | copy-start | bytes 12582916
  11.1 2.2 %copy-start.4 = (bf16[1024,2048]{1,0:T(8,128)(2,1)S(1)}, bf16[1024,2048]{1,0:T(8,128)(2,1)}, u32[]{:S(2)}) copy-start(bf16[1024,2048]{1,0:T(8,128)(2,1)} %value_ref.5) | copy-start | bytes 12582916
  15.4 9.8 %collective-permute-start.1 = (f32[1024,128]{1,0:T(8,128)S(1)}, f32[1024,128]{1,0:T(8,128)S(1)}, u32[]{:S(2)}, u32[]{:S(2)}) collective-permute-start(f32[1024,128]{1,0:T(8,128)S(1)} %multiply_add_fusion.3), channel_id=1, source_target_pairs={{0,8},{4,20},{8,0},{12,28},{16,24},{20,4},{24,16},{28,12},{1,9},{5... | collective-permute-start | bytes 1572872 | tf_op jit(solution)/shard_map/ppermute | solution.py:236
  25.2 9.3 %collective-permute-start.2 = (f32[1024,128]{1,0:T(8,128)S(1)}, f32[1024,128]{1,0:T(8,128)S(1)}, u32[]{:S(2)}, u32[]{:S(2)}) collective-permute-start(f32[1024,128]{1,0:T(8,128)S(1)} %multiply_add_fusion.1), channel_id=1, source_target_pairs={{0,16},{4,12},{8,24},{12,4},{16,0},{20,28},{24,8},{28,20},{1,17},{... | collective-permute-start | bytes 1572872 | tf_op jit(solution)/shard_map/ppermute | solution.py:239
  34.6 18.3 %collective-permute-start.3 = (f32[1024,128]{1,0:T(8,128)S(1)}, f32[1024,128]{1,0:T(8,128)S(1)}, u32[]{:S(2)}, u32[]{:S(2)}) collective-permute-start(f32[1024,128]{1,0:T(8,128)S(1)} %multiply_add_fusion), channel_id=1, source_target_pairs={{0,4},{4,0},{8,12},{12,8},{16,20},{20,16},{24,28},{28,24},{1,5},{5... | collective-permute-start | bytes 1572872 | tf_op jit(solution)/shard_map/ppermute | solution.py:258
  34.7 2.2 %copy-start.2 = (bf16[1024,2048]{1,0:T(8,128)(2,1)S(1)}, bf16[1024,2048]{1,0:T(8,128)(2,1)}, u32[]{:S(2)}) copy-start(bf16[1024,2048]{1,0:T(8,128)(2,1)} %key_ref.5) | copy-start | bytes 12582916
  36.9 2.2 %copy-start.5 = (bf16[1024,2048]{1,0:T(8,128)(2,1)S(1)}, bf16[1024,2048]{1,0:T(8,128)(2,1)}, u32[]{:S(2)}) copy-start(bf16[1024,2048]{1,0:T(8,128)(2,1)} %value_ref.5) | copy-start | bytes 12582916
  39.0 2.2 %copy-start.6 = (bf16[1024,2048]{1,0:T(8,128)(2,1)S(1)}, bf16[1024,2048]{1,0:T(8,128)(2,1)}, u32[]{:S(2)}) copy-start(bf16[1024,2048]{1,0:T(8,128)(2,1)} %query_ref.3) | copy-start | bytes 12582916
  53.2 11.6 %copy-start.7 = (bf16[1024,2048]{1,0:T(8,128)(2,1)S(1)}, bf16[1024,2048]{1,0:T(8,128)(2,1)}, u32[]{:S(2)}) copy-start(bf16[1024,2048]{1,0:T(8,128)(2,1)} %gate_ref.1) | copy-start | bytes 12582916
  53.2 11.6 %copy-start.8 = (f32[2048]{0:T(1024)S(1)}, f32[2048]{0:T(1024)}, u32[]{:S(2)}) copy-start(f32[2048]{0:T(1024)} %param.10) | copy-start | bytes 24580
  58.0 3.7 %collective-permute-start.4 = (f32[1,1024]{1,0:T(1,128)S(1)}, f32[1,1024]{1,0:T(1,128)S(1)}, u32[]{:S(2)}, u32[]{:S(2)}) collective-permute-start(f32[1,1024]{1,0:T(1,128)S(1)} %get-tuple-element.8), channel_id=1, source_target_pairs={{0,1},{1,0},{2,3},{3,2},{4,5},{5,4},{6,7},{7,6},{8,9},{9,8},{10,11... | collective-permute-start | bytes 12296 | tf_op jit(solution)/shard_map/ppermute | solution.py:269
  61.7 6.4 %collective-permute-start.5 = (f32[1,1024]{1,0:T(1,128)S(1)}, f32[1,1024]{1,0:T(1,128)S(1)}, u32[]{:S(2)}, u32[]{:S(2)}) collective-permute-start(f32[1,1024]{1,0:T(1,128)S(1)} %add.67), channel_id=1, source_target_pairs={{0,2},{1,3},{2,0},{3,1},{4,6},{5,7},{6,4},{7,5},{8,10},{9,11},{10,... | collective-permute-start | bytes 12296 | tf_op jit(solution)/shard_map/ppermute | solution.py:269

commit v2 on v0

v2 whole, which is shorter than its diff:
```python
import jax
import jax.numpy as jnp
from jax import lax
from jax.experimental import pallas as pl
from jax.experimental.pallas import tpu as pltpu
from jax.sharding import PartitionSpec as P

HEAD_DIM = 128
CHUNK = 256
MIB = 1024 * 1024
F32 = jnp.float32
BF16 = jnp.bfloat16
WHOLE = pl.BlockSpec(memory_space=pltpu.VMEM)
SCALARS = pl.BlockSpec(memory_space=pltpu.SMEM)
ANYWHERE = pl.BlockSpec(memory_space=pl.ANY)


def params(mib):
    return pltpu.CompilerParams(vmem_limit_bytes=mib * MIB)


def in_hbm(x):
    return pltpu.with_memory_space_constraint(x, pltpu.HBM)


def in_vmem(x):
    return pltpu.with_memory_space_constraint(x, pltpu.VMEM)


def cost(flops, bytes_accessed):
    return pl.CostEstimate(flops=flops, bytes_accessed=bytes_accessed, transcendentals=0)


def dot_tn(a, b):
    return lax.dot_general(a, b, (((0,), (0,)), ((), ())), preferred_element_type=F32)


def dot_nt(a, b):
    return lax.dot_general(a, b, (((1,), (1,)), ((), ())), preferred_element_type=F32)


def dot_nn(a, b):
    return lax.dot_general(a, b, (((1,), (0,)), ((), ())), preferred_element_type=F32)


def head(h):
    return slice(h * HEAD_DIM, (h + 1) * HEAD_DIM)


def chunk(c):
    return slice(c * CHUNK, (c + 1) * CHUNK)


def columns(place_ref, mine, half):
    core = place_ref[0] & 1
    return pl.ds(pl.multiple_of((core if mine else 1 - core) * half, half), half)


def states_kernel(mine, place_ref, key_ref, value_ref, state_ref, before_ref, keys, vals, sems):
    tokens, half = keys.shape
    cols = columns(place_ref, mine, half)
    copies = []
    for c in range(tokens // CHUNK):
        for j, (source, to) in enumerate(((key_ref, keys), (value_ref, vals))):
            copies.append(pltpu.make_async_copy(source.at[chunk(c), cols], to.at[chunk(c), :], sems.at[2 * c + j]))
            copies[-1].start()
    for c in range(tokens // CHUNK):
        copies[2 * c].wait()
        copies[2 * c + 1].wait()
        for h in range(half // HEAD_DIM):
            new = dot_tn(keys[chunk(c), head(h)], vals[chunk(c), head(h)])
            if c == 0:
                state_ref[head(h), :] = new
            else:
                old = state_ref[head(h), :]
                at = (c - 1) * half + h * HEAD_DIM
                before_ref[at : at + HEAD_DIM, :] = old.astype(BF16)
                state_ref[head(h), :] = old + new


def half_states(place, key_rows, values, mine):
    tokens, width = key_rows.shape
    half = width // 2
    chunks = tokens // CHUNK
    return pl.pallas_call(
        lambda *refs: states_kernel(mine, *refs),
        in_specs=[SCALARS, ANYWHERE, ANYWHERE],
        out_specs=[WHOLE] * 4,
        out_shape=[
            pltpu.VMEM((half, HEAD_DIM), F32),
            pltpu.VMEM(((chunks - 1) * half, HEAD_DIM), BF16),
            pltpu.VMEM((tokens, half), BF16),
            pltpu.VMEM((tokens, half), BF16),
        ],
        scratch_shapes=[pltpu.SemaphoreType.DMA((2 * chunks,))],
        compiler_params=params(24),
        cost_estimate=cost(tokens * width * HEAD_DIM, 2 * tokens * width),
        name="states",
    )(place, in_hbm(key_rows), in_hbm(values))


def write_weights(place_ref, session_ref, weight_ref):
    place = place_ref[0]
    core = place & 1
    chip = lax.shift_right_logical(place, 1)

    def flag(condition):
        return jnp.where(condition, 1.0, 0.0).astype(F32)

    def need(to, source):
        same = session_ref[2 * to] == session_ref[2 * source + 1]
        return flag(jnp.logical_and(source < to, same))

    even = core == 0
    if session_ref.shape[0] == 8:
        partner = jnp.where(even, chip ^ 1, chip ^ 2)
        to = jnp.where(even, chip ^ 2, chip ^ 1)
        rows = [need(to, chip), need(to, partner), need(chip, partner), flag(even), flag(core == 1)]
    else:
        rows = [flag(even)] * 5
    for r, value in enumerate(rows):
        weight_ref[r : r + 1, :] = jnp.full((1, HEAD_DIM), value, F32)


def inner_kernel(
    mine, place_ref, session_ref, query_ref, gate_ref, gain_ref, key_ref, value_ref, before_ref,
    after_ref, inner_ref, query_out_ref, factor_ref, weight_ref, gates, sems,
):
    tokens, half = key_ref.shape
    cols = columns(place_ref, mine, half)
    copies = []
    for c in range(tokens // CHUNK):
        for j, (source, to) in enumerate(((query_ref, query_out_ref), (gate_ref, gates))):
            copies.append(pltpu.make_async_copy(source.at[chunk(c), cols], to.at[chunk(c), :], sems.at[2 * c + j]))
            copies[-1].start()
    write_weights(place_ref, session_ref, weight_ref)
    rows_at = lax.broadcasted_iota(jnp.int32, (CHUNK, CHUNK), 0)
    cols_at = lax.broadcasted_iota(jnp.int32, (CHUNK, CHUNK), 1)
    causal = rows_at >= cols_at
    gain = gain_ref[:, cols]
    for c in range(tokens // CHUNK):
        copies[2 * c].wait()
        for h in range(half // HEAD_DIM):
            query = query_out_ref[chunk(c), head(h)]
            scores = dot_nt(query, key_ref[chunk(c), head(h)])
            scores = jnp.where(causal, scores, 0.0).astype(BF16)
            out = dot_nn(scores, value_ref[chunk(c), head(h)])
            if c > 0:
                at = (c - 1) * half + h * HEAD_DIM
                out += dot_nn(query, before_ref[at : at + HEAD_DIM, :])
            inner_ref[chunk(c), head(h)] = out
        copies[2 * c + 1].wait()
        for h in range(half // HEAD_DIM):
            gate = gates[chunk(c), head(h)].astype(F32)
            factor_ref[chunk(c), head(h)] = (0.5 * gain[:, head(h)]) * (1.0 + jnp.tanh(0.5 * gate))


def half_inner(place, session_of, queries, gate_input, norm_gain, keys, vals, before, after, mine):
    tokens, width = queries.shape
    half = width // 2
    chunks = tokens // CHUNK
    return pl.pallas_call(
        lambda *refs: inner_kernel(mine, *refs),
        in_specs=[SCALARS, SCALARS, ANYWHERE, ANYWHERE, WHOLE, WHOLE, WHOLE, WHOLE, ANYWHERE],
        out_specs=[WHOLE] * 4,
        out_shape=[
            pltpu.VMEM((tokens, half), F32),
            pltpu.VMEM((tokens, half), BF16),
            pltpu.VMEM((tokens, half), F32),
            pltpu.VMEM((8, HEAD_DIM), F32),
        ],
        scratch_shapes=[pltpu.VMEM((tokens, half), BF16), pltpu.SemaphoreType.DMA((2 * chunks,))],
        compiler_params=params(32),
        cost_estimate=cost(tokens * width * 3 * CHUNK, 6 * tokens * width),
        name="inner",
    )(
        place, session_of, in_hbm(queries), in_hbm(gate_input), norm_gain.reshape(1, width),
        in_vmem(keys), in_vmem(vals), in_vmem(before), after,
    )


def pair_prefix(prefix_ref, h):
    zero = jnp.zeros((HEAD_DIM, HEAD_DIM), BF16)
    top = jnp.concatenate([prefix_ref[head(h), :].astype(BF16), zero], axis=1)
    low = jnp.concatenate([zero, prefix_ref[head(h + 1), :].astype(BF16)], axis=1)
    return jnp.concatenate([top, low], axis=0)


def mix_kernel(last, query_ref, inner_ref, prefix_ref, extra_ref, mixed_ref, result_ref):
    tokens, half = query_ref.shape
    blocks = [pair_prefix(prefix_ref, h) for h in range(0, half // HEAD_DIM, 2)]
    for c in range(tokens // CHUNK):
        squares = extra_ref[chunk(c), :] if last else None
        for p, block in enumerate(blocks):
            both = slice(2 * p * HEAD_DIM, (2 * p + 2) * HEAD_DIM)
            outer = dot_nn(query_ref[chunk(c), both], block)
            for j in range(2):
                at = head(2 * p + j)
                mixed = inner_ref[chunk(c), at] + outer[:, head(j)]
                square = mixed * mixed
                squares = square if squares is None else squares + square
                mixed_ref[chunk(c), at] = mixed if last else mixed * extra_ref[chunk(c), at]
        if last:
            result_ref[:, chunk(c)] = jnp.sum(jnp.transpose(squares), axis=0, keepdims=True)
        else:
            result_ref[chunk(c), :] = squares


def mix(queries, inner, prefix, extra, last):
    tokens, half = queries.shape
    return pl.pallas_call(
        lambda *refs: mix_kernel(last, *refs),
        in_specs=[WHOLE] * 4,
        out_specs=[WHOLE, WHOLE],
        out_shape=[
            pltpu.VMEM((tokens, half), F32),
            pltpu.VMEM((1, tokens) if last else (tokens, HEAD_DIM), F32),
        ],
        input_output_aliases={1: 0},
        compiler_params=params(24),
        cost_estimate=cost(2 * tokens * half * HEAD_DIM, 2 * tokens * half),
        name="mix",
    )(*[in_vmem(x) for x in (queries, inner, prefix, extra)])


def gate_kernel(mixed_ref, factor_ref, gated_ref):
    for c in range(mixed_ref.shape[0] // CHUNK):
        gated_ref[chunk(c), :] = mixed_ref[chunk(c), :] * factor_ref[chunk(c), :]


def gated(mixed, factor):
    return pl.pallas_call(
        gate_kernel,
        in_specs=[WHOLE, WHOLE],
        out_specs=WHOLE,
        out_shape=pltpu.VMEM(mixed.shape, F32),
        input_output_aliases={0: 0},
        compiler_params=params(24),
        cost_estimate=cost(mixed.size, 4 * mixed.size),
        name="gate",
    )(in_vmem(mixed), in_vmem(factor))


def scale_kernel(features, place_ref, mine_ref, other_ref, power_ref, out_ref, mine_out, other_out, sems):
    tokens, half = mine_ref.shape
    rows = HEAD_DIM
    copies = []
    for c in range(tokens // rows):
        at = slice(c * rows, (c + 1) * rows)
        power = jnp.broadcast_to(power_ref[:, at], (HEAD_DIM, rows))
        factor = lax.rsqrt(jnp.transpose(power) / features + 1e-06)
        for j, (source, to) in enumerate(((mine_ref, mine_out), (other_ref, other_out))):
            for h in range(half // HEAD_DIM):
                to[at, head(h)] = (source[at, head(h)] * factor).astype(BF16)
            cols = columns(place_ref, j == 0, half)
            copies.append(pltpu.make_async_copy(to.at[at, :], out_ref.at[at, cols], sems.at[2 * c + j]))
            copies[-1].start()
    for copy in copies:
        copy.wait()


def scale(place, mine, other, power, features):
    tokens, half = mine.shape
    return pl.pallas_call(
        lambda *refs: scale_kernel(features, *refs),
        in_specs=[SCALARS, WHOLE, WHOLE, WHOLE],
        out_specs=ANYWHERE,
        out_shape=jax.ShapeDtypeStruct((tokens, 2 * half), BF16),
        scratch_shapes=[
            pltpu.VMEM((tokens, half), BF16),
            pltpu.VMEM((tokens, half), BF16),
            pltpu.SemaphoreType.DMA((2 * tokens // HEAD_DIM,)),
        ],
        compiler_params=params(24),
        cost_estimate=cost(4 * tokens * half, 4 * tokens * half),
        name="scale",
    )(place, in_vmem(mine), in_vmem(other), in_vmem(power))


def swap(count, bit):
    return [(i, i ^ bit) for i in range(count)]


def general_prefix(blocks, chip, session_of, chip_sum):
    total = chip_sum
    prefix = jnp.zeros_like(chip_sum)
    bit = 1
    while 2 * bit < blocks:
        there = lax.ppermute(total, "ctx", swap(blocks, 2 * bit))
        partner = chip ^ bit
        lower = partner < chip
        end_here = session_of[2 * (chip | (bit - 1)) + 1]
        end_there = session_of[2 * (partner | (bit - 1)) + 1]
        reaches = jnp.logical_and(lower, end_there == session_of[2 * chip])
        prefix = prefix + jnp.where(reaches, 1.0, 0.0) * there
        joined = jnp.where(end_here == end_there, 1.0, 0.0)
        total = jnp.where(lower, total + joined * there, joined * total + there)
        bit *= 2
    return prefix


def on_device(blocks, features, queries, key_rows, values, gate_input, norm_gain, session_of):
    width = queries.shape[1]
    index = lax.axis_index("ctx").astype(jnp.int32)
    place = index.reshape(1)

    def inner_of(half, after, mine):
        _, before, keys, vals = half
        return half_inner(
            place, session_of, queries, gate_input, norm_gain, keys, vals, before, after, mine
        )

    sent = half_states(place, key_rows, values, False)
    got = lax.ppermute(sent[0], "ctx", swap(blocks, 1))
    kept = half_states(place, key_rows, values, True)
    chip_sum = kept[0] + got
    inner_mine, query_mine, factor_mine, weight = inner_of(kept, chip_sum, True)

    if blocks == 8:
        first_step = [(i, i ^ (2 if i % 2 == 0 else 4)) for i in range(blocks)]
        second_step = [(i, i ^ (4 if i % 2 == 0 else 2)) for i in range(blocks)]
        there = lax.ppermute(chip_sum, "ctx", first_step)
        onward = weight[0:1] * chip_sum + weight[1:2] * there
        arrived = lax.ppermute(onward, "ctx", second_step)
        inner_other, query_other, factor_other, weight = inner_of(sent, onward, False)
        prefix = weight[2:3] * there + arrived
    else:
        inner_other, query_other, factor_other, weight = inner_of(sent, chip_sum, False)
        prefix = general_prefix(blocks, index >> 1, session_of, chip_sum)

    core = index & 1
    even, odd = (weight[3:4], weight[4:5]) if blocks == 8 else ((1 - core).astype(F32), core.astype(F32))
    other = lax.ppermute(prefix + even * kept[0], "ctx", swap(blocks, 1))
    mine = prefix + odd * got
    mixed_mine, squares = mix(query_mine, inner_mine, mine, factor_mine, False)
    mixed_other, power = mix(query_other, inner_other, other, squares, True)
    bit = 1
    while bit < features // width:
        power = power + lax.ppermute(power, "head", swap(features // width, bit))
        bit *= 2
    return scale(place, mixed_mine, gated(mixed_other, factor_other), power, features)


def solution(mesh):
    blocks = mesh.shape["ctx"]

    def whole(queries, key_rows, values, gate_input, norm_gain, session_of):
        features = queries.shape[1]
        return jax.shard_map(
            lambda *args: on_device(blocks, features, *args),
            mesh=mesh,
            in_specs=(
                P("ctx", "head"),
                P("ctx", "head"),
                P("ctx", "head"),
                P("ctx", "head"),
                P("head"),
                P(),
            ),
            out_specs=P("ctx", "head"),
            check_vma=False,
        )(queries, key_rows, values, gate_input, norm_gain, session_of)

    return whole
```

time: 203 us -> 40.1 us (0.20)
  the two profiles are of different devices: /device:TPU:7 before, /device:TPU:0 now
where the time goes in v2:
time: 40.1 us; the launch traced here: 40 us
  Pallas kernels  25.4 us (63%)
  starting transfers between devices  10.5 us (26%)
  waiting for transfers between devices  3.57 us (9%)
    pallas_call x2, Pallas kernels, half_inner(): pl.pallas_call(lambda *refs: inner_kernel(mine, *refs), in_specs=[SCALARS...  13.3 us
    pallas_call x2, Pallas kernels, half_states(): pl.pallas_call(lambda *refs: states_kernel(mine, *refs), in_specs=[SCALAR...  5.39 us
    ppermute x2, starting transfers between devices, on_device(): power = power + lax.ppermute(power, 'head', swap(features // width, bit))  5.2 us
    pallas_call x2, Pallas kernels, mix(): pl.pallas_call(lambda *refs: mix_kernel(last, *refs), in_specs=[WHOLE] *...  3.65 us
    ppermute x1, starting transfers between devices, on_device(): there = lax.ppermute(chip_sum, 'ctx', first_step)  2.57 us
    ppermute x2, waiting for transfers between devices, on_device(): power = power + lax.ppermute(power, 'head', swap(features // width, bit))  2.43 us
    pallas_call x1, Pallas kernels, scale(): pl.pallas_call(lambda *refs: scale_kernel(features, *refs), in_specs=[SCA...  2.36 us
    ppermute x1, starting transfers between devices, on_device(): arrived = lax.ppermute(onward, 'ctx', second_step)  2.11 us
  transfers between devices with their start and end apart: 6, of which 5 were waited for; matrix products, arithmetic and copies ran while one was open for 0% of the time, Pallas kernels for 46%

profile of v2, /device:TPU:0, one launch (start us, length us, event | category | flops | bytes accessed | tf_op | source)
XLA Modules:
  0.0 40.0 jit_solution(7980150182525414082)
XLA Ops:
  0.0 2.7 %states.3 = (f32[1024,128]{1,0:T(8,128)S(1)}, bf16[3072,128]{1,0:T(8,128)(2,1)S(1)}, bf16[1024,1024]{1,0:T(8,128)(2,1)S(1)}, bf16[1024,1024]{1,0:T(8,128)(2,1)S(1)}) custom-call(s32[1]{0:T(128)} %bitcast.refs_0_, bf16[1024,2048]{1,0:T(8,128)(2,1)} %refs_1_.5, bf16[1024,2048]{1,0:T(8,128)(2,1)} %refs_2_.5), custom_call_target="tpu_custom_call" | custom-call | flops 268435456 | bytes 4194304 | tf_op jit(solution)/shard_map/states/pallas_call | solution.py:85
  2.7 0.0 copy-start
  2.7 0.0 copy-start.1
  2.7 0.5 %collective-permute-start = (f32[1024,128]{1,0:T(8,128)S(1)}, f32[1024,128]{1,0:T(8,128)S(1)}, u32[]{:S(2)}, u32[]{:S(2)}) collective-permute-start(f32[1024,128]{1,0:T(8,128)S(1)} %get-tuple-element.29), channel_id=1, source_target_pairs={{0,4},{4,0},{8,12},{12,8},{16,20},{20,16},{24,28},{28,24},{1,5},{5... | collective-permute-start | bytes 1572872 | tf_op jit(solution)/shard_map/ppermute | solution.py:314
  3.2 2.7 %states.2 = (f32[1024,128]{1,0:T(8,128)S(1)}, bf16[3072,128]{1,0:T(8,128)(2,1)S(1)}, bf16[1024,1024]{1,0:T(8,128)(2,1)S(1)}, bf16[1024,1024]{1,0:T(8,128)(2,1)S(1)}) custom-call(s32[1]{0:T(128)} %bitcast.refs_0_, bf16[1024,2048]{1,0:T(8,128)(2,1)} %refs_1_.5, bf16[1024,2048]{1,0:T(8,128)(2,1)} %refs_2_.5), custom_call_target="tpu_custom_call" | custom-call | flops 268435456 | bytes 4194304 | tf_op jit(solution)/shard_map/states/pallas_call | solution.py:85
  5.9 0.0 collective-permute-done
  6.0 0.1 add.21.refs_8_
  6.0 2.6 %collective-permute-start.1 = (f32[1024,128]{1,0:T(8,128)S(1)}, f32[1024,128]{1,0:T(8,128)S(1)}, u32[]{:S(2)}, u32[]{:S(2)}) collective-permute-start(f32[1024,128]{1,0:T(8,128)S(1)} %add.21.refs_8_), channel_id=1, source_target_pairs={{0,8},{4,20},{8,0},{12,28},{16,24},{20,4},{24,16},{28,12},{1,9},{5... | collective-permute-start | bytes 1572872 | tf_op jit(solution)/shard_map/ppermute | solution.py:322
  8.6 0.0 copy-done
  8.6 0.0 copy-done.1
  8.6 6.5 %inner.2 = (f32[1024,1024]{1,0:T(8,128)S(1)}, bf16[1024,1024]{1,0:T(8,128)(2,1)S(1)}, f32[1024,1024]{1,0:T(8,128)S(1)}, f32[8,128]{1,0:T(8,128)S(1)}) custom-call(s32[1]{0:T(128)} %bitcast.refs_0_, s32[8]{0:T(128)S(1)} %copy-done.1, bf16[1024,2048]{1,0:T(8,128)(2,1)} %refs_2_.7, bf16[1024,2048]{1,0:T(8,128)(2,1)} %refs_3_.3, f32[1,2048]{1,0:T(1,128)S(1)} %bitcast.12, ...), custom_call_target="tpu_custom_call" | custom-call | flops 1610612736 | bytes 12582912 | tf_op jit(solution)/shard_map/inner/pallas_call | solution.py:162
  15.2 0.6 %collective-permute-done.1 = f32[1024,128]{1,0:T(8,128)S(1)} collective-permute-done((f32[1024,128]{1,0:T(8,128)S(1)}, f32[1024,128]{1,0:T(8,128)S(1)}, u32[]{:S(2)}, u32[]{:S(2)}) %collective-permute-start.1) | collective-permute-done | bytes 524320 | tf_op jit(solution)/shard_map/ppermute | solution.py:322
  15.8 0.1 multiply_add_fusion.3.refs_8_
  15.8 2.1 %collective-permute-start.2 = (f32[1024,128]{1,0:T(8,128)S(1)}, f32[1024,128]{1,0:T(8,128)S(1)}, u32[]{:S(2)}, u32[]{:S(2)}) collective-permute-start(f32[1024,128]{1,0:T(8,128)S(1)} %multiply_add_fusion.3.refs_8_), channel_id=1, source_target_pairs={{0,16},{4,12},{8,24},{12,4},{16,0},{20,28},{24,8},{28,20},{1,17},{... | collective-permute-start | bytes 1572872 | tf_op jit(solution)/shard_map/ppermute | solution.py:324
  17.9 6.7 %inner.3 = (f32[1024,1024]{1,0:T(8,128)S(1)}, bf16[1024,1024]{1,0:T(8,128)(2,1)S(1)}, f32[1024,1024]{1,0:T(8,128)S(1)}, f32[8,128]{1,0:T(8,128)S(1)}) custom-call(s32[1]{0:T(128)} %bitcast.refs_0_, s32[8]{0:T(128)S(1)} %copy-done.1, bf16[1024,2048]{1,0:T(8,128)(2,1)} %refs_2_.7, bf16[1024,2048]{1,0:T(8,128)(2,1)} %refs_3_.3, f32[1,2048]{1,0:T(1,128)S(1)} %bitcast.13, ...), custom_call_target="tpu_custom_call" | custom-call | flops 1610612736 | bytes 12582912 | tf_op jit(solution)/shard_map/inner/pallas_call | solution.py:162
  24.7 0.4 %collective-permute-done.2 = f32[1024,128]{1,0:T(8,128)S(1)} collective-permute-done((f32[1024,128]{1,0:T(8,128)S(1)}, f32[1024,128]{1,0:T(8,128)S(1)}, u32[]{:S(2)}, u32[]{:S(2)}) %collective-permute-start.2) | collective-permute-done | bytes 524320 | tf_op jit(solution)/shard_map/ppermute | solution.py:324
  25.1 0.1 multiply_add_fusion
  25.2 0.1 collective-permute-start.3
  25.3 1.8 %mix.2 = (f32[1024,1024]{1,0:T(8,128)S(1)}, f32[1024,128]{1,0:T(8,128)S(1)}) custom-call(bf16[1024,1024]{1,0:T(8,128)(2,1)S(1)} %get-tuple-element.30.refs_0_, f32[1024,1024]{1,0:T(8,128)S(1)} %get-tuple-element.31.refs_1_, f32[1024,128]{1,0:T(8,128)S(1)} %get-tuple-element.46.refs_2_, ...), custom_call_target="tpu_custom_call", output_to_operand_aliasing={{0}: (1, {})} | custom-call | flops 268435456 | bytes 2097152 | tf_op jit(solution)/shard_map/mix/pallas_call | solution.py:211
  27.1 0.1 collective-permute-done.3.refs_2_
  27.2 1.9 %mix.3 = (f32[1024,1024]{1,0:T(8,128)S(1)}, f32[1,1024]{1,0:T(1,128)S(1)}) custom-call(bf16[1024,1024]{1,0:T(8,128)(2,1)S(1)} %get-tuple-element.39.refs_0_, f32[1024,1024]{1,0:T(8,128)S(1)} %get-tuple-element.40.refs_1_, f32[1024,128]{1,0:T(8,128)S(1)} %collective-permute-done.3.refs_2_, ...), custom_call_target="tpu_custom_call", output_to_operand_aliasing={{0}: (1, {})} | custom-call | flops 268435456 | bytes 2097152 | tf_op jit(solution)/shard_map/mix/pallas_call | solution.py:211
  29.1 2.2 %collective-permute-start.4 = (f32[1,1024]{1,0:T(1,128)S(1)}, f32[1,1024]{1,0:T(1,128)S(1)}, u32[]{:S(2)}, u32[]{:S(2)}) collective-permute-start(f32[1,1024]{1,0:T(1,128)S(1)} %get-tuple-element.44), channel_id=1, source_target_pairs={{0,1},{1,0},{2,3},{3,2},{4,5},{5,4},{6,7},{7,6},{8,9},{9,8},{10,11... | collective-permute-start | bytes 12296 | tf_op jit(solution)/shard_map/ppermute | solution.py:339
  31.3 1.6 %collective-permute-done.4 = f32[1,1024]{1,0:T(1,128)S(1)} collective-permute-done((f32[1,1024]{1,0:T(1,128)S(1)}, f32[1,1024]{1,0:T(1,128)S(1)}, u32[]{:S(2)}, u32[]{:S(2)}) %collective-permute-start.4) | collective-permute-done | bytes 4128 | tf_op jit(solution)/shard_map/ppermute | solution.py:339
  32.8 3.0 %collective-permute-start.5 = (f32[1,1024]{1,0:T(1,128)S(1)}, f32[1,1024]{1,0:T(1,128)S(1)}, u32[]{:S(2)}, u32[]{:S(2)}) collective-permute-start(f32[1,1024]{1,0:T(1,128)S(1)} %add.26), channel_id=1, source_target_pairs={{0,2},{1,3},{2,0},{3,1},{4,6},{5,7},{6,4},{7,5},{8,10},{9,11},{10,... | collective-permute-start | bytes 12296 | tf_op jit(solution)/shard_map/ppermute | solution.py:339
  35.9 0.7 %gate.1.refs_2_ = f32[1024,1024]{1,0:T(8,128)S(1)} custom-call(f32[1024,1024]{1,0:T(8,128)S(1)} %get-tuple-element.42.mixed_ref, f32[1024,1024]{1,0:T(8,128)S(1)} %get-tuple-element.43.factor_ref), custom_call_target="tpu_custom_call", output_to_operand_aliasing={{}: (0, {})} | custom-call | flops 1048576 | bytes 4194304 | tf_op jit(solution)/shard_map/gate/pallas_call | solution.py:232
  36.6 0.9 %collective-permute-done.5 = f32[1,1024]{1,0:T(1,128)S(1)} collective-permute-done((f32[1,1024]{1,0:T(1,128)S(1)}, f32[1,1024]{1,0:T(1,128)S(1)}, u32[]{:S(2)}, u32[]{:S(2)}) %collective-permute-start.5) | collective-permute-done | bytes 4128 | tf_op jit(solution)/shard_map/ppermute | solution.py:339
  37.5 2.4 %scale.1 = bf16[1024,2048]{1,0:T(8,128)(2,1)} custom-call(s32[1]{0:T(128)} %bitcast.refs_0_, f32[1024,1024]{1,0:T(8,128)S(1)} %get-tuple-element.38.refs_1_, f32[1024,1024]{1,0:T(8,128)S(1)} %gate.1.refs_2_, f32[1,1024]{1,0:T(1,128)S(1)} %add.27.refs_3_), custom_call_target="tpu_custom_call" | custom-call | flops 4194304 | bytes 4194304 | tf_op jit(solution)/shard_map/scale/pallas_call | solution.py:264
  (4 shorter events, 0.0 us)
Async XLA Ops:
  2.7 5.9 %copy-start = (f32[2048]{0:T(1024)S(1)}, f32[2048]{0:T(1024)}, u32[]{:S(2)}) copy-start(f32[2048]{0:T(1024)} %param.10) | copy-start | bytes 24580
  2.7 5.9 %copy-start.1 = (s32[8]{0:T(128)S(1)}, s32[8]{0:T(128)}, u32[]{:S(2)}) copy-start(s32[8]{0:T(128)} %refs_1_.7) | copy-start | bytes 100
  2.7 3.2 %collective-permute-start = (f32[1024,128]{1,0:T(8,128)S(1)}, f32[1024,128]{1,0:T(8,128)S(1)}, u32[]{:S(2)}, u32[]{:S(2)}) collective-permute-start(f32[1024,128]{1,0:T(8,128)S(1)} %get-tuple-element.29), channel_id=1, source_target_pairs={{0,4},{4,0},{8,12},{12,8},{16,20},{20,16},{24,28},{28,24},{1,5},{5... | collective-permute-start | bytes 1572872 | tf_op jit(solution)/shard_map/ppermute | solution.py:314
  6.0 9.7 %collective-permute-start.1 = (f32[1024,128]{1,0:T(8,128)S(1)}, f32[1024,128]{1,0:T(8,128)S(1)}, u32[]{:S(2)}, u32[]{:S(2)}) collective-permute-start(f32[1024,128]{1,0:T(8,128)S(1)} %add.21.refs_8_), channel_id=1, source_target_pairs={{0,8},{4,20},{8,0},{12,28},{16,24},{20,4},{24,16},{28,12},{1,9},{5... | collective-permute-start | bytes 1572872 | tf_op jit(solution)/shard_map/ppermute | solution.py:322
  15.8 9.3 %collective-permute-start.2 = (f32[1024,128]{1,0:T(8,128)S(1)}, f32[1024,128]{1,0:T(8,128)S(1)}, u32[]{:S(2)}, u32[]{:S(2)}) collective-permute-start(f32[1024,128]{1,0:T(8,128)S(1)} %multiply_add_fusion.3.refs_8_), channel_id=1, source_target_pairs={{0,16},{4,12},{8,24},{12,4},{16,0},{20,28},{24,8},{28,20},{1,17},{... | collective-permute-start | bytes 1572872 | tf_op jit(solution)/shard_map/ppermute | solution.py:324
  25.2 2.0 %collective-permute-start.3 = (f32[1024,128]{1,0:T(8,128)S(1)}, f32[1024,128]{1,0:T(8,128)S(1)}, u32[]{:S(2)}, u32[]{:S(2)}) collective-permute-start(f32[1024,128]{1,0:T(8,128)S(1)} %get-tuple-element.45), channel_id=1, source_target_pairs={{0,4},{4,0},{8,12},{12,8},{16,20},{20,16},{24,28},{28,24},{1,5},{5... | collective-permute-start | bytes 1572872 | tf_op jit(solution)/shard_map/ppermute | solution.py:333
  29.1 3.7 %collective-permute-start.4 = (f32[1,1024]{1,0:T(1,128)S(1)}, f32[1,1024]{1,0:T(1,128)S(1)}, u32[]{:S(2)}, u32[]{:S(2)}) collective-permute-start(f32[1,1024]{1,0:T(1,128)S(1)} %get-tuple-element.44), channel_id=1, source_target_pairs={{0,1},{1,0},{2,3},{3,2},{4,5},{5,4},{6,7},{7,6},{8,9},{9,8},{10,11... | collective-permute-start | bytes 12296 | tf_op jit(solution)/shard_map/ppermute | solution.py:339
  32.8 4.6 %collective-permute-start.5 = (f32[1,1024]{1,0:T(1,128)S(1)}, f32[1,1024]{1,0:T(1,128)S(1)}, u32[]{:S(2)}, u32[]{:S(2)}) collective-permute-start(f32[1,1024]{1,0:T(1,128)S(1)} %add.26), channel_id=1, source_target_pairs={{0,2},{1,3},{2,0},{3,1},{4,6},{5,7},{6,4},{7,5},{8,10},{9,11},{10,... | collective-permute-start | bytes 12296 | tf_op jit(solution)/shard_map/ppermute | solution.py:339

commit v3 on v2

v3 whole, which is shorter than its diff:
```python
import jax
import jax.numpy as jnp
from jax import lax
from jax.experimental import pallas as pl
from jax.experimental.pallas import tpu as pltpu
from jax.sharding import PartitionSpec as P

HEAD_DIM = 128
CHUNK = 256
GROUPS = 2
MIB = 1024 * 1024
F32 = jnp.float32
BF16 = jnp.bfloat16
WHOLE = pl.BlockSpec(memory_space=pltpu.VMEM)
SCALARS = pl.BlockSpec(memory_space=pltpu.SMEM)
ANYWHERE = pl.BlockSpec(memory_space=pl.ANY)


def params(mib):
    return pltpu.CompilerParams(vmem_limit_bytes=mib * MIB)


def in_hbm(x):
    return pltpu.with_memory_space_constraint(x, pltpu.HBM)


def in_vmem(x):
    return pltpu.with_memory_space_constraint(x, pltpu.VMEM)


def cost(flops, bytes_accessed):
    return pl.CostEstimate(flops=flops, bytes_accessed=bytes_accessed, transcendentals=0)


def dot_tn(a, b):
    return lax.dot_general(a, b, (((0,), (0,)), ((), ())), preferred_element_type=F32)


def dot_nt(a, b):
    return lax.dot_general(a, b, (((1,), (1,)), ((), ())), preferred_element_type=F32)


def dot_nn(a, b):
    return lax.dot_general(a, b, (((1,), (0,)), ((), ())), preferred_element_type=F32)


def head(h):
    return slice(h * HEAD_DIM, (h + 1) * HEAD_DIM)


def chunk(c):
    return slice(c * CHUNK, (c + 1) * CHUNK)


def columns(place_ref, mine, half):
    core = place_ref[0] & 1
    return pl.ds(pl.multiple_of((core if mine else 1 - core) * half, half), half)


def states_kernel(mine, planned, groups, place_ref, key_ref, value_ref, *refs):
    if planned:
        session_ref, *refs = refs
    state_refs, refs = refs[:groups], refs[groups:]
    if planned:
        before_ref, keys, vals, weight_ref, sems, sessions, session_sem = refs
        session_copy = pltpu.make_async_copy(session_ref, sessions, session_sem)
        session_copy.start()
    else:
        before_ref, keys, vals, sems = refs
    tokens, half = keys.shape
    cols = columns(place_ref, mine, half)
    copies = []
    for c in range(tokens // CHUNK):
        for j, (source, to) in enumerate(((key_ref, keys), (value_ref, vals))):
            copies.append(pltpu.make_async_copy(source.at[chunk(c), cols], to.at[chunk(c), :], sems.at[2 * c + j]))
            copies[-1].start()
    if planned:
        session_copy.wait()
        write_weights(place_ref, sessions, weight_ref)
    for c in range(tokens // CHUNK):
        copies[2 * c].wait()
        copies[2 * c + 1].wait()
        for h in range(half // HEAD_DIM):
            new = dot_tn(keys[chunk(c), head(h)], vals[chunk(c), head(h)])
            per = half // HEAD_DIM // groups
            state_ref, rows = state_refs[h // per], head(h % per)
            if c == 0:
                state_ref[rows, :] = new
            else:
                old = state_ref[rows, :]
                at = (c - 1) * half + h * HEAD_DIM
                before_ref[at : at + HEAD_DIM, :] = old.astype(BF16)
                state_ref[rows, :] = old + new


def half_states(place, key_rows, values, mine, groups, session_of=None):
    tokens, width = key_rows.shape
    half = width // 2
    chunks = tokens // CHUNK
    planned = session_of is not None
    out_shape = [pltpu.VMEM((half // groups, HEAD_DIM), F32)] * groups + [
        pltpu.VMEM(((chunks - 1) * half, HEAD_DIM), BF16),
        pltpu.VMEM((tokens, half), BF16),
        pltpu.VMEM((tokens, half), BF16),
    ]
    scratch_shapes = [pltpu.SemaphoreType.DMA((2 * chunks,))]
    operands = [place, in_hbm(key_rows), in_hbm(values)]
    if planned:
        out_shape += [pltpu.VMEM((8, HEAD_DIM), F32)]
        scratch_shapes += [pltpu.SMEM(session_of.shape, jnp.int32), pltpu.SemaphoreType.DMA(())]
        operands += [in_hbm(session_of)]
    results = pl.pallas_call(
        lambda *refs: states_kernel(mine, planned, groups, *refs),
        in_specs=[SCALARS] + [ANYWHERE] * (len(operands) - 1),
        out_specs=[WHOLE] * len(out_shape),
        out_shape=out_shape,
        scratch_shapes=scratch_shapes,
        compiler_params=params(24),
        cost_estimate=cost(tokens * width * HEAD_DIM, 2 * tokens * width),
        name="states",
    )(*operands)
    return results[:groups], results[groups:]


def write_weights(place_ref, session_ref, weight_ref):
    place = place_ref[0]
    core = place & 1
    chip = lax.shift_right_logical(place, 1)

    def flag(condition):
        return jnp.where(condition, 1.0, 0.0).astype(F32)

    def need(to, source):
        same = session_ref[2 * to] == session_ref[2 * source + 1]
        return flag(jnp.logical_and(source < to, same))

    even = core == 0
    partner = jnp.where(even, chip ^ 1, chip ^ 2)
    to = jnp.where(even, chip ^ 2, chip ^ 1)
    rows = [flag(even), flag(core == 1), need(to, chip), need(to, partner), need(chip, partner)]
    for r, value in enumerate(rows):
        weight_ref[r : r + 1, :] = jnp.full((1, HEAD_DIM), value, F32)


def half_heads(place_ref, mine, half):
    start = (place_ref[0] & 1 if mine else 1 - (place_ref[0] & 1)) * half
    return lambda h: pl.ds(pl.multiple_of(start + h * HEAD_DIM, HEAD_DIM), HEAD_DIM)


def inner_kernel(mine, place_ref, query_ref, key_ref, value_ref, before_ref, after_ref, inner_ref, zero_ref):
    tokens, half = key_ref.shape
    heads = range(half // HEAD_DIM)
    columns_of = half_heads(place_ref, mine, half)
    zero_ref[...] = jnp.zeros_like(zero_ref)
    rows_at = lax.broadcasted_iota(jnp.int32, (CHUNK, CHUNK), 0)
    cols_at = lax.broadcasted_iota(jnp.int32, (CHUNK, CHUNK), 1)
    causal = rows_at >= cols_at
    for c in range(tokens // CHUNK):
        scores = []
        for h in heads:
            full = dot_nt(query_ref[chunk(c), columns_of(h)], key_ref[chunk(c), head(h)])
            scores.append(jnp.where(causal, full, 0.0).astype(BF16))
        for h in heads:
            left, right = scores[h], value_ref[chunk(c), head(h)]
            if c > 0:
                at = (c - 1) * half + h * HEAD_DIM
                left = jnp.concatenate([left, query_ref[chunk(c), columns_of(h)]], axis=1)
                right = jnp.concatenate([right, before_ref[at : at + HEAD_DIM, :]], axis=0)
            inner_ref[chunk(c), head(h)] = dot_nn(left, right)


def half_inner(place, queries, half_of_heads, after, mine):
    before, keys, vals = half_of_heads[:3]
    tokens, half = keys.shape
    return pl.pallas_call(
        lambda *refs: inner_kernel(mine, *refs),
        in_specs=[SCALARS, WHOLE, WHOLE, WHOLE, WHOLE, ANYWHERE],
        out_specs=[WHOLE] * 2,
        out_shape=[pltpu.VMEM((tokens, half), F32), pltpu.VMEM((1, HEAD_DIM), F32)],
        compiler_params=params(24),
        cost_estimate=cost(tokens * half * 6 * CHUNK, 12 * tokens * half),
        name="inner",
    )(place, in_vmem(queries), in_vmem(keys), in_vmem(vals), in_vmem(before), after)


def mix_kernel(mine, heads, first, last, place_ref, query_ref, inner_ref, prefix_ref, *refs):
    extra_ref, mixed_ref, result_ref = (None, *refs) if first else refs
    tokens, half = inner_ref.shape
    columns_of = half_heads(place_ref, mine, half)
    blocks = [prefix_ref[head(h - heads[0]), :].astype(BF16) for h in heads]
    for c in range(tokens // CHUNK):
        squares = None if first else extra_ref[chunk(c), :]
        for h, block in zip(heads, blocks):
            mixed = inner_ref[chunk(c), head(h)] + dot_nn(query_ref[chunk(c), columns_of(h)], block)
            square = mixed * mixed
            squares = square if squares is None else squares + square
            mixed_ref[chunk(c), head(h)] = mixed
        if last:
            result_ref[:, chunk(c)] = jnp.sum(jnp.transpose(squares), axis=0, keepdims=True)
        else:
            result_ref[chunk(c), :] = squares


def mix(place, queries, inner, prefix, squares, mine, group, last):
    tokens, half = inner.shape
    count = prefix.shape[0] // HEAD_DIM
    heads = range(group * count, (group + 1) * count)
    first = squares is None
    operands = [queries, inner, prefix] + ([] if first else [squares])
    return pl.pallas_call(
        lambda *refs: mix_kernel(mine, heads, first, last, *refs),
        in_specs=[SCALARS] + [WHOLE] * len(operands),
        out_specs=[WHOLE, WHOLE],
        out_shape=[
            pltpu.VMEM((tokens, half), F32),
            pltpu.VMEM((1, tokens) if last else (tokens, HEAD_DIM), F32),
        ],
        input_output_aliases={2: 0},
        compiler_params=params(24),
        cost_estimate=cost(2 * tokens * prefix.size, 2 * tokens * half),
        name="mix",
    )(place, *[in_vmem(x) for x in operands])


def gate_kernel(mine, place_ref, mixed_ref, gate_ref, gain_ref, after_ref, gated_ref, zero_ref):
    tokens, half = mixed_ref.shape
    zero_ref[...] = jnp.zeros_like(zero_ref)
    rows = HEAD_DIM
    columns_of = half_heads(place_ref, mine, half)

    def step(i, carry):
        at = pl.ds(pl.multiple_of(i * rows, rows), rows)
        for h in range(half // HEAD_DIM):
            gate = gate_ref[at, columns_of(h)].astype(F32)
            factor = (0.5 * gain_ref[:, columns_of(h)]) * (1.0 + jnp.tanh(0.5 * gate))
            gated_ref[at, head(h)] = mixed_ref[at, head(h)] * factor
        return carry

    lax.fori_loop(0, tokens // rows, step, 0)


def gated(place, mixed, gate_input, norm_gain, after, mine):
    tokens, width = gate_input.shape
    return pl.pallas_call(
        lambda *refs: gate_kernel(mine, *refs),
        in_specs=[SCALARS, WHOLE, WHOLE, WHOLE, ANYWHERE],
        out_specs=[WHOLE, WHOLE],
        out_shape=[pltpu.VMEM(mixed.shape, F32), pltpu.VMEM((1, tokens), F32)],
        input_output_aliases={1: 0},
        compiler_params=params(24),
        cost_estimate=cost(16 * mixed.size, 4 * mixed.size),
        name="gate",
    )(place, in_vmem(mixed), in_vmem(gate_input), norm_gain.reshape(1, width), after)


def scale_kernel(features, place_ref, mine_ref, other_ref, power_ref, out_ref, mine_out, other_out, sems):
    tokens, half = mine_ref.shape
    rows = HEAD_DIM
    copies = []
    for c in range(tokens // rows):
        at = slice(c * rows, (c + 1) * rows)
        power = jnp.broadcast_to(power_ref[:, at], (HEAD_DIM, rows))
        factor = lax.rsqrt(jnp.transpose(power) / features + 1e-06)
        for j, (source, to) in enumerate(((mine_ref, mine_out), (other_ref, other_out))):
            for h in range(half // HEAD_DIM):
                to[at, head(h)] = (source[at, head(h)] * factor).astype(BF16)
            cols = columns(place_ref, j == 0, half)
            copies.append(pltpu.make_async_copy(to.at[at, :], out_ref.at[at, cols], sems.at[2 * c + j]))
            copies[-1].start()
    for copy in copies:
        copy.wait()


def scale(place, mine, other, power, features):
    tokens, half = mine.shape
    return pl.pallas_call(
        lambda *refs: scale_kernel(features, *refs),
        in_specs=[SCALARS, WHOLE, WHOLE, WHOLE],
        out_specs=ANYWHERE,
        out_shape=pltpu.HBM((tokens, 2 * half), BF16),
        scratch_shapes=[
            pltpu.VMEM((tokens, half), BF16),
            pltpu.VMEM((tokens, half), BF16),
            pltpu.SemaphoreType.DMA((2 * tokens // HEAD_DIM,)),
        ],
        compiler_params=params(24),
        cost_estimate=cost(4 * tokens * half, 4 * tokens * half),
        name="scale",
    )(place, in_vmem(mine), in_vmem(other), in_vmem(power))


def swap(count, bit):
    return [(i, i ^ bit) for i in range(count)]


def general_prefix(blocks, chip, session_of, chip_sum):
    total = chip_sum
    prefix = jnp.zeros_like(chip_sum)
    bit = 1
    while 2 * bit < blocks:
        there = lax.ppermute(total, "ctx", swap(blocks, 2 * bit))
        partner = chip ^ bit
        lower = partner < chip
        end_here = session_of[2 * (chip | (bit - 1)) + 1]
        end_there = session_of[2 * (partner | (bit - 1)) + 1]
        reaches = jnp.logical_and(lower, end_there == session_of[2 * chip])
        prefix = prefix + jnp.where(reaches, 1.0, 0.0) * there
        joined = jnp.where(end_here == end_there, 1.0, 0.0)
        total = jnp.where(lower, total + joined * there, joined * total + there)
        bit *= 2
    return prefix


def zero_after(x):
    def kernel(after_ref, zero_ref):
        zero_ref[...] = jnp.zeros_like(zero_ref)

    return pl.pallas_call(
        kernel,
        in_specs=[ANYWHERE],
        out_specs=WHOLE,
        out_shape=pltpu.VMEM((1, HEAD_DIM), F32),
        compiler_params=params(1),
        name="then",
    )(x)


def two_steps(sums, weight, between, beside):
    there = [lax.ppermute(x, "ctx", [(i, i ^ (2 if i % 2 == 0 else 4)) for i in range(8)]) for x in sums]
    zero = between(sums[0])
    onward = []
    for x, y in zip(sums, there):
        onward.append(weight[2:3] * x + weight[3:4] * y + zero)
        zero = zero_after(onward[-1])
    arrived = [lax.ppermute(x, "ctx", [(i, i ^ (4 if i % 2 == 0 else 2)) for i in range(8)]) for x in onward]
    zero = beside(onward[-1])
    prefixes = []
    for x, y in zip(there, arrived):
        prefixes.append(weight[4:5] * x + y + zero)
        zero = zero_after(prefixes[-1])
    return prefixes


def on_device(blocks, features, queries, key_rows, values, gate_input, norm_gain, session_of):
    width = queries.shape[1]
    index = lax.axis_index("ctx").astype(jnp.int32)
    place = index.reshape(1)
    group_rows = width // 2 // GROUPS

    (sent,), sent_half = half_states(place, key_rows, values, False, 1, session_of if blocks == 8 else None)
    got = lax.ppermute(sent, "ctx", swap(blocks, 1))
    kept, kept_half = half_states(place, key_rows, values, True, GROUPS)
    got = [got[g * group_rows : (g + 1) * group_rows] for g in range(GROUPS)]
    sums = [x + y for x, y in zip(kept, got)]
    inner = {}

    def inner_of(half, mine):
        def run(after):
            inner[mine], zero = half_inner(place, queries, half, after, mine)
            return zero

        return run

    if blocks == 8:
        weight = sent_half[3]
        prefixes = two_steps(sums, weight, inner_of(kept_half, True), inner_of(sent_half, False))
        even, odd = weight[0:1], weight[1:2]
    else:
        zero = inner_of(kept_half, True)(sums[0]) + inner_of(sent_half, False)(sums[0])
        prefixes = [general_prefix(blocks, index >> 1, session_of, x) + zero for x in sums]
        odd = (index & 1).astype(F32)
        even = 1.0 - odd

    squares = None
    for g, prefix in enumerate(prefixes):
        other = lax.ppermute(prefix + even * kept[g], "ctx", swap(blocks, 1))
        inner[True], squares = mix(place, queries, inner[True], prefix + odd * got[g], squares, True, g, False)
        inner[False], squares = mix(place, queries, inner[False], other, squares, False, g, g == GROUPS - 1)
    power = squares
    gated_other, zero = gated(place, inner[False], gate_input, norm_gain, power, False)
    power = power + lax.ppermute(power, "head", swap(features // width, 1)) + zero
    gated_mine, zero = gated(place, inner[True], gate_input, norm_gain, power, True)
    bit = 2
    while bit < features // width:
        power = power + lax.ppermute(power, "head", swap(features // width, bit))
        bit *= 2
    return scale(place, gated_mine, gated_other, power + zero, features)


def solution(mesh):
    blocks = mesh.shape["ctx"]

    def whole(queries, key_rows, values, gate_input, norm_gain, session_of):
        features = queries.shape[1]
        return jax.shard_map(
            lambda *args: on_device(blocks, features, *args),
            mesh=mesh,
            in_specs=(
                P("ctx", "head"),
                P("ctx", "head"),
                P("ctx", "head"),
                P("ctx", "head"),
                P("head"),
                P(),
            ),
            out_specs=P("ctx", "head"),
            check_vma=False,
        )(queries, key_rows, values, gate_input, norm_gain, session_of)

    return whole
```

time: 40.1 us -> 37.3 us (0.930)
  Pallas kernels: 25.4 us -> 19.9 us
  starting transfers between devices: 10.5 us -> 12.9 us
    pallas_call x2, Pallas kernels: 13.3 us -> 5.78 us  [half_inner(): pl.pallas_call(lambda *refs: inner_kernel(mine, *refs), in_specs=[SCALARS...]
    ppermute x4 -> x8, starting transfers between devices: 5.28 us -> 9.76 us  [the longest x2 4.4 us: two_steps(): lax.ppermute(x, 'ctx', [(i, i ^ (4 if i % 2 == 0 else 2)) for i in range(...]
    ppermute x4 -> x8, waiting for transfers between devices: 1.13 us -> 3.61 us  [the longest x2 1.97 us: two_steps(): lax.ppermute(x, 'ctx', [(i, i ^ (2 if i % 2 == 0 else 4)) for i in range(...]
    ppermute x2 -> x1, waiting for transfers between devices: 2.43 us -> 0.29 us  [on_device(): power = power + lax.ppermute(power, 'head', swap(features // width, bit))]
    ppermute x2 -> x1, starting transfers between devices: 5.2 us -> 3.1 us  [on_device(): power = power + lax.ppermute(power, 'head', swap(features // width, bit))]
    pallas_call x5 -> x10, Pallas kernels: 9.76 us -> 11.7 us  [the longest x2 5.66 us: half_states(): pl.pallas_call(lambda *refs: states_kernel(mine, planned, groups, *refs),...]
  transfers between devices with their start and end apart: 6 -> 9, of which waited for: 5 -> 5; matrix products, arithmetic and copies ran while one was open for 0% -> 1% of each run, Pallas kernels for 46% -> 37%
where the time goes in v3:
time: 37.3 us; the launch traced here: 37.2 us
  Pallas kernels  19.9 us (53%)
  starting transfers between devices  12.9 us (35%)
  waiting for transfers between devices  3.9 us (10%)
    pallas_call x2, Pallas kernels, half_inner(): pl.pallas_call(lambda *refs: inner_kernel(mine, *refs), in_specs=[SCALARS...  5.78 us
    pallas_call x2, Pallas kernels, half_states(): pl.pallas_call(lambda *refs: states_kernel(mine, planned, groups, *refs),...  5.66 us
    ppermute x2, starting transfers between devices, two_steps(): lax.ppermute(x, 'ctx', [(i, i ^ (4 if i % 2 == 0 else 2)) for i in range(...  4.4 us
    pallas_call x4, Pallas kernels, mix(): pl.pallas_call(lambda *refs: mix_kernel(mine, heads, first, last, *refs),...  3.53 us
    ppermute x1, starting transfers between devices, on_device(): power = power + lax.ppermute(power, 'head', swap(features // width, bit))  3.1 us
    pallas_call x2, Pallas kernels, gated(): pl.pallas_call(lambda *refs: gate_kernel(mine, *refs), in_specs=[SCALARS,...  2.56 us
    ppermute x2, starting transfers between devices, two_steps(): lax.ppermute(x, 'ctx', [(i, i ^ (2 if i % 2 == 0 else 4)) for i in range(...  2.56 us
    pallas_call x1, Pallas kernels, scale(): pl.pallas_call(lambda *refs: scale_kernel(features, *refs), in_specs=[SCA...  2.35 us
  transfers between devices with their start and end apart: 9, of which 5 were waited for; matrix products, arithmetic and copies ran while one was open for 1% of the time, Pallas kernels for 37%

profile of v3, /device:TPU:0, one launch (start us, length us, event | category | flops | bytes accessed | tf_op | source)
XLA Modules:
  0.0 37.2 jit_solution(2836684782264407287)
XLA Ops:
  0.0 2.7 %states.3 = (f32[1024,128]{1,0:T(8,128)S(1)}, bf16[3072,128]{1,0:T(8,128)(2,1)S(1)}, bf16[1024,1024]{1,0:T(8,128)(2,1)S(1)}, bf16[1024,1024]{1,0:T(8,128)(2,1)S(1)}, f32[8,128]{1,0:T(8,128)S(1)}) custom-call(s32[1]{0:T(128)} %bitcast.refs_0_, bf16[1024,2048]{1,0:T(8,128)(2,1)} %refs_1_.9, bf16[1024,2048]{1,0:T(8,128)(2,1)} %refs_2_.5, s32[8]{0:T(128)} %refs_3_.1), custom_call_target="tpu_custom_call" | custom-call | flops 268435456 | bytes 4194304 | tf_op jit(solution)/shard_map/states/pallas_call | solution.py:112
  2.7 0.0 copy-start
  2.7 0.5 %collective-permute-start = (f32[1024,128]{1,0:T(8,128)S(1)}, f32[1024,128]{1,0:T(8,128)S(1)}, u32[]{:S(2)}, u32[]{:S(2)}) collective-permute-start(f32[1024,128]{1,0:T(8,128)S(1)} %get-tuple-element.35), channel_id=1, source_target_pairs={{0,4},{4,0},{8,12},{12,8},{16,20},{20,16},{24,28},{28,24},{1,5},{5... | collective-permute-start | bytes 1572872 | tf_op jit(solution)/shard_map/ppermute | solution.py:351
  3.2 3.0 %states.2 = (f32[512,128]{1,0:T(8,128)S(1)}, f32[512,128]{1,0:T(8,128)S(1)}, bf16[3072,128]{1,0:T(8,128)(2,1)S(1)}, bf16[1024,1024]{1,0:T(8,128)(2,1)S(1)}, bf16[1024,1024]{1,0:T(8,128)(2,1)S(1)}) custom-call(s32[1]{0:T(128)} %bitcast.refs_0_, bf16[1024,2048]{1,0:T(8,128)(2,1)} %refs_1_.9, bf16[1024,2048]{1,0:T(8,128)(2,1)} %refs_2_.5), custom_call_target="tpu_custom_call" | custom-call | flops 268435456 | bytes 4194304 | tf_op jit(solution)/shard_map/states/pallas_call | solution.py:112
  6.2 0.1 slice_add_fusion
  6.3 2.5 %collective-permute-start.1 = (f32[512,128]{1,0:T(8,128)S(1)}, f32[512,128]{1,0:T(8,128)S(1)}, u32[]{:S(2)}, u32[]{:S(2)}) collective-permute-start(f32[512,128]{1,0:T(8,128)S(1)} %get-tuple-element.63.refs_5_), channel_id=1, source_target_pairs={{0,8},{4,20},{8,0},{12,28},{16,24},{20,4},{24,16},{28,12},{1,9},{5... | collective-permute-start | bytes 786440 | tf_op jit(solution)/shard_map/ppermute | solution.py:329
  8.8 0.1 collective-permute-start.3
  8.9 2.9 %inner.2 = (f32[1024,1024]{1,0:T(8,128)S(1)}, f32[1,128]{1,0:T(1,128)S(1)}) custom-call(s32[1]{0:T(128)} %bitcast.refs_0_, bf16[1024,2048]{1,0:T(8,128)(2,1)S(1)} %copy-done, bf16[1024,1024]{1,0:T(8,128)(2,1)S(1)} %get-tuple-element.31.refs_2_, bf16[1024,1024]{1,0:T(8,128)(2,1)S(1)} %get-tuple-element.32.refs_3_, ...), custom_call_target="tpu_custom_call" | custom-call | flops 1610612736 | bytes 12582912 | tf_op jit(solution)/shard_map/inner/pallas_call | solution.py:175
  11.8 1.3 %collective-permute-done.1 = f32[512,128]{1,0:T(8,128)S(1)} collective-permute-done((f32[512,128]{1,0:T(8,128)S(1)}, f32[512,128]{1,0:T(8,128)S(1)}, u32[]{:S(2)}, u32[]{:S(2)}) %collective-permute-start.1) | collective-permute-done | bytes 262176 | tf_op jit(solution)/shard_map/ppermute | solution.py:329
  13.2 2.1 %collective-permute-start.2 = (f32[512,128]{1,0:T(8,128)S(1)}, f32[512,128]{1,0:T(8,128)S(1)}, u32[]{:S(2)}, u32[]{:S(2)}) collective-permute-start(f32[512,128]{1,0:T(8,128)S(1)} %add_add_fusion.3.after_ref), channel_id=1, source_target_pairs={{0,16},{4,12},{8,24},{12,4},{16,0},{20,28},{24,8},{28,20},{1,17},{... | collective-permute-start | bytes 786440 | tf_op jit(solution)/shard_map/ppermute | solution.py:335
  15.3 0.6 %collective-permute-done.3 = f32[512,128]{1,0:T(8,128)S(1)} collective-permute-done((f32[512,128]{1,0:T(8,128)S(1)}, f32[512,128]{1,0:T(8,128)S(1)}, u32[]{:S(2)}, u32[]{:S(2)}) %collective-permute-start.3) | collective-permute-done | bytes 262176 | tf_op jit(solution)/shard_map/ppermute | solution.py:329
  16.0 2.3 %collective-permute-start.4 = (f32[512,128]{1,0:T(8,128)S(1)}, f32[512,128]{1,0:T(8,128)S(1)}, u32[]{:S(2)}, u32[]{:S(2)}) collective-permute-start(f32[512,128]{1,0:T(8,128)S(1)} %add_add_fusion.1.refs_5_), channel_id=1, source_target_pairs={{0,16},{4,12},{8,24},{12,4},{16,0},{20,28},{24,8},{28,20},{1,17},{... | collective-permute-start | bytes 786440 | tf_op jit(solution)/shard_map/ppermute | solution.py:335
  18.3 2.8 %inner.3 = (f32[1024,1024]{1,0:T(8,128)S(1)}, f32[1,128]{1,0:T(1,128)S(1)}) custom-call(s32[1]{0:T(128)} %bitcast.refs_0_, bf16[1024,2048]{1,0:T(8,128)(2,1)S(1)} %copy-done, bf16[1024,1024]{1,0:T(8,128)(2,1)S(1)} %get-tuple-element.39.refs_2_, bf16[1024,1024]{1,0:T(8,128)(2,1)S(1)} %get-tuple-element.40.refs_3_, ...), custom_call_target="tpu_custom_call" | custom-call | flops 1610612736 | bytes 12582912 | tf_op jit(solution)/shard_map/inner/pallas_call | solution.py:175
  21.1 0.0 collective-permute-done.2
  21.1 0.1 multiply_add_fusion.1
  21.2 0.1 collective-permute-start.5
  21.3 1.3 %collective-permute-done.4 = f32[512,128]{1,0:T(8,128)S(1)} collective-permute-done((f32[512,128]{1,0:T(8,128)S(1)}, f32[512,128]{1,0:T(8,128)S(1)}, u32[]{:S(2)}, u32[]{:S(2)}) %collective-permute-start.4) | collective-permute-done | bytes 262176 | tf_op jit(solution)/shard_map/ppermute | solution.py:335
  22.6 0.1 multiply_add_fusion
  22.7 0.1 collective-permute-start.6
  22.8 0.8 %mix.4 = (f32[1024,1024]{1,0:T(8,128)S(1)}, f32[1024,128]{1,0:T(8,128)S(1)}) custom-call(s32[1]{0:T(128)} %bitcast.refs_0_, bf16[1024,2048]{1,0:T(8,128)(2,1)S(1)} %copy-done, f32[1024,1024]{1,0:T(8,128)S(1)} %get-tuple-element.36.refs_2_, f32[512,128]{1,0:T(8,128)S(1)} %get-tuple-element.61.refs_3_), custom_call_target="tpu_custom_call", output_to_operand_aliasing={{0}: (2, {})} | custom-call | flops 134217728 | bytes 2097152 | tf_op jit(solution)/shard_map/mix/pallas_call | solution.py:210
  23.7 0.9 %mix.5 = (f32[1024,1024]{1,0:T(8,128)S(1)}, f32[1024,128]{1,0:T(8,128)S(1)}) custom-call(s32[1]{0:T(128)} %bitcast.refs_0_, bf16[1024,2048]{1,0:T(8,128)(2,1)S(1)} %copy-done, f32[1024,1024]{1,0:T(8,128)S(1)} %get-tuple-element.45.refs_2_, f32[512,128]{1,0:T(8,128)S(1)} %collective-permute-done.5.refs_3_, ...), custom_call_target="tpu_custom_call", output_to_operand_aliasing={{0}: (2, {})} | custom-call | flops 134217728 | bytes 2097152 | tf_op jit(solution)/shard_map/mix/pallas_call | solution.py:210
  24.5 0.9 %mix.6 = (f32[1024,1024]{1,0:T(8,128)S(1)}, f32[1024,128]{1,0:T(8,128)S(1)}) custom-call(s32[1]{0:T(128)} %bitcast.refs_0_, bf16[1024,2048]{1,0:T(8,128)(2,1)S(1)} %copy-done, f32[1024,1024]{1,0:T(8,128)S(1)} %get-tuple-element.44.refs_2_, f32[512,128]{1,0:T(8,128)S(1)} %get-tuple-element.60.refs_3_, ...), custom_call_target="tpu_custom_call", output_to_operand_aliasing={{0}: (2, {})} | custom-call | flops 134217728 | bytes 2097152 | tf_op jit(solution)/shard_map/mix/pallas_call | solution.py:210
  25.4 0.0 copy-start.1
  25.4 0.0 copy-start.2
  25.4 1.0 %mix.7 = (f32[1024,1024]{1,0:T(8,128)S(1)}, f32[1,1024]{1,0:T(1,128)S(1)}) custom-call(s32[1]{0:T(128)} %bitcast.refs_0_, bf16[1024,2048]{1,0:T(8,128)(2,1)S(1)} %copy-done, f32[1024,1024]{1,0:T(8,128)S(1)} %get-tuple-element.49.refs_2_, f32[512,128]{1,0:T(8,128)S(1)} %collective-permute-done.6.refs_3_, ...), custom_call_target="tpu_custom_call", output_to_operand_aliasing={{0}: (2, {})} | custom-call | flops 134217728 | bytes 2097152 | tf_op jit(solution)/shard_map/mix/pallas_call | solution.py:210
  26.4 2.1 %collective-permute-start.7 = (f32[1,1024]{1,0:T(1,128)S(1)}, f32[1,1024]{1,0:T(1,128)S(1)}, u32[]{:S(2)}, u32[]{:S(2)}) collective-permute-start(f32[1,1024]{1,0:T(1,128)S(1)} %get-tuple-element.51.refs_4_), channel_id=1, source_target_pairs={{0,1},{1,0},{2,3},{3,2},{4,5},{5,4},{6,7},{7,6},{8,9},{9,8},{10,11... | collective-permute-start | bytes 12296 | tf_op jit(solution)/shard_map/ppermute | solution.py:381
  28.6 1.3 %gate.2 = (f32[1024,1024]{1,0:T(8,128)S(1)}, f32[1,1024]{1,0:T(1,128)S(1)}) custom-call(s32[1]{0:T(128)} %bitcast.refs_0_, f32[1024,1024]{1,0:T(8,128)S(1)} %get-tuple-element.52.refs_1_, bf16[1024,2048]{1,0:T(8,128)(2,1)S(1)} %copy-done.1, f32[1,2048]{1,0:T(1,128)S(1)} %bitcast.16, ...), custom_call_target="tpu_custom_call", output_to_operand_aliasing={{0}: (1, {})} | custom-call | flops 16777216 | bytes 4194304 | tf_op jit(solution)/shard_map/gate/pallas_call | solution.py:244
  29.8 0.3 collective-permute-done.7
  30.1 3.1 %collective-permute-start.8 = (f32[1,1024]{1,0:T(1,128)S(1)}, f32[1,1024]{1,0:T(1,128)S(1)}, u32[]{:S(2)}, u32[]{:S(2)}) collective-permute-start(f32[1,1024]{1,0:T(1,128)S(1)} %add_add_fusion.5.refs_4_), channel_id=1, source_target_pairs={{0,2},{1,3},{2,0},{3,1},{4,6},{5,7},{6,4},{7,5},{8,10},{9,11},{10,... | collective-permute-start | bytes 12296 | tf_op jit(solution)/shard_map/ppermute | solution.py:385
  33.2 1.3 %gate.3 = (f32[1024,1024]{1,0:T(8,128)S(1)}, f32[1,1024]{1,0:T(1,128)S(1)}) custom-call(s32[1]{0:T(128)} %bitcast.refs_0_, f32[1024,1024]{1,0:T(8,128)S(1)} %get-tuple-element.48.refs_1_, bf16[1024,2048]{1,0:T(8,128)(2,1)S(1)} %copy-done.1, f32[1,2048]{1,0:T(1,128)S(1)} %bitcast.17, f32[1,1024]{1,0:T(1,128)S(1)} %add_add_fusion.5.refs_4_), custom_call_target="tpu_custom_call", output_to_operand_aliasing={{0}: (1, {})} | custom-call | flops 16777216 | bytes 4194304 | tf_op jit(solution)/shard_map/gate/pallas_call | solution.py:244
  34.5 0.3 collective-permute-done.8
  34.8 2.3 %scale.1 = bf16[1024,2048]{1,0:T(8,128)(2,1)} custom-call(s32[1]{0:T(128)} %bitcast.refs_0_, f32[1024,1024]{1,0:T(8,128)S(1)} %get-tuple-element.54.refs_1_, f32[1024,1024]{1,0:T(8,128)S(1)} %get-tuple-element.55.refs_2_, f32[1,1024]{1,0:T(1,128)S(1)} %add_add_fusion.4.refs_3_), custom_call_target="tpu_custom_call" | custom-call | flops 4194304 | bytes 4194304 | tf_op jit(solution)/shard_map/scale/pallas_call | solution.py:276
  (13 shorter events, 0.1 us)
Async XLA Ops:
  2.7 6.1 %copy-start = (bf16[1024,2048]{1,0:T(8,128)(2,1)S(1)}, bf16[1024,2048]{1,0:T(8,128)(2,1)}, u32[]{:S(2)}) copy-start(bf16[1024,2048]{1,0:T(8,128)(2,1)} %refs_1_.15) | copy-start | bytes 12582916
  2.7 3.5 %collective-permute-start = (f32[1024,128]{1,0:T(8,128)S(1)}, f32[1024,128]{1,0:T(8,128)S(1)}, u32[]{:S(2)}, u32[]{:S(2)}) collective-permute-start(f32[1024,128]{1,0:T(8,128)S(1)} %get-tuple-element.35), channel_id=1, source_target_pairs={{0,4},{4,0},{8,12},{12,8},{16,20},{20,16},{24,28},{28,24},{1,5},{5... | collective-permute-start | bytes 1572872 | tf_op jit(solution)/shard_map/ppermute | solution.py:351
  6.3 6.8 %collective-permute-start.1 = (f32[512,128]{1,0:T(8,128)S(1)}, f32[512,128]{1,0:T(8,128)S(1)}, u32[]{:S(2)}, u32[]{:S(2)}) collective-permute-start(f32[512,128]{1,0:T(8,128)S(1)} %get-tuple-element.63.refs_5_), channel_id=1, source_target_pairs={{0,8},{4,20},{8,0},{12,28},{16,24},{20,4},{24,16},{28,12},{1,9},{5... | collective-permute-start | bytes 786440 | tf_op jit(solution)/shard_map/ppermute | solution.py:329
  8.8 7.2 %collective-permute-start.3 = (f32[512,128]{1,0:T(8,128)S(1)}, f32[512,128]{1,0:T(8,128)S(1)}, u32[]{:S(2)}, u32[]{:S(2)}) collective-permute-start(f32[512,128]{1,0:T(8,128)S(1)} %get-tuple-element.62), channel_id=1, source_target_pairs={{0,8},{4,20},{8,0},{12,28},{16,24},{20,4},{24,16},{28,12},{1,9},{5... | collective-permute-start | bytes 786440 | tf_op jit(solution)/shard_map/ppermute | solution.py:329
  13.2 8.0 %collective-permute-start.2 = (f32[512,128]{1,0:T(8,128)S(1)}, f32[512,128]{1,0:T(8,128)S(1)}, u32[]{:S(2)}, u32[]{:S(2)}) collective-permute-start(f32[512,128]{1,0:T(8,128)S(1)} %add_add_fusion.3.after_ref), channel_id=1, source_target_pairs={{0,16},{4,12},{8,24},{12,4},{16,0},{20,28},{24,8},{28,20},{1,17},{... | collective-permute-start | bytes 786440 | tf_op jit(solution)/shard_map/ppermute | solution.py:335
  16.0 6.6 %collective-permute-start.4 = (f32[512,128]{1,0:T(8,128)S(1)}, f32[512,128]{1,0:T(8,128)S(1)}, u32[]{:S(2)}, u32[]{:S(2)}) collective-permute-start(f32[512,128]{1,0:T(8,128)S(1)} %add_add_fusion.1.refs_5_), channel_id=1, source_target_pairs={{0,16},{4,12},{8,24},{12,4},{16,0},{20,28},{24,8},{28,20},{1,17},{... | collective-permute-start | bytes 786440 | tf_op jit(solution)/shard_map/ppermute | solution.py:335
  21.2 2.4 %collective-permute-start.5 = (f32[512,128]{1,0:T(8,128)S(1)}, f32[512,128]{1,0:T(8,128)S(1)}, u32[]{:S(2)}, u32[]{:S(2)}) collective-permute-start(f32[512,128]{1,0:T(8,128)S(1)} %get-tuple-element.57), channel_id=1, source_target_pairs={{0,4},{4,0},{8,12},{12,8},{16,20},{20,16},{24,28},{28,24},{1,5},{5... | collective-permute-start | bytes 786440 | tf_op jit(solution)/shard_map/ppermute | solution.py:376
  22.7 2.7 %collective-permute-start.6 = (f32[512,128]{1,0:T(8,128)S(1)}, f32[512,128]{1,0:T(8,128)S(1)}, u32[]{:S(2)}, u32[]{:S(2)}) collective-permute-start(f32[512,128]{1,0:T(8,128)S(1)} %get-tuple-element.59), channel_id=1, source_target_pairs={{0,4},{4,0},{8,12},{12,8},{16,20},{20,16},{24,28},{28,24},{1,5},{5... | collective-permute-start | bytes 786440 | tf_op jit(solution)/shard_map/ppermute | solution.py:376
  25.4 3.1 %copy-start.1 = (bf16[1024,2048]{1,0:T(8,128)(2,1)S(1)}, bf16[1024,2048]{1,0:T(8,128)(2,1)}, u32[]{:S(2)}) copy-start(bf16[1024,2048]{1,0:T(8,128)(2,1)} %refs_2_.7) | copy-start | bytes 12582916
  25.4 3.1 %copy-start.2 = (f32[2048]{0:T(1024)S(1)}, f32[2048]{0:T(1024)}, u32[]{:S(2)}) copy-start(f32[2048]{0:T(1024)} %param.10) | copy-start | bytes 24580
  26.4 3.7 %collective-permute-start.7 = (f32[1,1024]{1,0:T(1,128)S(1)}, f32[1,1024]{1,0:T(1,128)S(1)}, u32[]{:S(2)}, u32[]{:S(2)}) collective-permute-start(f32[1,1024]{1,0:T(1,128)S(1)} %get-tuple-element.51.refs_4_), channel_id=1, source_target_pairs={{0,1},{1,0},{2,3},{3,2},{4,5},{5,4},{6,7},{7,6},{8,9},{9,8},{10,11... | collective-permute-start | bytes 12296 | tf_op jit(solution)/shard_map/ppermute | solution.py:381
  30.1 4.7 %collective-permute-start.8 = (f32[1,1024]{1,0:T(1,128)S(1)}, f32[1,1024]{1,0:T(1,128)S(1)}, u32[]{:S(2)}, u32[]{:S(2)}) collective-permute-start(f32[1,1024]{1,0:T(1,128)S(1)} %add_add_fusion.5.refs_4_), channel_id=1, source_target_pairs={{0,2},{1,3},{2,0},{3,1},{4,6},{5,7},{6,4},{7,5},{8,10},{9,11},{10,... | collective-permute-start | bytes 12296 | tf_op jit(solution)/shard_map/ppermute | solution.py:385

commit v4 on v3

--- a/solution.py
+++ b/solution.py
@@ -115,7 +115,7 @@
         out_specs=[WHOLE] * len(out_shape),
         out_shape=out_shape,
         scratch_shapes=scratch_shapes,
-        compiler_params=params(24),
+        compiler_params=params(8),
         cost_estimate=cost(tokens * width * HEAD_DIM, 2 * tokens * width),
         name="states",
     )(*operands)
@@ -177,7 +177,7 @@
         in_specs=[SCALARS, WHOLE, WHOLE, WHOLE, WHOLE, ANYWHERE],
         out_specs=[WHOLE] * 2,
         out_shape=[pltpu.VMEM((tokens, half), F32), pltpu.VMEM((1, HEAD_DIM), F32)],
-        compiler_params=params(24),
+        compiler_params=params(8),
         cost_estimate=cost(tokens * half * 6 * CHUNK, 12 * tokens * half),
         name="inner",
     )(place, in_vmem(queries), in_vmem(keys), in_vmem(vals), in_vmem(before), after)
@@ -187,14 +187,14 @@
     extra_ref, mixed_ref, result_ref = (None, *refs) if first else refs
     tokens, half = inner_ref.shape
     columns_of = half_heads(place_ref, mine, half)
-    blocks = [prefix_ref[head(h - heads[0]), :].astype(BF16) for h in heads]
+    blocks = [prefix_ref[head(j), :].astype(BF16) for j in range(len(heads))]
     for c in range(tokens // CHUNK):
         squares = None if first else extra_ref[chunk(c), :]
-        for h, block in zip(heads, blocks):
-            mixed = inner_ref[chunk(c), head(h)] + dot_nn(query_ref[chunk(c), columns_of(h)], block)
+        for j, h in enumerate(heads):
+            mixed = inner_ref[chunk(c), head(h)] + dot_nn(query_ref[chunk(c), columns_of(h)], blocks[j])
             square = mixed * mixed
             squares = square if squares is None else squares + square
-            mixed_ref[chunk(c), head(h)] = mixed
+            mixed_ref[chunk(c), head(j)] = mixed
         if last:
             result_ref[:, chunk(c)] = jnp.sum(jnp.transpose(squares), axis=0, keepdims=True)
         else:
@@ -212,28 +212,29 @@
         in_specs=[SCALARS] + [WHOLE] * len(operands),
         out_specs=[WHOLE, WHOLE],
         out_shape=[
-            pltpu.VMEM((tokens, half), F32),
+            pltpu.VMEM((tokens, count * HEAD_DIM), F32),
             pltpu.VMEM((1, tokens) if last else (tokens, HEAD_DIM), F32),
         ],
-        input_output_aliases={2: 0},
-        compiler_params=params(24),
+        compiler_params=params(8),
         cost_estimate=cost(2 * tokens * prefix.size, 2 * tokens * half),
         name="mix",
     )(place, *[in_vmem(x) for x in operands])
 
 
-def gate_kernel(mine, place_ref, mixed_ref, gate_ref, gain_ref, after_ref, gated_ref, zero_ref):
-    tokens, half = mixed_ref.shape
+def gate_kernel(mine, place_ref, gate_ref, gain_ref, after_ref, *refs):
+    *mixed_refs, gated_ref, zero_ref = refs
+    tokens, half = gated_ref.shape
     zero_ref[...] = jnp.zeros_like(zero_ref)
     rows = HEAD_DIM
     columns_of = half_heads(place_ref, mine, half)
+    per = half // HEAD_DIM // len(mixed_refs)
 
     def step(i, carry):
         at = pl.ds(pl.multiple_of(i * rows, rows), rows)
         for h in range(half // HEAD_DIM):
             gate = gate_ref[at, columns_of(h)].astype(F32)
             factor = (0.5 * gain_ref[:, columns_of(h)]) * (1.0 + jnp.tanh(0.5 * gate))
-            gated_ref[at, head(h)] = mixed_ref[at, head(h)] * factor
+            gated_ref[at, head(h)] = mixed_refs[h // per][at, head(h % per)] * factor
         return carry
 
     lax.fori_loop(0, tokens // rows, step, 0)
@@ -243,14 +244,13 @@
     tokens, width = gate_input.shape
     return pl.pallas_call(
         lambda *refs: gate_kernel(mine, *refs),
-        in_specs=[SCALARS, WHOLE, WHOLE, WHOLE, ANYWHERE],
+        in_specs=[SCALARS, WHOLE, WHOLE, ANYWHERE] + [WHOLE] * len(mixed),
         out_specs=[WHOLE, WHOLE],
-        out_shape=[pltpu.VMEM(mixed.shape, F32), pltpu.VMEM((1, tokens), F32)],
-        input_output_aliases={1: 0},
-        compiler_params=params(24),
-        cost_estimate=cost(16 * mixed.size, 4 * mixed.size),
+        out_shape=[pltpu.VMEM((tokens, width // 2), F32), pltpu.VMEM((1, tokens), F32)],
+        compiler_params=params(8),
+        cost_estimate=cost(8 * tokens * width, 2 * tokens * width),
         name="gate",
-    )(place, in_vmem(mixed), in_vmem(gate_input), norm_gain.reshape(1, width), after)
+    )(place, in_vmem(gate_input), norm_gain.reshape(1, width), after, *[in_vmem(x) for x in mixed])
 
 
 def scale_kernel(features, place_ref, mine_ref, other_ref, power_ref, out_ref, mine_out, other_out, sems):
@@ -283,7 +283,7 @@
             pltpu.VMEM((tokens, half), BF16),
             pltpu.SemaphoreType.DMA((2 * tokens // HEAD_DIM,)),
         ],
-        compiler_params=params(24),
+        compiler_params=params(8),
         cost_estimate=cost(4 * tokens * half, 4 * tokens * half),
         name="scale",
     )(place, in_vmem(mine), in_vmem(other), in_vmem(power))
@@ -334,11 +334,7 @@
         zero = zero_after(onward[-1])
     arrived = [lax.ppermute(x, "ctx", [(i, i ^ (4 if i % 2 == 0 else 2)) for i in range(8)]) for x in onward]
     zero = beside(onward[-1])
-    prefixes = []
-    for x, y in zip(there, arrived):
-        prefixes.append(weight[4:5] * x + y + zero)
-        zero = zero_after(prefixes[-1])
-    return prefixes
+    return [weight[4:5] * x + y + zero for x, y in zip(there, arrived)]
 
 
 def on_device(blocks, features, queries, key_rows, values, gate_input, norm_gain, session_of):
@@ -371,15 +367,21 @@
         odd = (index & 1).astype(F32)
         even = 1.0 - odd
 
+    mixed = {True: [], False: []}
     squares = None
+    zero = jnp.zeros((1, HEAD_DIM), F32)
     for g, prefix in enumerate(prefixes):
+        prefix = prefix + zero
         other = lax.ppermute(prefix + even * kept[g], "ctx", swap(blocks, 1))
-        inner[True], squares = mix(place, queries, inner[True], prefix + odd * got[g], squares, True, g, False)
-        inner[False], squares = mix(place, queries, inner[False], other, squares, False, g, g == GROUPS - 1)
+        part, squares = mix(place, queries, inner[True], prefix + odd * got[g], squares, True, g, False)
+        mixed[True].append(part)
+        zero = zero_after(squares)
+        part, squares = mix(place, queries, inner[False], other, squares, False, g, g == GROUPS - 1)
+        mixed[False].append(part)
     power = squares
-    gated_other, zero = gated(place, inner[False], gate_input, norm_gain, power, False)
+    gated_other, zero = gated(place, mixed[False], gate_input, norm_gain, power, False)
     power = power + lax.ppermute(power, "head", swap(features // width, 1)) + zero
-    gated_mine, zero = gated(place, inner[True], gate_input, norm_gain, power, True)
+    gated_mine, zero = gated(place, mixed[True], gate_input, norm_gain, power, True)
     bit = 2
     while bit < features // width:
         power = power + lax.ppermute(power, "head", swap(features // width, bit))

time: 37.3 us -> 35.9 us (0.962)
  Pallas kernels: 19.9 us -> 18 us
  waiting for transfers between devices: 3.9 us -> 4.34 us
    pallas_call x4, Pallas kernels: 3.53 us -> 2.22 us  [mix(): pl.pallas_call(lambda *refs: mix_kernel(mine, heads, first, last, *refs),...]
    pallas_call x2, Pallas kernels: 2.56 us -> 1.98 us  [gated(): pl.pallas_call(lambda *refs: gate_kernel(mine, *refs), in_specs=[SCALARS,...]
    ppermute x2, waiting for transfers between devices: 1.33 us -> 0.79 us  [two_steps(): lax.ppermute(x, 'ctx', [(i, i ^ (4 if i % 2 == 0 else 2)) for i in range(...]
    ppermute x2, waiting for transfers between devices: 0.01 us -> 0.42 us  [on_device(): other = lax.ppermute(prefix + even * kept[g], 'ctx', swap(blocks, 1))]
  transfers between devices with their start and end apart: 9 -> 9, of which waited for: 5 -> 6; matrix products, arithmetic and copies ran while one was open for 1% -> 1% of each run, Pallas kernels for 37% -> 35%
where the time goes in v4:
time: 35.9 us; the launch traced here: 35.7 us
  Pallas kernels  18 us (50%)
  starting transfers between devices  12.8 us (36%)
  waiting for transfers between devices  4.34 us (12%)
  other arithmetic  0.36 us (1%)
    pallas_call x2, Pallas kernels, half_inner(): pl.pallas_call(lambda *refs: inner_kernel(mine, *refs), in_specs=[SCALARS...  5.77 us
    pallas_call x2, Pallas kernels, half_states(): pl.pallas_call(lambda *refs: states_kernel(mine, planned, groups, *refs),...  5.71 us
    ppermute x2, starting transfers between devices, two_steps(): lax.ppermute(x, 'ctx', [(i, i ^ (4 if i % 2 == 0 else 2)) for i in range(...  4.38 us
    ppermute x1, starting transfers between devices, on_device(): power = power + lax.ppermute(power, 'head', swap(features // width, bit))  3.11 us
    ppermute x2, starting transfers between devices, two_steps(): lax.ppermute(x, 'ctx', [(i, i ^ (2 if i % 2 == 0 else 4)) for i in range(...  2.55 us
    pallas_call x1, Pallas kernels, scale(): pl.pallas_call(lambda *refs: scale_kernel(features, *refs), in_specs=[SCA...  2.35 us
    pallas_call x4, Pallas kernels, mix(): pl.pallas_call(lambda *refs: mix_kernel(mine, heads, first, last, *refs),...  2.22 us
    ppermute x1, starting transfers between devices, on_device(): lax.ppermute(power, 'head', swap(features // width, 1))  2.14 us
  transfers between devices with their start and end apart: 9, of which 6 were waited for; matrix products, arithmetic and copies ran while one was open for 1% of the time, Pallas kernels for 35%

profile of v4, /device:TPU:0, one launch (start us, length us, event | category | flops | bytes accessed | tf_op | source)
XLA Modules:
  0.0 35.7 jit_solution(17916783375732440701)
XLA Ops:
  0.0 2.7 %states.2 = (f32[1024,128]{1,0:T(8,128)S(1)}, bf16[3072,128]{1,0:T(8,128)(2,1)S(1)}, bf16[1024,1024]{1,0:T(8,128)(2,1)S(1)}, bf16[1024,1024]{1,0:T(8,128)(2,1)S(1)}, f32[8,128]{1,0:T(8,128)S(1)}) custom-call(s32[1]{0:T(128)} %bitcast.refs_0_, bf16[1024,2048]{1,0:T(8,128)(2,1)} %refs_1_.11, bf16[1024,2048]{1,0:T(8,128)(2,1)} %refs_2_.3, s32[8]{0:T(128)} %refs_3_.1), custom_call_target="tpu_custom_call" | custom-call | flops 268435456 | bytes 4194304 | tf_op jit(solution)/shard_map/states/pallas_call | solution.py:112
  2.7 0.0 copy-start
  2.7 0.5 %collective-permute-start = (f32[1024,128]{1,0:T(8,128)S(1)}, f32[1024,128]{1,0:T(8,128)S(1)}, u32[]{:S(2)}, u32[]{:S(2)}) collective-permute-start(f32[1024,128]{1,0:T(8,128)S(1)} %get-tuple-element.36), channel_id=1, source_target_pairs={{0,4},{4,0},{8,12},{12,8},{16,20},{20,16},{24,28},{28,24},{1,5},{5... | collective-permute-start | bytes 1572872 | tf_op jit(solution)/shard_map/ppermute | solution.py:347
  3.2 3.0 %states.3 = (f32[512,128]{1,0:T(8,128)S(1)}, f32[512,128]{1,0:T(8,128)S(1)}, bf16[3072,128]{1,0:T(8,128)(2,1)S(1)}, bf16[1024,1024]{1,0:T(8,128)(2,1)S(1)}, bf16[1024,1024]{1,0:T(8,128)(2,1)S(1)}) custom-call(s32[1]{0:T(128)} %bitcast.refs_0_, bf16[1024,2048]{1,0:T(8,128)(2,1)} %refs_1_.11, bf16[1024,2048]{1,0:T(8,128)(2,1)} %refs_2_.3), custom_call_target="tpu_custom_call" | custom-call | flops 268435456 | bytes 4194304 | tf_op jit(solution)/shard_map/states/pallas_call | solution.py:112
  6.3 0.1 slice_add_fusion
  6.3 2.5 %collective-permute-start.2 = (f32[512,128]{1,0:T(8,128)S(1)}, f32[512,128]{1,0:T(8,128)S(1)}, u32[]{:S(2)}, u32[]{:S(2)}) collective-permute-start(f32[512,128]{1,0:T(8,128)S(1)} %get-tuple-element.61.refs_5_), channel_id=1, source_target_pairs={{0,8},{4,20},{8,0},{12,28},{16,24},{20,4},{24,16},{28,12},{1,9},{5... | collective-permute-start | bytes 786440 | tf_op jit(solution)/shard_map/ppermute | solution.py:329
  8.8 0.1 collective-permute-start.1
  8.9 2.9 %inner.2 = (f32[1024,1024]{1,0:T(8,128)S(1)}, f32[1,128]{1,0:T(1,128)S(1)}) custom-call(s32[1]{0:T(128)} %bitcast.refs_0_, bf16[1024,2048]{1,0:T(8,128)(2,1)S(1)} %copy-done, bf16[1024,1024]{1,0:T(8,128)(2,1)S(1)} %get-tuple-element.38.refs_2_, bf16[1024,1024]{1,0:T(8,128)(2,1)S(1)} %get-tuple-element.39.refs_3_, ...), custom_call_target="tpu_custom_call" | custom-call | flops 1610612736 | bytes 12582912 | tf_op jit(solution)/shard_map/inner/pallas_call | solution.py:175
  11.8 1.3 %collective-permute-done.2 = f32[512,128]{1,0:T(8,128)S(1)} collective-permute-done((f32[512,128]{1,0:T(8,128)S(1)}, f32[512,128]{1,0:T(8,128)S(1)}, u32[]{:S(2)}, u32[]{:S(2)}) %collective-permute-start.2) | collective-permute-done | bytes 262176 | tf_op jit(solution)/shard_map/ppermute | solution.py:329
  13.2 0.1 add_add_fusion.2.after_ref
  13.2 2.1 %collective-permute-start.4 = (f32[512,128]{1,0:T(8,128)S(1)}, f32[512,128]{1,0:T(8,128)S(1)}, u32[]{:S(2)}, u32[]{:S(2)}) collective-permute-start(f32[512,128]{1,0:T(8,128)S(1)} %add_add_fusion.2.after_ref), channel_id=1, source_target_pairs={{0,16},{4,12},{8,24},{12,4},{16,0},{20,28},{24,8},{28,20},{1,17},{... | collective-permute-start | bytes 786440 | tf_op jit(solution)/shard_map/ppermute | solution.py:335
  15.3 0.6 %collective-permute-done.1 = f32[512,128]{1,0:T(8,128)S(1)} collective-permute-done((f32[512,128]{1,0:T(8,128)S(1)}, f32[512,128]{1,0:T(8,128)S(1)}, u32[]{:S(2)}, u32[]{:S(2)}) %collective-permute-start.1) | collective-permute-done | bytes 262176 | tf_op jit(solution)/shard_map/ppermute | solution.py:329
  16.0 2.3 %collective-permute-start.3 = (f32[512,128]{1,0:T(8,128)S(1)}, f32[512,128]{1,0:T(8,128)S(1)}, u32[]{:S(2)}, u32[]{:S(2)}) collective-permute-start(f32[512,128]{1,0:T(8,128)S(1)} %add_add_fusion.3.refs_5_), channel_id=1, source_target_pairs={{0,16},{4,12},{8,24},{12,4},{16,0},{20,28},{24,8},{28,20},{1,17},{... | collective-permute-start | bytes 786440 | tf_op jit(solution)/shard_map/ppermute | solution.py:335
  18.3 2.8 %inner.3 = (f32[1024,1024]{1,0:T(8,128)S(1)}, f32[1,128]{1,0:T(1,128)S(1)}) custom-call(s32[1]{0:T(128)} %bitcast.refs_0_, bf16[1024,2048]{1,0:T(8,128)(2,1)S(1)} %copy-done, bf16[1024,1024]{1,0:T(8,128)(2,1)S(1)} %get-tuple-element.31.refs_2_, bf16[1024,1024]{1,0:T(8,128)(2,1)S(1)} %get-tuple-element.32.refs_3_, ...), custom_call_target="tpu_custom_call" | custom-call | flops 1610612736 | bytes 12582912 | tf_op jit(solution)/shard_map/inner/pallas_call | solution.py:175
  21.1 0.1 multiply_add_fusion
  21.2 0.1 collective-permute-start.6
  21.3 0.5 %mix.4 = (f32[1024,512]{1,0:T(8,128)S(1)}, f32[1024,128]{1,0:T(8,128)S(1)}) custom-call(s32[1]{0:T(128)} %bitcast.refs_0_, bf16[1024,2048]{1,0:T(8,128)(2,1)S(1)} %copy-done, f32[1024,1024]{1,0:T(8,128)S(1)} %get-tuple-element.44.refs_2_, f32[512,128]{1,0:T(8,128)S(1)} %get-tuple-element.60.refs_3_), custom_call_target="tpu_custom_call" | custom-call | flops 134217728 | bytes 2097152 | tf_op jit(solution)/shard_map/mix/pallas_call | solution.py:210
  21.8 0.8 %collective-permute-done.3 = f32[512,128]{1,0:T(8,128)S(1)} collective-permute-done((f32[512,128]{1,0:T(8,128)S(1)}, f32[512,128]{1,0:T(8,128)S(1)}, u32[]{:S(2)}, u32[]{:S(2)}) %collective-permute-start.3) | collective-permute-done | bytes 262176 | tf_op jit(solution)/shard_map/ppermute | solution.py:335
  22.6 0.1 multiply_add_fusion.1
  22.7 0.1 collective-permute-start.5
  22.8 0.0 collective-permute-done.6.refs_3_
  22.8 0.5 %mix.5 = (f32[1024,512]{1,0:T(8,128)S(1)}, f32[1024,128]{1,0:T(8,128)S(1)}) custom-call(s32[1]{0:T(128)} %bitcast.refs_0_, bf16[1024,2048]{1,0:T(8,128)(2,1)S(1)} %copy-done, f32[1024,1024]{1,0:T(8,128)S(1)} %get-tuple-element.42.refs_2_, f32[512,128]{1,0:T(8,128)S(1)} %collective-permute-done.6.refs_3_, f32[1024,128]{1,0:T(8,128)S(1)} %get-tuple-element.45.after_ref.refs_4_), custom_call_target="tpu_custom_call" | custom-call | flops 134217728 | bytes 2097152 | tf_op jit(solution)/shard_map/mix/pallas_call | solution.py:210
  23.4 0.5 %mix.6 = (f32[1024,512]{1,0:T(8,128)S(1)}, f32[1024,128]{1,0:T(8,128)S(1)}) custom-call(s32[1]{0:T(128)} %bitcast.refs_0_, bf16[1024,2048]{1,0:T(8,128)(2,1)S(1)} %copy-done, f32[1024,1024]{1,0:T(8,128)S(1)} %get-tuple-element.44.refs_2_, f32[512,128]{1,0:T(8,128)S(1)} %get-tuple-element.57.refs_3_, f32[1024,128]{1,0:T(8,128)S(1)} %get-tuple-element.46.refs_4_), custom_call_target="tpu_custom_call" | custom-call | flops 134217728 | bytes 2097152 | tf_op jit(solution)/shard_map/mix/pallas_call | solution.py:210
  23.9 0.4 %collective-permute-done.5.refs_3_ = f32[512,128]{1,0:T(8,128)S(1)} collective-permute-done((f32[512,128]{1,0:T(8,128)S(1)}, f32[512,128]{1,0:T(8,128)S(1)}, u32[]{:S(2)}, u32[]{:S(2)}) %collective-permute-start.5) | collective-permute-done | bytes 262176 | tf_op jit(solution)/shard_map/ppermute | solution.py:375
  24.3 0.6 %mix.7 = (f32[1024,512]{1,0:T(8,128)S(1)}, f32[1,1024]{1,0:T(1,128)S(1)}) custom-call(s32[1]{0:T(128)} %bitcast.refs_0_, bf16[1024,2048]{1,0:T(8,128)(2,1)S(1)} %copy-done, f32[1024,1024]{1,0:T(8,128)S(1)} %get-tuple-element.42.refs_2_, f32[512,128]{1,0:T(8,128)S(1)} %collective-permute-done.5.refs_3_, f32[1024,128]{1,0:T(8,128)S(1)} %get-tuple-element.47.refs_4_), custom_call_target="tpu_custom_call" | custom-call | flops 134217728 | bytes 2097152 | tf_op jit(solution)/shard_map/mix/pallas_call | solution.py:210
  24.9 2.1 %collective-permute-start.7 = (f32[1,1024]{1,0:T(1,128)S(1)}, f32[1,1024]{1,0:T(1,128)S(1)}, u32[]{:S(2)}, u32[]{:S(2)}) collective-permute-start(f32[1,1024]{1,0:T(1,128)S(1)} %get-tuple-element.48.refs_3_), channel_id=1, source_target_pairs={{0,1},{1,0},{2,3},{3,2},{4,5},{5,4},{6,7},{7,6},{8,9},{9,8},{10,11... | collective-permute-start | bytes 12296 | tf_op jit(solution)/shard_map/ppermute | solution.py:383
  27.1 1.0 %gate.2 = (f32[1024,1024]{1,0:T(8,128)S(1)}, f32[1,1024]{1,0:T(1,128)S(1)}) custom-call(s32[1]{0:T(128)} %bitcast.refs_0_, bf16[1024,2048]{1,0:T(8,128)(2,1)S(1)} %copy-done.1, f32[1,2048]{1,0:T(1,128)S(1)} %bitcast.16, f32[1,1024]{1,0:T(1,128)S(1)} %get-tuple-element.48.refs_3_, f32[1024,512]{1,0:T(8,128)S(1)} %get-tuple-element.49.refs_4_, ...), custom_call_target="tpu_custom_call" | custom-call | flops 16777216 | bytes 4194304 | tf_op jit(solution)/shard_map/gate/pallas_call | solution.py:245
  28.1 0.5 %collective-permute-done.7 = f32[1,1024]{1,0:T(1,128)S(1)} collective-permute-done((f32[1,1024]{1,0:T(1,128)S(1)}, f32[1,1024]{1,0:T(1,128)S(1)}, u32[]{:S(2)}, u32[]{:S(2)}) %collective-permute-start.7) | collective-permute-done | bytes 4128 | tf_op jit(solution)/shard_map/ppermute | solution.py:383
  28.7 3.1 %collective-permute-start.8 = (f32[1,1024]{1,0:T(1,128)S(1)}, f32[1,1024]{1,0:T(1,128)S(1)}, u32[]{:S(2)}, u32[]{:S(2)}) collective-permute-start(f32[1,1024]{1,0:T(1,128)S(1)} %add_add_fusion.5.refs_3_), channel_id=1, source_target_pairs={{0,2},{1,3},{2,0},{3,1},{4,6},{5,7},{6,4},{7,5},{8,10},{9,11},{10,... | collective-permute-start | bytes 12296 | tf_op jit(solution)/shard_map/ppermute | solution.py:387
  31.8 0.9 %gate.3 = (f32[1024,1024]{1,0:T(8,128)S(1)}, f32[1,1024]{1,0:T(1,128)S(1)}) custom-call(s32[1]{0:T(128)} %bitcast.refs_0_, bf16[1024,2048]{1,0:T(8,128)(2,1)S(1)} %copy-done.1, f32[1,2048]{1,0:T(1,128)S(1)} %bitcast.17, f32[1,1024]{1,0:T(1,128)S(1)} %add_add_fusion.5.refs_3_, f32[1024,512]{1,0:T(8,128)S(1)} %get-tuple-element.52.refs_4_, ...), custom_call_target="tpu_custom_call" | custom-call | flops 16777216 | bytes 4194304 | tf_op jit(solution)/shard_map/gate/pallas_call | solution.py:245
  32.7 0.6 %collective-permute-done.8 = f32[1,1024]{1,0:T(1,128)S(1)} collective-permute-done((f32[1,1024]{1,0:T(1,128)S(1)}, f32[1,1024]{1,0:T(1,128)S(1)}, u32[]{:S(2)}, u32[]{:S(2)}) %collective-permute-start.8) | collective-permute-done | bytes 4128 | tf_op jit(solution)/shard_map/ppermute | solution.py:387
  33.4 2.3 %scale.1 = bf16[1024,2048]{1,0:T(8,128)(2,1)} custom-call(s32[1]{0:T(128)} %bitcast.refs_0_, f32[1024,1024]{1,0:T(8,128)S(1)} %get-tuple-element.54.refs_1_, f32[1024,1024]{1,0:T(8,128)S(1)} %get-tuple-element.55.refs_2_, f32[1,1024]{1,0:T(1,128)S(1)} %add_add_fusion.4.refs_3_), custom_call_target="tpu_custom_call" | custom-call | flops 4194304 | bytes 4194304 | tf_op jit(solution)/shard_map/scale/pallas_call | solution.py:276
  (13 shorter events, 0.1 us)
Async XLA Ops:
  2.7 6.2 %copy-start = (bf16[1024,2048]{1,0:T(8,128)(2,1)S(1)}, bf16[1024,2048]{1,0:T(8,128)(2,1)}, u32[]{:S(2)}) copy-start(bf16[1024,2048]{1,0:T(8,128)(2,1)} %refs_1_.17) | copy-start | bytes 12582916
  2.7 3.5 %collective-permute-start = (f32[1024,128]{1,0:T(8,128)S(1)}, f32[1024,128]{1,0:T(8,128)S(1)}, u32[]{:S(2)}, u32[]{:S(2)}) collective-permute-start(f32[1024,128]{1,0:T(8,128)S(1)} %get-tuple-element.36), channel_id=1, source_target_pairs={{0,4},{4,0},{8,12},{12,8},{16,20},{20,16},{24,28},{28,24},{1,5},{5... | collective-permute-start | bytes 1572872 | tf_op jit(solution)/shard_map/ppermute | solution.py:347
  6.3 6.8 %collective-permute-start.2 = (f32[512,128]{1,0:T(8,128)S(1)}, f32[512,128]{1,0:T(8,128)S(1)}, u32[]{:S(2)}, u32[]{:S(2)}) collective-permute-start(f32[512,128]{1,0:T(8,128)S(1)} %get-tuple-element.61.refs_5_), channel_id=1, source_target_pairs={{0,8},{4,20},{8,0},{12,28},{16,24},{20,4},{24,16},{28,12},{1,9},{5... | collective-permute-start | bytes 786440 | tf_op jit(solution)/shard_map/ppermute | solution.py:329
  8.8 7.2 %collective-permute-start.1 = (f32[512,128]{1,0:T(8,128)S(1)}, f32[512,128]{1,0:T(8,128)S(1)}, u32[]{:S(2)}, u32[]{:S(2)}) collective-permute-start(f32[512,128]{1,0:T(8,128)S(1)} %get-tuple-element.62), channel_id=1, source_target_pairs={{0,8},{4,20},{8,0},{12,28},{16,24},{20,4},{24,16},{28,12},{1,9},{5... | collective-permute-start | bytes 786440 | tf_op jit(solution)/shard_map/ppermute | solution.py:329
  13.2 7.9 %collective-permute-start.4 = (f32[512,128]{1,0:T(8,128)S(1)}, f32[512,128]{1,0:T(8,128)S(1)}, u32[]{:S(2)}, u32[]{:S(2)}) collective-permute-start(f32[512,128]{1,0:T(8,128)S(1)} %add_add_fusion.2.after_ref), channel_id=1, source_target_pairs={{0,16},{4,12},{8,24},{12,4},{16,0},{20,28},{24,8},{28,20},{1,17},{... | collective-permute-start | bytes 786440 | tf_op jit(solution)/shard_map/ppermute | solution.py:335
  16.0 6.6 %collective-permute-start.3 = (f32[512,128]{1,0:T(8,128)S(1)}, f32[512,128]{1,0:T(8,128)S(1)}, u32[]{:S(2)}, u32[]{:S(2)}) collective-permute-start(f32[512,128]{1,0:T(8,128)S(1)} %add_add_fusion.3.refs_5_), channel_id=1, source_target_pairs={{0,16},{4,12},{8,24},{12,4},{16,0},{20,28},{24,8},{28,20},{1,17},{... | collective-permute-start | bytes 786440 | tf_op jit(solution)/shard_map/ppermute | solution.py:335
  21.2 1.6 %collective-permute-start.6 = (f32[512,128]{1,0:T(8,128)S(1)}, f32[512,128]{1,0:T(8,128)S(1)}, u32[]{:S(2)}, u32[]{:S(2)}) collective-permute-start(f32[512,128]{1,0:T(8,128)S(1)} %get-tuple-element.59), channel_id=1, source_target_pairs={{0,4},{4,0},{8,12},{12,8},{16,20},{20,16},{24,28},{28,24},{1,5},{5... | collective-permute-start | bytes 786440 | tf_op jit(solution)/shard_map/ppermute | solution.py:375
  22.7 1.6 %collective-permute-start.5 = (f32[512,128]{1,0:T(8,128)S(1)}, f32[512,128]{1,0:T(8,128)S(1)}, u32[]{:S(2)}, u32[]{:S(2)}) collective-permute-start(f32[512,128]{1,0:T(8,128)S(1)} %get-tuple-element.58), channel_id=1, source_target_pairs={{0,4},{4,0},{8,12},{12,8},{16,20},{20,16},{24,28},{28,24},{1,5},{5... | collective-permute-start | bytes 786440 | tf_op jit(solution)/shard_map/ppermute | solution.py:375
  24.3 2.8 %copy-start.1 = (bf16[1024,2048]{1,0:T(8,128)(2,1)S(1)}, bf16[1024,2048]{1,0:T(8,128)(2,1)}, u32[]{:S(2)}) copy-start(bf16[1024,2048]{1,0:T(8,128)(2,1)} %refs_1_.19) | copy-start | bytes 12582916
  24.3 2.8 %copy-start.2 = (f32[2048]{0:T(1024)S(1)}, f32[2048]{0:T(1024)}, u32[]{:S(2)}) copy-start(f32[2048]{0:T(1024)} %param.10) | copy-start | bytes 24580
  24.9 3.7 %collective-permute-start.7 = (f32[1,1024]{1,0:T(1,128)S(1)}, f32[1,1024]{1,0:T(1,128)S(1)}, u32[]{:S(2)}, u32[]{:S(2)}) collective-permute-start(f32[1,1024]{1,0:T(1,128)S(1)} %get-tuple-element.48.refs_3_), channel_id=1, source_target_pairs={{0,1},{1,0},{2,3},{3,2},{4,5},{5,4},{6,7},{7,6},{8,9},{9,8},{10,11... | collective-permute-start | bytes 12296 | tf_op jit(solution)/shard_map/ppermute | solution.py:383
  28.7 4.7 %collective-permute-start.8 = (f32[1,1024]{1,0:T(1,128)S(1)}, f32[1,1024]{1,0:T(1,128)S(1)}, u32[]{:S(2)}, u32[]{:S(2)}) collective-permute-start(f32[1,1024]{1,0:T(1,128)S(1)} %add_add_fusion.5.refs_3_), channel_id=1, source_target_pairs={{0,2},{1,3},{2,0},{3,1},{4,6},{5,7},{6,4},{7,5},{8,10},{9,11},{10,... | collective-permute-start | bytes 12296 | tf_op jit(solution)/shard_map/ppermute | solution.py:387

commit v5 on v4

--- a/solution.py
+++ b/solution.py
@@ -57,69 +57,123 @@
     return pl.ds(pl.multiple_of((core if mine else 1 - core) * half, half), half)
 
 
-def states_kernel(mine, planned, groups, place_ref, key_ref, value_ref, *refs):
-    if planned:
-        session_ref, *refs = refs
-    state_refs, refs = refs[:groups], refs[groups:]
-    if planned:
-        before_ref, keys, vals, weight_ref, sems, sessions, session_sem = refs
-        session_copy = pltpu.make_async_copy(session_ref, sessions, session_sem)
-        session_copy.start()
-    else:
-        before_ref, keys, vals, sems = refs
-    tokens, half = keys.shape
-    cols = columns(place_ref, mine, half)
+def group_sizes(heads):
+    return [(heads + GROUPS - 1 - g) // GROUPS for g in range(GROUPS)]
+
+
+def fetch(copies, sems, place_ref, mine, pairs, chunks, base=0):
+    for c in chunks:
+        for source, to in pairs:
+            cols = columns(place_ref, mine, to.shape[1])
+            rows = slice((c - base) * CHUNK, (c - base + 1) * CHUNK)
+            copies.append(pltpu.make_async_copy(source.at[chunk(c), cols], to.at[rows, :], sems.at[len(copies)]))
+            copies[-1].start()
+
+
+def add_chunk(c, keys, vals, rows, state_refs, before_ref):
+    half = keys.shape[1]
+    h = 0
+    for state_ref in state_refs:
+        for j in range(state_ref.shape[0] // HEAD_DIM):
+            new = dot_tn(keys[rows, head(h)], vals[rows, head(h)])
+            if c == 0:
+                state_ref[head(j), :] = new
+            else:
+                old = state_ref[head(j), :]
+                at = (c - 1) * half + h * HEAD_DIM
+                before_ref[at : at + HEAD_DIM, :] = old.astype(BF16)
+                state_ref[head(j), :] = old + new
+            h += 1
+
+
+def sent_kernel(place_ref, session_ref, key_ref, value_ref, state_ref, before_ref, keys, vals,
+                next_keys, next_vals, weight_ref, sems, sessions, session_sem):
+    chunks = keys.shape[0] // CHUNK
+    early = next_keys.shape[0] // CHUNK
+    session_copy = pltpu.make_async_copy(session_ref, sessions, session_sem)
+    session_copy.start()
     copies = []
-    for c in range(tokens // CHUNK):
-        for j, (source, to) in enumerate(((key_ref, keys), (value_ref, vals))):
-            copies.append(pltpu.make_async_copy(source.at[chunk(c), cols], to.at[chunk(c), :], sems.at[2 * c + j]))
-            copies[-1].start()
-    if planned:
-        session_copy.wait()
-        write_weights(place_ref, sessions, weight_ref)
-    for c in range(tokens // CHUNK):
+    fetch(copies, sems, place_ref, False, ((key_ref, keys), (value_ref, vals)), range(chunks))
+    fetch(copies, sems, place_ref, True, ((key_ref, next_keys), (value_ref, next_vals)), range(early))
+    session_copy.wait()
+    write_weights(place_ref, sessions, weight_ref)
+    for c in range(chunks):
         copies[2 * c].wait()
         copies[2 * c + 1].wait()
-        for h in range(half // HEAD_DIM):
-            new = dot_tn(keys[chunk(c), head(h)], vals[chunk(c), head(h)])
-            per = half // HEAD_DIM // groups
-            state_ref, rows = state_refs[h // per], head(h % per)
-            if c == 0:
-                state_ref[rows, :] = new
-            else:
-                old = state_ref[rows, :]
-                at = (c - 1) * half + h * HEAD_DIM
-                before_ref[at : at + HEAD_DIM, :] = old.astype(BF16)
-                state_ref[rows, :] = old + new
-
-
-def half_states(place, key_rows, values, mine, groups, session_of=None):
+        add_chunk(c, keys, vals, chunk(c), [state_ref], before_ref)
+    for copy in copies[2 * chunks :]:
+        copy.wait()
+
+
+def sent_states(place, session_of, key_rows, values):
     tokens, width = key_rows.shape
     half = width // 2
     chunks = tokens // CHUNK
-    planned = session_of is not None
-    out_shape = [pltpu.VMEM((half // groups, HEAD_DIM), F32)] * groups + [
+    early = chunks // 2
+    return pl.pallas_call(
+        sent_kernel,
+        in_specs=[SCALARS] + [ANYWHERE] * 3,
+        out_specs=[WHOLE] * 7,
+        out_shape=[
+            pltpu.VMEM((half, HEAD_DIM), F32),
+            pltpu.VMEM(((chunks - 1) * half, HEAD_DIM), BF16),
+            pltpu.VMEM((tokens, half), BF16),
+            pltpu.VMEM((tokens, half), BF16),
+            pltpu.VMEM((early * CHUNK, half), BF16),
+            pltpu.VMEM((early * CHUNK, half), BF16),
+            pltpu.VMEM((8, HEAD_DIM), F32),
+        ],
+        scratch_shapes=[
+            pltpu.SemaphoreType.DMA((2 * chunks + 2 * early,)),
+            pltpu.SMEM(session_of.shape, jnp.int32),
+            pltpu.SemaphoreType.DMA(()),
+        ],
+        compiler_params=params(8),
+        cost_estimate=cost(tokens * width * HEAD_DIM, 3 * tokens * width),
+        name="states",
+    )(place, in_hbm(session_of), in_hbm(key_rows), in_hbm(values))
+
+
+def kept_kernel(place_ref, key_ref, value_ref, query_ref, first_keys, first_vals, *refs):
+    *state_refs, before_ref, keys, vals, queries, sems = refs
+    early = first_keys.shape[0] // CHUNK
+    chunks = early + keys.shape[0] // CHUNK
+    copies = []
+    fetch(copies, sems, place_ref, True, ((key_ref, keys), (value_ref, vals)), range(early, chunks), early)
+    fetch(copies, sems, place_ref, True, ((query_ref, queries),), range(early))
+    for c in range(early):
+        add_chunk(c, first_keys, first_vals, chunk(c), state_refs, before_ref)
+    for c in range(early, chunks):
+        copies[2 * (c - early)].wait()
+        copies[2 * (c - early) + 1].wait()
+        add_chunk(c, keys, vals, chunk(c - early), state_refs, before_ref)
+    for copy in copies[2 * (chunks - early) :]:
+        copy.wait()
+
+
+def kept_states(place, key_rows, values, queries, first_keys, first_vals):
+    tokens, width = key_rows.shape
+    half = width // 2
+    chunks = tokens // CHUNK
+    late = tokens - first_keys.shape[0]
+    sizes = group_sizes(half // HEAD_DIM)
+    out_shape = [pltpu.VMEM((n * HEAD_DIM, HEAD_DIM), F32) for n in sizes] + [
         pltpu.VMEM(((chunks - 1) * half, HEAD_DIM), BF16),
-        pltpu.VMEM((tokens, half), BF16),
-        pltpu.VMEM((tokens, half), BF16),
+        pltpu.VMEM((late, half), BF16),
+        pltpu.VMEM((late, half), BF16),
+        pltpu.VMEM((tokens - late, half), BF16),
     ]
-    scratch_shapes = [pltpu.SemaphoreType.DMA((2 * chunks,))]
-    operands = [place, in_hbm(key_rows), in_hbm(values)]
-    if planned:
-        out_shape += [pltpu.VMEM((8, HEAD_DIM), F32)]
-        scratch_shapes += [pltpu.SMEM(session_of.shape, jnp.int32), pltpu.SemaphoreType.DMA(())]
-        operands += [in_hbm(session_of)]
     results = pl.pallas_call(
-        lambda *refs: states_kernel(mine, planned, groups, *refs),
-        in_specs=[SCALARS] + [ANYWHERE] * (len(operands) - 1),
+        kept_kernel,
+        in_specs=[SCALARS] + [ANYWHERE] * 3 + [WHOLE] * 2,
         out_specs=[WHOLE] * len(out_shape),
         out_shape=out_shape,
-        scratch_shapes=scratch_shapes,
-        compiler_params=params(8),
-        cost_estimate=cost(tokens * width * HEAD_DIM, 2 * tokens * width),
+        scratch_shapes=[pltpu.SemaphoreType.DMA((chunks + late // CHUNK,))],
+        compiler_params=params(8),
+        cost_estimate=cost(tokens * width * HEAD_DIM, tokens * width),
         name="states",
-    )(*operands)
-    return results[:groups], results[groups:]
+    )(place, in_hbm(key_rows), in_hbm(values), in_hbm(queries), in_vmem(first_keys), in_vmem(first_vals))
+    return results[: len(sizes)], results[len(sizes) :]
 
 
 def write_weights(place_ref, session_ref, weight_ref):
@@ -135,9 +189,11 @@
         return flag(jnp.logical_and(source < to, same))
 
     even = core == 0
-    partner = jnp.where(even, chip ^ 1, chip ^ 2)
-    to = jnp.where(even, chip ^ 2, chip ^ 1)
-    rows = [flag(even), flag(core == 1), need(to, chip), need(to, partner), need(chip, partner)]
+    rows = [flag(even), flag(core == 1)]
+    if session_ref.shape[0] == 8:
+        partner = jnp.where(even, chip ^ 1, chip ^ 2)
+        to = jnp.where(even, chip ^ 2, chip ^ 1)
+        rows += [need(to, chip), need(to, partner), need(chip, partner)]
     for r, value in enumerate(rows):
         weight_ref[r : r + 1, :] = jnp.full((1, HEAD_DIM), value, F32)
 
@@ -147,51 +203,103 @@
     return lambda h: pl.ds(pl.multiple_of(start + h * HEAD_DIM, HEAD_DIM), HEAD_DIM)
 
 
-def inner_kernel(mine, place_ref, query_ref, key_ref, value_ref, before_ref, after_ref, inner_ref, zero_ref):
-    tokens, half = key_ref.shape
-    heads = range(half // HEAD_DIM)
-    columns_of = half_heads(place_ref, mine, half)
+def chunk_in(refs, c):
+    for ref in refs:
+        chunks = ref.shape[0] // CHUNK
+        if c < chunks:
+            return ref, chunk(c)
+        c -= chunks
+
+
+def inner_body(chunks, waits, query_refs, key_refs, value_refs, before_ref, inner_refs, zero_ref):
     zero_ref[...] = jnp.zeros_like(zero_ref)
     rows_at = lax.broadcasted_iota(jnp.int32, (CHUNK, CHUNK), 0)
     cols_at = lax.broadcasted_iota(jnp.int32, (CHUNK, CHUNK), 1)
     causal = rows_at >= cols_at
-    for c in range(tokens // CHUNK):
+    homes = [(ref, j) for ref in inner_refs for j in range(ref.shape[1] // HEAD_DIM)]
+    half = len(homes) * HEAD_DIM
+    for c in range(chunks):
+        if c in waits:
+            waits[c].wait()
+        (query_ref, q), (key_ref, k), (value_ref, v) = (chunk_in(x, c) for x in (query_refs, key_refs, value_refs))
         scores = []
-        for h in heads:
-            full = dot_nt(query_ref[chunk(c), columns_of(h)], key_ref[chunk(c), head(h)])
+        for h in range(len(homes)):
+            full = dot_nt(query_ref[q, head(h)], key_ref[k, head(h)])
             scores.append(jnp.where(causal, full, 0.0).astype(BF16))
-        for h in heads:
-            left, right = scores[h], value_ref[chunk(c), head(h)]
+        for h, (inner_ref, j) in enumerate(homes):
+            left, right = scores[h], value_ref[v, head(h)]
             if c > 0:
                 at = (c - 1) * half + h * HEAD_DIM
-                left = jnp.concatenate([left, query_ref[chunk(c), columns_of(h)]], axis=1)
+                left = jnp.concatenate([left, query_ref[q, head(h)]], axis=1)
                 right = jnp.concatenate([right, before_ref[at : at + HEAD_DIM, :]], axis=0)
-            inner_ref[chunk(c), head(h)] = dot_nn(left, right)
-
-
-def half_inner(place, queries, half_of_heads, after, mine):
-    before, keys, vals = half_of_heads[:3]
-    tokens, half = keys.shape
-    return pl.pallas_call(
-        lambda *refs: inner_kernel(mine, *refs),
-        in_specs=[SCALARS, WHOLE, WHOLE, WHOLE, WHOLE, ANYWHERE],
-        out_specs=[WHOLE] * 2,
-        out_shape=[pltpu.VMEM((tokens, half), F32), pltpu.VMEM((1, HEAD_DIM), F32)],
+            inner_ref[chunk(c), head(j)] = dot_nn(left, right)
+
+
+def mine_kernel(place_ref, query_ref, after_ref, first_queries, key_first, key_late, value_first, value_late,
+                before_ref, late_queries, other_queries, *refs):
+    *inner_refs, zero_ref, sems = refs
+    chunks = other_queries.shape[0] // CHUNK
+    early = first_queries.shape[0] // CHUNK
+    copies = []
+    fetch(copies, sems, place_ref, True, ((query_ref, late_queries),), range(early, chunks), early)
+    fetch(copies, sems, place_ref, False, ((query_ref, other_queries),), range(chunks))
+    waits = {c: copies[c - early] for c in range(early, chunks)}
+    inner_body(
+        chunks, waits, (first_queries, late_queries), (key_first, key_late), (value_first, value_late),
+        before_ref, inner_refs, zero_ref,
+    )
+    for copy in copies[chunks - early :]:
+        copy.wait()
+
+
+def mine_inner(place, queries, first_queries, keys, vals, before, after, sizes):
+    tokens, width = queries.shape
+    half = width // 2
+    late = tokens - first_queries.shape[0]
+    out_shape = [pltpu.VMEM((late, half), BF16), pltpu.VMEM((tokens, half), BF16)]
+    out_shape += [pltpu.VMEM((tokens, n * HEAD_DIM), F32) for n in sizes] + [pltpu.VMEM((1, HEAD_DIM), F32)]
+    return pl.pallas_call(
+        mine_kernel,
+        in_specs=[SCALARS, ANYWHERE, ANYWHERE] + [WHOLE] * 6,
+        out_specs=[WHOLE] * len(out_shape),
+        out_shape=out_shape,
+        scratch_shapes=[pltpu.SemaphoreType.DMA(((late + tokens) // CHUNK,))],
         compiler_params=params(8),
         cost_estimate=cost(tokens * half * 6 * CHUNK, 12 * tokens * half),
         name="inner",
-    )(place, in_vmem(queries), in_vmem(keys), in_vmem(vals), in_vmem(before), after)
-
-
-def mix_kernel(mine, heads, first, last, place_ref, query_ref, inner_ref, prefix_ref, *refs):
+    )(place, in_hbm(queries), after, *[in_vmem(x) for x in (first_queries, *keys, *vals, before)])
+
+
+def other_kernel(after_ref, query_ref, key_ref, value_ref, before_ref, *refs):
+    *inner_refs, zero_ref = refs
+    chunks = query_ref.shape[0] // CHUNK
+    inner_body(chunks, {}, (query_ref,), (key_ref,), (value_ref,), before_ref, inner_refs, zero_ref)
+
+
+def other_inner(queries, keys, vals, before, after, sizes):
+    tokens, half = queries.shape
+    out_shape = [pltpu.VMEM((tokens, n * HEAD_DIM), F32) for n in sizes] + [pltpu.VMEM((1, HEAD_DIM), F32)]
+    return pl.pallas_call(
+        other_kernel,
+        in_specs=[ANYWHERE] + [WHOLE] * 4,
+        out_specs=[WHOLE] * len(out_shape),
+        out_shape=out_shape,
+        compiler_params=params(8),
+        cost_estimate=cost(tokens * half * 6 * CHUNK, 12 * tokens * half),
+        name="inner",
+    )(after, *[in_vmem(x) for x in (queries, keys, vals, before)])
+
+
+def mix_kernel(parts, first_head, first, last, *refs):
+    query_refs, (inner_ref, prefix_ref, *refs) = refs[:parts], refs[parts:]
     extra_ref, mixed_ref, result_ref = (None, *refs) if first else refs
-    tokens, half = inner_ref.shape
-    columns_of = half_heads(place_ref, mine, half)
-    blocks = [prefix_ref[head(j), :].astype(BF16) for j in range(len(heads))]
-    for c in range(tokens // CHUNK):
+    heads = range(inner_ref.shape[1] // HEAD_DIM)
+    blocks = [prefix_ref[head(j), :].astype(BF16) for j in heads]
+    for c in range(inner_ref.shape[0] // CHUNK):
         squares = None if first else extra_ref[chunk(c), :]
-        for j, h in enumerate(heads):
-            mixed = inner_ref[chunk(c), head(h)] + dot_nn(query_ref[chunk(c), columns_of(h)], blocks[j])
+        query_ref, q = chunk_in(query_refs, c)
+        for j in heads:
+            mixed = inner_ref[chunk(c), head(j)] + dot_nn(query_ref[q, head(first_head + j)], blocks[j])
             square = mixed * mixed
             squares = square if squares is None else squares + square
             mixed_ref[chunk(c), head(j)] = mixed
@@ -201,24 +309,22 @@
             result_ref[chunk(c), :] = squares
 
 
-def mix(place, queries, inner, prefix, squares, mine, group, last):
-    tokens, half = inner.shape
-    count = prefix.shape[0] // HEAD_DIM
-    heads = range(group * count, (group + 1) * count)
+def mix(queries, inner_group, prefix, squares, first_head, last):
+    tokens = inner_group.shape[0]
     first = squares is None
-    operands = [queries, inner, prefix] + ([] if first else [squares])
-    return pl.pallas_call(
-        lambda *refs: mix_kernel(mine, heads, first, last, *refs),
-        in_specs=[SCALARS] + [WHOLE] * len(operands),
+    operands = [*queries, inner_group, prefix] + ([] if first else [squares])
+    return pl.pallas_call(
+        lambda *refs: mix_kernel(len(queries), first_head, first, last, *refs),
+        in_specs=[WHOLE] * len(operands),
         out_specs=[WHOLE, WHOLE],
         out_shape=[
-            pltpu.VMEM((tokens, count * HEAD_DIM), F32),
+            pltpu.VMEM(inner_group.shape, F32),
             pltpu.VMEM((1, tokens) if last else (tokens, HEAD_DIM), F32),
         ],
         compiler_params=params(8),
-        cost_estimate=cost(2 * tokens * prefix.size, 2 * tokens * half),
+        cost_estimate=cost(2 * tokens * prefix.size, 12 * inner_group.size),
         name="mix",
-    )(place, *[in_vmem(x) for x in operands])
+    )(*[in_vmem(x) for x in operands])
 
 
 def gate_kernel(mine, place_ref, gate_ref, gain_ref, after_ref, *refs):
@@ -227,14 +333,14 @@
     zero_ref[...] = jnp.zeros_like(zero_ref)
     rows = HEAD_DIM
     columns_of = half_heads(place_ref, mine, half)
-    per = half // HEAD_DIM // len(mixed_refs)
+    homes = [(ref, j) for ref in mixed_refs for j in range(ref.shape[1] // HEAD_DIM)]
 
     def step(i, carry):
         at = pl.ds(pl.multiple_of(i * rows, rows), rows)
-        for h in range(half // HEAD_DIM):
+        for h, (mixed_ref, j) in enumerate(homes):
             gate = gate_ref[at, columns_of(h)].astype(F32)
             factor = (0.5 * gain_ref[:, columns_of(h)]) * (1.0 + jnp.tanh(0.5 * gate))
-            gated_ref[at, head(h)] = mixed_refs[h // per][at, head(h % per)] * factor
+            gated_ref[at, head(h)] = mixed_ref[at, head(j)] * factor
         return carry
 
     lax.fori_loop(0, tokens // rows, step, 0)
@@ -341,31 +447,38 @@
     width = queries.shape[1]
     index = lax.axis_index("ctx").astype(jnp.int32)
     place = index.reshape(1)
-    group_rows = width // 2 // GROUPS
-
-    (sent,), sent_half = half_states(place, key_rows, values, False, 1, session_of if blocks == 8 else None)
+    sizes = group_sizes(width // 2 // HEAD_DIM)
+    starts = [sum(sizes[:g]) for g in range(GROUPS)]
+
+    sent, sent_before, sent_keys, sent_vals, first_keys, first_vals, weight = sent_states(
+        place, session_of, key_rows, values
+    )
     got = lax.ppermute(sent, "ctx", swap(blocks, 1))
-    kept, kept_half = half_states(place, key_rows, values, True, GROUPS)
-    got = [got[g * group_rows : (g + 1) * group_rows] for g in range(GROUPS)]
+    kept, (kept_before, late_keys, late_vals, first_queries) = kept_states(
+        place, key_rows, values, queries, first_keys, first_vals
+    )
+    got = [got[at * HEAD_DIM : (at + n) * HEAD_DIM] for at, n in zip(starts, sizes)]
     sums = [x + y for x, y in zip(kept, got)]
-    inner = {}
-
-    def inner_of(half, mine):
-        def run(after):
-            inner[mine], zero = half_inner(place, queries, half, after, mine)
-            return zero
-
-        return run
+    inside, held = {}, {}
+
+    def mine_inside(after):
+        keys, vals = (first_keys, late_keys), (first_vals, late_vals)
+        late_queries, other_queries, *inside[True], zero = mine_inner(
+            place, queries, first_queries, keys, vals, kept_before, after, sizes
+        )
+        held[True], held[False] = (first_queries, late_queries), (other_queries,)
+        return zero
+
+    def other_inside(after):
+        *inside[False], zero = other_inner(*held[False], sent_keys, sent_vals, sent_before, after, sizes)
+        return zero
 
     if blocks == 8:
-        weight = sent_half[3]
-        prefixes = two_steps(sums, weight, inner_of(kept_half, True), inner_of(sent_half, False))
-        even, odd = weight[0:1], weight[1:2]
+        prefixes = two_steps(sums, weight, mine_inside, other_inside)
     else:
-        zero = inner_of(kept_half, True)(sums[0]) + inner_of(sent_half, False)(sums[0])
+        zero = mine_inside(sums[0]) + other_inside(sums[0])
         prefixes = [general_prefix(blocks, index >> 1, session_of, x) + zero for x in sums]
-        odd = (index & 1).astype(F32)
-        even = 1.0 - odd
+    even, odd = weight[0:1], weight[1:2]
 
     mixed = {True: [], False: []}
     squares = None
@@ -373,10 +486,11 @@
     for g, prefix in enumerate(prefixes):
         prefix = prefix + zero
         other = lax.ppermute(prefix + even * kept[g], "ctx", swap(blocks, 1))
-        part, squares = mix(place, queries, inner[True], prefix + odd * got[g], squares, True, g, False)
+        mine = prefix + odd * got[g]
+        part, squares = mix(held[True], inside[True][g], mine, squares, starts[g], False)
         mixed[True].append(part)
         zero = zero_after(squares)
-        part, squares = mix(place, queries, inner[False], other, squares, False, g, g == GROUPS - 1)
+        part, squares = mix(held[False], inside[False][g], other, squares, starts[g], g == GROUPS - 1)
         mixed[False].append(part)
     power = squares
     gated_other, zero = gated(place, mixed[False], gate_input, norm_gain, power, False)

time: 35.9 us -> 35.5 us (0.989)
  waiting for transfers between devices: 4.34 us -> 3.38 us
  Pallas kernels: 18 us -> 18.4 us
    ppermute x2, waiting for transfers between devices: 1.95 us -> 0.71 us  [two_steps(): lax.ppermute(x, 'ctx', [(i, i ^ (2 if i % 2 == 0 else 4)) for i in range(...]
    pallas_call x8, Pallas kernels: 13.7 us -> 14.1 us  [the longest x1 4.17 us: mine_inner(): pl.pallas_call(mine_kernel, in_specs=[SCALARS, ANYWHERE, ANYWHERE] + [WHO...]
  transfers between devices with their start and end apart: 9 -> 9, of which waited for: 6 -> 6; matrix products, arithmetic and copies ran while one was open for 1% -> 1% of each run, Pallas kernels for 35% -> 36%
where the time goes in v5:
time: 35.5 us; the launch traced here: 35.4 us
  Pallas kernels  18.4 us (52%)
  starting transfers between devices  13 us (37%)
  waiting for transfers between devices  3.38 us (10%)
  other arithmetic  0.38 us (1%)
    ppermute x2, starting transfers between devices, two_steps(): lax.ppermute(x, 'ctx', [(i, i ^ (4 if i % 2 == 0 else 2)) for i in range(...  4.45 us
    pallas_call x1, Pallas kernels, mine_inner(): pl.pallas_call(mine_kernel, in_specs=[SCALARS, ANYWHERE, ANYWHERE] + [WHO...  4.17 us
    ppermute x1, starting transfers between devices, on_device(): power = power + lax.ppermute(power, 'head', swap(features // width, bit))  3.1 us
    pallas_call x1, Pallas kernels, sent_states(): pl.pallas_call(sent_kernel, in_specs=[SCALARS] + [ANYWHERE] * 3, out_spec...  2.88 us
    pallas_call x1, Pallas kernels, other_inner(): pl.pallas_call(other_kernel, in_specs=[ANYWHERE] + [WHOLE] * 4, out_specs...  2.84 us
    ppermute x2, starting transfers between devices, two_steps(): lax.ppermute(x, 'ctx', [(i, i ^ (2 if i % 2 == 0 else 4)) for i in range(...  2.66 us
    pallas_call x1, Pallas kernels, scale(): pl.pallas_call(lambda *refs: scale_kernel(features, *refs), in_specs=[SCA...  2.36 us
    pallas_call x1, Pallas kernels, kept_states(): pl.pallas_call(kept_kernel, in_specs=[SCALARS] + [ANYWHERE] * 3 + [WHOLE]...  2.33 us
  transfers between devices with their start and end apart: 9, of which 6 were waited for; matrix products, arithmetic and copies ran while one was open for 1% of the time, Pallas kernels for 36%

profile of v5, /device:TPU:0, one launch (start us, length us, event | category | flops | bytes accessed | tf_op | source)
XLA Modules:
  0.0 35.4 jit_solution(14262557815494018575)
XLA Ops:
  0.0 2.9 %states.2 = (f32[1024,128]{1,0:T(8,128)S(1)}, bf16[3072,128]{1,0:T(8,128)(2,1)S(1)}, bf16[1024,1024]{1,0:T(8,128)(2,1)S(1)}, bf16[1024,1024]{1,0:T(8,128)(2,1)S(...) custom-call(s32[1]{0:T(128)} %bitcast.place_ref.refs_0_, s32[8]{0:T(128)} %session_ref.1, ...), custom_call_target="tpu_custom_call" | custom-call | flops 268435456 | bytes 6291456 | tf_op jit(solution)/shard_map/states/pallas_call | solution.py:113
  2.9 0.5 %collective-permute-start = (f32[1024,128]{1,0:T(8,128)S(1)}, f32[1024,128]{1,0:T(8,128)S(1)}, u32[]{:S(2)}, u32[]{:S(2)}) collective-permute-start(f32[1024,128]{1,0:T(8,128)S(1)} %get-tuple-element.41), channel_id=1, source_target_pairs={{0,4},{4,0},{8,12},{12,8},{16,20},{20,16},{24,28},{28,24},{1,5},{5... | collective-permute-start | bytes 1572872 | tf_op jit(solution)/shard_map/ppermute | solution.py:456
  3.4 2.3 %states.3 = (f32[512,128]{1,0:T(8,128)S(1)}, f32[512,128]{1,0:T(8,128)S(1)}, bf16[3072,128]{1,0:T(8,128)(2,1)S(1)}, bf16[512,1024]{1,0:T(8,128)(2,1)S(1)}, bf16[...) custom-call(s32[1]{0:T(128)} %bitcast.place_ref.refs_0_, bf16[1024,2048]{1,0:T(8,128)(2,1)} %key_ref.3, ...), custom_call_target="tpu_custom_call" | custom-call | flops 268435456 | bytes 2097152 | tf_op jit(solution)/shard_map/states/pallas_call | solution.py:166
  5.7 0.0 collective-permute-done
  5.8 0.1 slice_add_fusion
  5.8 2.6 %collective-permute-start.2 = (f32[512,128]{1,0:T(8,128)S(1)}, f32[512,128]{1,0:T(8,128)S(1)}, u32[]{:S(2)}, u32[]{:S(2)}) collective-permute-start(f32[512,128]{1,0:T(8,128)S(1)} %get-tuple-element.76.after_ref), channel_id=1, source_target_pairs={{0,8},{4,20},{8,0},{12,28},{16,24},{20,4},{24,16},{28,12},{1,9},{5... | collective-permute-start | bytes 786440 | tf_op jit(solution)/shard_map/ppermute | solution.py:435
  8.4 0.1 collective-permute-start.1
  8.5 4.2 %inner.2 = (bf16[512,1024]{1,0:T(8,128)(2,1)S(1)}, bf16[1024,1024]{1,0:T(8,128)(2,1)S(1)}, f32[1024,512]{1,0:T(8,128)S(1)}, f32[1024,512]{1,0:T(8,128)S(1)}, f32[1,128]{1,0:T(1,128)S(1)}) custom-call(s32[1]{0:T(128)} %bitcast.place_ref.refs_0_, bf16[1024,2048]{1,0:T(8,128)(2,1)} %query_ref.3, f32[512,128]{1,0:T(8,128)S(1)} %get-tuple-element.76.after_ref, ...), custom_call_target="tpu_custom_call" | custom-call | flops 1610612736 | bytes 12582912 | tf_op jit(solution)/shard_map/inner/pallas_call | solution.py:261
  12.7 0.1 collective-permute-done.2
  12.8 0.1 add_add_fusion.2.after_ref
  12.8 2.1 %collective-permute-start.4 = (f32[512,128]{1,0:T(8,128)S(1)}, f32[512,128]{1,0:T(8,128)S(1)}, u32[]{:S(2)}, u32[]{:S(2)}) collective-permute-start(f32[512,128]{1,0:T(8,128)S(1)} %add_add_fusion.2.after_ref), channel_id=1, source_target_pairs={{0,16},{4,12},{8,24},{12,4},{16,0},{20,28},{24,8},{28,20},{1,17},{... | collective-permute-start | bytes 786440 | tf_op jit(solution)/shard_map/ppermute | solution.py:441
  14.9 0.6 %collective-permute-done.1 = f32[512,128]{1,0:T(8,128)S(1)} collective-permute-done((f32[512,128]{1,0:T(8,128)S(1)}, f32[512,128]{1,0:T(8,128)S(1)}, u32[]{:S(2)}, u32[]{:S(2)}) %collective-permute-start.1) | collective-permute-done | bytes 262176 | tf_op jit(solution)/shard_map/ppermute | solution.py:435
  15.6 2.3 %collective-permute-start.3 = (f32[512,128]{1,0:T(8,128)S(1)}, f32[512,128]{1,0:T(8,128)S(1)}, u32[]{:S(2)}, u32[]{:S(2)}) collective-permute-start(f32[512,128]{1,0:T(8,128)S(1)} %add_add_fusion.3.after_ref), channel_id=1, source_target_pairs={{0,16},{4,12},{8,24},{12,4},{16,0},{20,28},{24,8},{28,20},{1,17},{... | collective-permute-start | bytes 786440 | tf_op jit(solution)/shard_map/ppermute | solution.py:441
  18.0 2.8 %inner.3 = (f32[1024,512]{1,0:T(8,128)S(1)}, f32[1024,512]{1,0:T(8,128)S(1)}, f32[1,128]{1,0:T(1,128)S(1)}) custom-call(f32[512,128]{1,0:T(8,128)S(1)} %add_add_fusion.3.after_ref, bf16[1024,1024]{1,0:T(8,128)(2,1)S(1)} %get-tuple-element.46.query_ref.refs_0_, bf16[1024,1024]{1,0:T(8,128)(2,1)S(1)} %get-tuple-element.50.key_ref, ...), custom_call_target="tpu_custom_call" | custom-call | flops 1610612736 | bytes 12582912 | tf_op jit(solution)/shard_map/inner/pallas_call | solution.py:282
  20.8 0.1 multiply_add_fusion
  20.9 0.1 collective-permute-start.6
  21.0 0.5 %mix.4 = (f32[1024,512]{1,0:T(8,128)S(1)}, f32[1024,128]{1,0:T(8,128)S(1)}) custom-call(bf16[512,1024]{1,0:T(8,128)(2,1)S(1)} %get-tuple-element.42.first_queries.refs_0_, bf16[512,1024]{1,0:T(8,128)(2,1)S(1)} %get-tuple-element.55.refs_1_, f32[1024,512]{1,0:T(8,128)S(1)} %get-tuple-element.56.refs_2_, f32[512,128]{1,0:T(8,128)S(1)} %get-tuple-element.74.refs_3_), custom_call_target="tpu_custom_call" | custom-call | flops 134217728 | bytes 6291456 | tf_op jit(solution)/shard_map/mix/pallas_call | solution.py:316
  21.5 0.9 %collective-permute-done.3 = f32[512,128]{1,0:T(8,128)S(1)} collective-permute-done((f32[512,128]{1,0:T(8,128)S(1)}, f32[512,128]{1,0:T(8,128)S(1)}, u32[]{:S(2)}, u32[]{:S(2)}) %collective-permute-start.3) | collective-permute-done | bytes 262176 | tf_op jit(solution)/shard_map/ppermute | solution.py:441
  22.3 0.1 multiply_add_fusion.1
  22.4 0.1 collective-permute-start.5
  22.5 0.0 collective-permute-done.6.refs_2_
  22.5 0.5 %mix.5 = (f32[1024,512]{1,0:T(8,128)S(1)}, f32[1024,128]{1,0:T(8,128)S(1)}) custom-call(bf16[1024,1024]{1,0:T(8,128)(2,1)S(1)} %get-tuple-element.46.query_ref.refs_0_, f32[1024,512]{1,0:T(8,128)S(1)} %get-tuple-element.59.refs_1_, f32[512,128]{1,0:T(8,128)S(1)} %collective-permute-done.6.refs_2_, f32[1024,128]{1,0:T(8,128)S(1)} %get-tuple-element.57.after_ref.refs_3_), custom_call_target="tpu_custom_call" | custom-call | flops 134217728 | bytes 6291456 | tf_op jit(solution)/shard_map/mix/pallas_call | solution.py:316
  23.0 0.5 %mix.6 = (f32[1024,512]{1,0:T(8,128)S(1)}, f32[1024,128]{1,0:T(8,128)S(1)}) custom-call(bf16[512,1024]{1,0:T(8,128)(2,1)S(1)} %get-tuple-element.42.first_queries.refs_0_, bf16[512,1024]{1,0:T(8,128)(2,1)S(1)} %get-tuple-element.55.refs_1_, f32[1024,512]{1,0:T(8,128)S(1)} %get-tuple-element.58.refs_2_, f32[512,128]{1,0:T(8,128)S(1)} %get-tuple-element.71.refs_3_, ...), custom_call_target="tpu_custom_call" | custom-call | flops 134217728 | bytes 6291456 | tf_op jit(solution)/shard_map/mix/pallas_call | solution.py:316
  23.4 0.6 %collective-permute-done.5.refs_2_ = f32[512,128]{1,0:T(8,128)S(1)} collective-permute-done((f32[512,128]{1,0:T(8,128)S(1)}, f32[512,128]{1,0:T(8,128)S(1)}, u32[]{:S(2)}, u32[]{:S(2)}) %collective-permute-start.5) | collective-permute-done | bytes 262176 | tf_op jit(solution)/shard_map/ppermute | solution.py:488
  24.0 0.6 %mix.7 = (f32[1024,512]{1,0:T(8,128)S(1)}, f32[1,1024]{1,0:T(1,128)S(1)}) custom-call(bf16[1024,1024]{1,0:T(8,128)(2,1)S(1)} %get-tuple-element.46.query_ref.refs_0_, f32[1024,512]{1,0:T(8,128)S(1)} %get-tuple-element.53.refs_1_, f32[512,128]{1,0:T(8,128)S(1)} %collective-permute-done.5.refs_2_, f32[1024,128]{1,0:T(8,128)S(1)} %get-tuple-element.61.refs_3_), custom_call_target="tpu_custom_call" | custom-call | flops 134217728 | bytes 6291456 | tf_op jit(solution)/shard_map/mix/pallas_call | solution.py:316
  24.6 2.1 %collective-permute-start.7 = (f32[1,1024]{1,0:T(1,128)S(1)}, f32[1,1024]{1,0:T(1,128)S(1)}, u32[]{:S(2)}, u32[]{:S(2)}) collective-permute-start(f32[1,1024]{1,0:T(1,128)S(1)} %get-tuple-element.62.refs_3_), channel_id=1, source_target_pairs={{0,1},{1,0},{2,3},{3,2},{4,5},{5,4},{6,7},{7,6},{8,9},{9,8},{10,11... | collective-permute-start | bytes 12296 | tf_op jit(solution)/shard_map/ppermute | solution.py:497
  26.7 1.0 %gate.2 = (f32[1024,1024]{1,0:T(8,128)S(1)}, f32[1,1024]{1,0:T(1,128)S(1)}) custom-call(s32[1]{0:T(128)} %bitcast.place_ref.refs_0_, bf16[1024,2048]{1,0:T(8,128)(2,1)S(1)} %copy-done, f32[1,2048]{1,0:T(1,128)S(1)} %bitcast.16, f32[1,1024]{1,0:T(1,128)S(1)} %get-tuple-element.62.refs_3_, f32[1024,512]{1,0:T(8,128)S(1)} %get-tuple-element.63.refs_4_, ...), custom_call_target="tpu_custom_call" | custom-call | flops 16777216 | bytes 4194304 | tf_op jit(solution)/shard_map/gate/pallas_call | solution.py:351
  27.7 0.6 %collective-permute-done.7 = f32[1,1024]{1,0:T(1,128)S(1)} collective-permute-done((f32[1,1024]{1,0:T(1,128)S(1)}, f32[1,1024]{1,0:T(1,128)S(1)}, u32[]{:S(2)}, u32[]{:S(2)}) %collective-permute-start.7) | collective-permute-done | bytes 4128 | tf_op jit(solution)/shard_map/ppermute | solution.py:497
  28.3 3.1 %collective-permute-start.8 = (f32[1,1024]{1,0:T(1,128)S(1)}, f32[1,1024]{1,0:T(1,128)S(1)}, u32[]{:S(2)}, u32[]{:S(2)}) collective-permute-start(f32[1,1024]{1,0:T(1,128)S(1)} %add_add_fusion.5.refs_3_), channel_id=1, source_target_pairs={{0,2},{1,3},{2,0},{3,1},{4,6},{5,7},{6,4},{7,5},{8,10},{9,11},{10,... | collective-permute-start | bytes 12296 | tf_op jit(solution)/shard_map/ppermute | solution.py:501
  31.4 1.0 %gate.3 = (f32[1024,1024]{1,0:T(8,128)S(1)}, f32[1,1024]{1,0:T(1,128)S(1)}) custom-call(s32[1]{0:T(128)} %bitcast.place_ref.refs_0_, bf16[1024,2048]{1,0:T(8,128)(2,1)S(1)} %copy-done, f32[1,2048]{1,0:T(1,128)S(1)} %bitcast.17, f32[1,1024]{1,0:T(1,128)S(1)} %add_add_fusion.5.refs_3_, f32[1024,512]{1,0:T(8,128)S(1)} %get-tuple-element.66.refs_4_, ...), custom_call_target="tpu_custom_call" | custom-call | flops 16777216 | bytes 4194304 | tf_op jit(solution)/shard_map/gate/pallas_call | solution.py:351
  32.4 0.6 %collective-permute-done.8 = f32[1,1024]{1,0:T(1,128)S(1)} collective-permute-done((f32[1,1024]{1,0:T(1,128)S(1)}, f32[1,1024]{1,0:T(1,128)S(1)}, u32[]{:S(2)}, u32[]{:S(2)}) %collective-permute-start.8) | collective-permute-done | bytes 4128 | tf_op jit(solution)/shard_map/ppermute | solution.py:501
  33.0 2.4 %scale.1 = bf16[1024,2048]{1,0:T(8,128)(2,1)} custom-call(s32[1]{0:T(128)} %bitcast.place_ref.refs_0_, f32[1024,1024]{1,0:T(8,128)S(1)} %get-tuple-element.68.refs_1_, f32[1024,1024]{1,0:T(8,128)S(1)} %get-tuple-element.69.refs_2_, f32[1,1024]{1,0:T(1,128)S(1)} %add_add_fusion.4.refs_3_), custom_call_target="tpu_custom_call" | custom-call | flops 4194304 | bytes 4194304 | tf_op jit(solution)/shard_map/scale/pallas_call | solution.py:382
  (11 shorter events, 0.1 us)
Async XLA Ops:
  2.9 2.9 %collective-permute-start = (f32[1024,128]{1,0:T(8,128)S(1)}, f32[1024,128]{1,0:T(8,128)S(1)}, u32[]{:S(2)}, u32[]{:S(2)}) collective-permute-start(f32[1024,128]{1,0:T(8,128)S(1)} %get-tuple-element.41), channel_id=1, source_target_pairs={{0,4},{4,0},{8,12},{12,8},{16,20},{20,16},{24,28},{28,24},{1,5},{5... | collective-permute-start | bytes 1572872 | tf_op jit(solution)/shard_map/ppermute | solution.py:456
  5.8 6.9 %collective-permute-start.2 = (f32[512,128]{1,0:T(8,128)S(1)}, f32[512,128]{1,0:T(8,128)S(1)}, u32[]{:S(2)}, u32[]{:S(2)}) collective-permute-start(f32[512,128]{1,0:T(8,128)S(1)} %get-tuple-element.76.after_ref), channel_id=1, source_target_pairs={{0,8},{4,20},{8,0},{12,28},{16,24},{20,4},{24,16},{28,12},{1,9},{5... | collective-permute-start | bytes 786440 | tf_op jit(solution)/shard_map/ppermute | solution.py:435
  8.4 7.2 %collective-permute-start.1 = (f32[512,128]{1,0:T(8,128)S(1)}, f32[512,128]{1,0:T(8,128)S(1)}, u32[]{:S(2)}, u32[]{:S(2)}) collective-permute-start(f32[512,128]{1,0:T(8,128)S(1)} %get-tuple-element.75), channel_id=1, source_target_pairs={{0,8},{4,20},{8,0},{12,28},{16,24},{20,4},{24,16},{28,12},{1,9},{5... | collective-permute-start | bytes 786440 | tf_op jit(solution)/shard_map/ppermute | solution.py:435
  12.8 8.0 %collective-permute-start.4 = (f32[512,128]{1,0:T(8,128)S(1)}, f32[512,128]{1,0:T(8,128)S(1)}, u32[]{:S(2)}, u32[]{:S(2)}) collective-permute-start(f32[512,128]{1,0:T(8,128)S(1)} %add_add_fusion.2.after_ref), channel_id=1, source_target_pairs={{0,16},{4,12},{8,24},{12,4},{16,0},{20,28},{24,8},{28,20},{1,17},{... | collective-permute-start | bytes 786440 | tf_op jit(solution)/shard_map/ppermute | solution.py:441
  15.6 6.7 %collective-permute-start.3 = (f32[512,128]{1,0:T(8,128)S(1)}, f32[512,128]{1,0:T(8,128)S(1)}, u32[]{:S(2)}, u32[]{:S(2)}) collective-permute-start(f32[512,128]{1,0:T(8,128)S(1)} %add_add_fusion.3.after_ref), channel_id=1, source_target_pairs={{0,16},{4,12},{8,24},{12,4},{16,0},{20,28},{24,8},{28,20},{1,17},{... | collective-permute-start | bytes 786440 | tf_op jit(solution)/shard_map/ppermute | solution.py:441
  20.9 1.6 %collective-permute-start.6 = (f32[512,128]{1,0:T(8,128)S(1)}, f32[512,128]{1,0:T(8,128)S(1)}, u32[]{:S(2)}, u32[]{:S(2)}) collective-permute-start(f32[512,128]{1,0:T(8,128)S(1)} %get-tuple-element.73), channel_id=1, source_target_pairs={{0,4},{4,0},{8,12},{12,8},{16,20},{20,16},{24,28},{28,24},{1,5},{5... | collective-permute-start | bytes 786440 | tf_op jit(solution)/shard_map/ppermute | solution.py:488
  22.4 1.6 %collective-permute-start.5 = (f32[512,128]{1,0:T(8,128)S(1)}, f32[512,128]{1,0:T(8,128)S(1)}, u32[]{:S(2)}, u32[]{:S(2)}) collective-permute-start(f32[512,128]{1,0:T(8,128)S(1)} %get-tuple-element.72), channel_id=1, source_target_pairs={{0,4},{4,0},{8,12},{12,8},{16,20},{20,16},{24,28},{28,24},{1,5},{5... | collective-permute-start | bytes 786440 | tf_op jit(solution)/shard_map/ppermute | solution.py:488
  24.0 2.7 %copy-start = (bf16[1024,2048]{1,0:T(8,128)(2,1)S(1)}, bf16[1024,2048]{1,0:T(8,128)(2,1)}, u32[]{:S(2)}) copy-start(bf16[1024,2048]{1,0:T(8,128)(2,1)} %refs_1_.3) | copy-start | bytes 12582916
  24.0 2.7 %copy-start.1 = (f32[2048]{0:T(1024)S(1)}, f32[2048]{0:T(1024)}, u32[]{:S(2)}) copy-start(f32[2048]{0:T(1024)} %param.10) | copy-start | bytes 24580
  24.6 3.7 %collective-permute-start.7 = (f32[1,1024]{1,0:T(1,128)S(1)}, f32[1,1024]{1,0:T(1,128)S(1)}, u32[]{:S(2)}, u32[]{:S(2)}) collective-permute-start(f32[1,1024]{1,0:T(1,128)S(1)} %get-tuple-element.62.refs_3_), channel_id=1, source_target_pairs={{0,1},{1,0},{2,3},{3,2},{4,5},{5,4},{6,7},{7,6},{8,9},{9,8},{10,11... | collective-permute-start | bytes 12296 | tf_op jit(solution)/shard_map/ppermute | solution.py:497
  28.3 4.7 %collective-permute-start.8 = (f32[1,1024]{1,0:T(1,128)S(1)}, f32[1,1024]{1,0:T(1,128)S(1)}, u32[]{:S(2)}, u32[]{:S(2)}) collective-permute-start(f32[1,1024]{1,0:T(1,128)S(1)} %add_add_fusion.5.refs_3_), channel_id=1, source_target_pairs={{0,2},{1,3},{2,0},{3,1},{4,6},{5,7},{6,4},{7,5},{8,10},{9,11},{10,... | collective-permute-start | bytes 12296 | tf_op jit(solution)/shard_map/ppermute | solution.py:501

commit v6 on v5

--- a/solution.py
+++ b/solution.py
@@ -493,14 +493,23 @@
         part, squares = mix(held[False], inside[False][g], other, squares, starts[g], g == GROUPS - 1)
         mixed[False].append(part)
     power = squares
+    count = features // width
+
+    def crossed(bit):
+        pairs = [(c * count + z, (c ^ 1) * count + (z ^ bit)) for c in range(blocks) for z in range(count)]
+        return lax.ppermute(power, ("ctx", "head"), pairs) + lax.ppermute(power, "ctx", swap(blocks, 1))
+
     gated_other, zero = gated(place, mixed[False], gate_input, norm_gain, power, False)
-    power = power + lax.ppermute(power, "head", swap(features // width, 1)) + zero
+    power = crossed(1) + zero
     gated_mine, zero = gated(place, mixed[True], gate_input, norm_gain, power, True)
-    bit = 2
-    while bit < features // width:
-        power = power + lax.ppermute(power, "head", swap(features // width, bit))
-        bit *= 2
-    return scale(place, gated_mine, gated_other, power + zero, features)
+    power = crossed(2) + zero
+    bit, swapped = 4, False
+    while bit < count:
+        power = crossed(bit)
+        bit, swapped = 2 * bit, not swapped
+    if swapped:
+        power = lax.ppermute(power, "ctx", swap(blocks, 1))
+    return scale(place, gated_mine, gated_other, power, features)
 
 
 def solution(mesh):

time: 35.5 us -> 34.8 us (0.980)
  waiting for transfers between devices: 3.38 us -> 2.5 us
    ppermute x2 -> x4, waiting for transfers between devices: 1.23 us -> 0.36 us  [the longest x2 0.36 us: crossed(): lax.ppermute(power, ('ctx', 'head'), pairs)]
    ppermute x2 -> x4, starting transfers between devices: 5.24 us -> 5.37 us  [the longest x2 4.64 us: crossed(): lax.ppermute(power, ('ctx', 'head'), pairs)]
  transfers between devices with their start and end apart: 9 -> 11, of which waited for: 6 -> 5; matrix products, arithmetic and copies ran while one was open for 1% -> 1% of each run, Pallas kernels for 36% -> 37%
where the time goes in v6:
time: 34.8 us; the launch traced here: 34.6 us
  Pallas kernels  18.4 us (53%)
  starting transfers between devices  13.1 us (38%)
  waiting for transfers between devices  2.5 us (7%)
  other arithmetic  0.38 us (1%)
    ppermute x2, starting transfers between devices, crossed(): lax.ppermute(power, ('ctx', 'head'), pairs)  4.64 us
    ppermute x2, starting transfers between devices, two_steps(): lax.ppermute(x, 'ctx', [(i, i ^ (4 if i % 2 == 0 else 2)) for i in range(...  4.45 us
    pallas_call x1, Pallas kernels, mine_inner(): pl.pallas_call(mine_kernel, in_specs=[SCALARS, ANYWHERE, ANYWHERE] + [WHO...  4.17 us
    pallas_call x1, Pallas kernels, sent_states(): pl.pallas_call(sent_kernel, in_specs=[SCALARS] + [ANYWHERE] * 3, out_spec...  2.88 us
    pallas_call x1, Pallas kernels, other_inner(): pl.pallas_call(other_kernel, in_specs=[ANYWHERE] + [WHOLE] * 4, out_specs...  2.84 us
    ppermute x2, starting transfers between devices, two_steps(): lax.ppermute(x, 'ctx', [(i, i ^ (2 if i % 2 == 0 else 4)) for i in range(...  2.66 us
    pallas_call x1, Pallas kernels, scale(): pl.pallas_call(lambda *refs: scale_kernel(features, *refs), in_specs=[SCA...  2.35 us
    pallas_call x1, Pallas kernels, kept_states(): pl.pallas_call(kept_kernel, in_specs=[SCALARS] + [ANYWHERE] * 3 + [WHOLE]...  2.33 us
  transfers between devices with their start and end apart: 11, of which 5 were waited for; matrix products, arithmetic and copies ran while one was open for 1% of the time, Pallas kernels for 37%

profile of v6, /device:TPU:0, one launch (start us, length us, event | category | flops | bytes accessed | tf_op | source)
XLA Modules:
  0.0 34.6 jit_solution(98474838723680103)
XLA Ops:
  0.0 2.9 %states.2 = (f32[1024,128]{1,0:T(8,128)S(1)}, bf16[3072,128]{1,0:T(8,128)(2,1)S(1)}, bf16[1024,1024]{1,0:T(8,128)(2,1)S(1)}, bf16[1024,1024]{1,0:T(8,128)(2,1)S(...) custom-call(s32[1]{0:T(128)} %bitcast.place_ref.refs_0_, s32[8]{0:T(128)} %session_ref.1, ...), custom_call_target="tpu_custom_call" | custom-call | flops 268435456 | bytes 6291456 | tf_op jit(solution)/shard_map/states/pallas_call | solution.py:113
  2.9 0.5 %collective-permute-start = (f32[1024,128]{1,0:T(8,128)S(1)}, f32[1024,128]{1,0:T(8,128)S(1)}, u32[]{:S(2)}, u32[]{:S(2)}) collective-permute-start(f32[1024,128]{1,0:T(8,128)S(1)} %get-tuple-element.41), channel_id=1, source_target_pairs={{0,4},{4,0},{8,12},{12,8},{16,20},{20,16},{24,28},{28,24},{1,5},{5... | collective-permute-start | bytes 1572872 | tf_op jit(solution)/shard_map/ppermute | solution.py:456
  3.4 2.3 %states.3 = (f32[512,128]{1,0:T(8,128)S(1)}, f32[512,128]{1,0:T(8,128)S(1)}, bf16[3072,128]{1,0:T(8,128)(2,1)S(1)}, bf16[512,1024]{1,0:T(8,128)(2,1)S(1)}, bf16[...) custom-call(s32[1]{0:T(128)} %bitcast.place_ref.refs_0_, bf16[1024,2048]{1,0:T(8,128)(2,1)} %key_ref.3, ...), custom_call_target="tpu_custom_call" | custom-call | flops 268435456 | bytes 2097152 | tf_op jit(solution)/shard_map/states/pallas_call | solution.py:166
  5.8 0.1 slice_add_fusion
  5.8 2.6 %collective-permute-start.2 = (f32[512,128]{1,0:T(8,128)S(1)}, f32[512,128]{1,0:T(8,128)S(1)}, u32[]{:S(2)}, u32[]{:S(2)}) collective-permute-start(f32[512,128]{1,0:T(8,128)S(1)} %get-tuple-element.76.after_ref), channel_id=1, source_target_pairs={{0,8},{4,20},{8,0},{12,28},{16,24},{20,4},{24,16},{28,12},{1,9},{5... | collective-permute-start | bytes 786440 | tf_op jit(solution)/shard_map/ppermute | solution.py:435
  8.4 0.1 collective-permute-start.1
  8.5 4.2 %inner.2 = (bf16[512,1024]{1,0:T(8,128)(2,1)S(1)}, bf16[1024,1024]{1,0:T(8,128)(2,1)S(1)}, f32[1024,512]{1,0:T(8,128)S(1)}, f32[1024,512]{1,0:T(8,128)S(1)}, f32[1,128]{1,0:T(1,128)S(1)}) custom-call(s32[1]{0:T(128)} %bitcast.place_ref.refs_0_, bf16[1024,2048]{1,0:T(8,128)(2,1)} %query_ref.3, f32[512,128]{1,0:T(8,128)S(1)} %get-tuple-element.76.after_ref, ...), custom_call_target="tpu_custom_call" | custom-call | flops 1610612736 | bytes 12582912 | tf_op jit(solution)/shard_map/inner/pallas_call | solution.py:261
  12.7 0.1 collective-permute-done.2
  12.8 0.1 add_add_fusion.2.after_ref
  12.8 2.1 %collective-permute-start.4 = (f32[512,128]{1,0:T(8,128)S(1)}, f32[512,128]{1,0:T(8,128)S(1)}, u32[]{:S(2)}, u32[]{:S(2)}) collective-permute-start(f32[512,128]{1,0:T(8,128)S(1)} %add_add_fusion.2.after_ref), channel_id=1, source_target_pairs={{0,16},{4,12},{8,24},{12,4},{16,0},{20,28},{24,8},{28,20},{1,17},{... | collective-permute-start | bytes 786440 | tf_op jit(solution)/shard_map/ppermute | solution.py:441
  14.9 0.6 %collective-permute-done.1 = f32[512,128]{1,0:T(8,128)S(1)} collective-permute-done((f32[512,128]{1,0:T(8,128)S(1)}, f32[512,128]{1,0:T(8,128)S(1)}, u32[]{:S(2)}, u32[]{:S(2)}) %collective-permute-start.1) | collective-permute-done | bytes 262176 | tf_op jit(solution)/shard_map/ppermute | solution.py:435
  15.6 2.3 %collective-permute-start.3 = (f32[512,128]{1,0:T(8,128)S(1)}, f32[512,128]{1,0:T(8,128)S(1)}, u32[]{:S(2)}, u32[]{:S(2)}) collective-permute-start(f32[512,128]{1,0:T(8,128)S(1)} %add_add_fusion.3.after_ref), channel_id=1, source_target_pairs={{0,16},{4,12},{8,24},{12,4},{16,0},{20,28},{24,8},{28,20},{1,17},{... | collective-permute-start | bytes 786440 | tf_op jit(solution)/shard_map/ppermute | solution.py:441
  18.0 2.8 %inner.3 = (f32[1024,512]{1,0:T(8,128)S(1)}, f32[1024,512]{1,0:T(8,128)S(1)}, f32[1,128]{1,0:T(1,128)S(1)}) custom-call(f32[512,128]{1,0:T(8,128)S(1)} %add_add_fusion.3.after_ref, bf16[1024,1024]{1,0:T(8,128)(2,1)S(1)} %get-tuple-element.46.query_ref.refs_0_, bf16[1024,1024]{1,0:T(8,128)(2,1)S(1)} %get-tuple-element.50.key_ref, ...), custom_call_target="tpu_custom_call" | custom-call | flops 1610612736 | bytes 12582912 | tf_op jit(solution)/shard_map/inner/pallas_call | solution.py:282
  20.8 0.1 multiply_add_fusion
  20.9 0.1 collective-permute-start.6
  21.0 0.5 %mix.4 = (f32[1024,512]{1,0:T(8,128)S(1)}, f32[1024,128]{1,0:T(8,128)S(1)}) custom-call(bf16[512,1024]{1,0:T(8,128)(2,1)S(1)} %get-tuple-element.42.first_queries.refs_0_, bf16[512,1024]{1,0:T(8,128)(2,1)S(1)} %get-tuple-element.55.refs_1_, f32[1024,512]{1,0:T(8,128)S(1)} %get-tuple-element.56.refs_2_, f32[512,128]{1,0:T(8,128)S(1)} %get-tuple-element.74.refs_3_), custom_call_target="tpu_custom_call" | custom-call | flops 134217728 | bytes 6291456 | tf_op jit(solution)/shard_map/mix/pallas_call | solution.py:316
  21.5 0.9 %collective-permute-done.3 = f32[512,128]{1,0:T(8,128)S(1)} collective-permute-done((f32[512,128]{1,0:T(8,128)S(1)}, f32[512,128]{1,0:T(8,128)S(1)}, u32[]{:S(2)}, u32[]{:S(2)}) %collective-permute-start.3) | collective-permute-done | bytes 262176 | tf_op jit(solution)/shard_map/ppermute | solution.py:441
  22.3 0.1 multiply_add_fusion.1
  22.4 0.1 collective-permute-start.5
  22.5 0.0 collective-permute-done.6.refs_2_
  22.5 0.5 %mix.5 = (f32[1024,512]{1,0:T(8,128)S(1)}, f32[1024,128]{1,0:T(8,128)S(1)}) custom-call(bf16[1024,1024]{1,0:T(8,128)(2,1)S(1)} %get-tuple-element.46.query_ref.refs_0_, f32[1024,512]{1,0:T(8,128)S(1)} %get-tuple-element.59.refs_1_, f32[512,128]{1,0:T(8,128)S(1)} %collective-permute-done.6.refs_2_, f32[1024,128]{1,0:T(8,128)S(1)} %get-tuple-element.57.after_ref.refs_3_), custom_call_target="tpu_custom_call" | custom-call | flops 134217728 | bytes 6291456 | tf_op jit(solution)/shard_map/mix/pallas_call | solution.py:316
  23.0 0.5 %mix.6 = (f32[1024,512]{1,0:T(8,128)S(1)}, f32[1024,128]{1,0:T(8,128)S(1)}) custom-call(bf16[512,1024]{1,0:T(8,128)(2,1)S(1)} %get-tuple-element.42.first_queries.refs_0_, bf16[512,1024]{1,0:T(8,128)(2,1)S(1)} %get-tuple-element.55.refs_1_, f32[1024,512]{1,0:T(8,128)S(1)} %get-tuple-element.58.refs_2_, f32[512,128]{1,0:T(8,128)S(1)} %get-tuple-element.71.refs_3_, ...), custom_call_target="tpu_custom_call" | custom-call | flops 134217728 | bytes 6291456 | tf_op jit(solution)/shard_map/mix/pallas_call | solution.py:316
  23.4 0.6 %collective-permute-done.5.refs_2_ = f32[512,128]{1,0:T(8,128)S(1)} collective-permute-done((f32[512,128]{1,0:T(8,128)S(1)}, f32[512,128]{1,0:T(8,128)S(1)}, u32[]{:S(2)}, u32[]{:S(2)}) %collective-permute-start.5) | collective-permute-done | bytes 262176 | tf_op jit(solution)/shard_map/ppermute | solution.py:488
  24.0 0.6 %mix.7 = (f32[1024,512]{1,0:T(8,128)S(1)}, f32[1,1024]{1,0:T(1,128)S(1)}) custom-call(bf16[1024,1024]{1,0:T(8,128)(2,1)S(1)} %get-tuple-element.46.query_ref.refs_0_, f32[1024,512]{1,0:T(8,128)S(1)} %get-tuple-element.53.refs_1_, f32[512,128]{1,0:T(8,128)S(1)} %collective-permute-done.5.refs_2_, f32[1024,128]{1,0:T(8,128)S(1)} %get-tuple-element.61.refs_3_), custom_call_target="tpu_custom_call" | custom-call | flops 134217728 | bytes 6291456 | tf_op jit(solution)/shard_map/mix/pallas_call | solution.py:316
  24.6 1.9 %collective-permute-start.7 = (f32[1,1024]{1,0:T(1,128)S(1)}, f32[1,1024]{1,0:T(1,128)S(1)}, u32[]{:S(2)}, u32[]{:S(2)}) collective-permute-start(f32[1,1024]{1,0:T(1,128)S(1)} %get-tuple-element.62.refs_3_), channel_id=1, source_target_pairs={{0,5},{1,4},{2,7},{3,6},{4,1},{5,0},{6,3},{7,2},{8,13},{9,12},{10,... | collective-permute-start | bytes 12296 | tf_op jit(solution)/shard_map/ppermute | solution.py:500
  26.5 0.4 %collective-permute-start.8 = (f32[1,1024]{1,0:T(1,128)S(1)}, f32[1,1024]{1,0:T(1,128)S(1)}, u32[]{:S(2)}, u32[]{:S(2)}) collective-permute-start(f32[1,1024]{1,0:T(1,128)S(1)} %get-tuple-element.62.refs_3_), channel_id=1, source_target_pairs={{0,4},{4,0},{8,12},{12,8},{16,20},{20,16},{24,28},{28,24},{1,5},{5... | collective-permute-start | bytes 12296 | tf_op jit(solution)/shard_map/ppermute | solution.py:500
  26.8 1.0 %gate.2 = (f32[1024,1024]{1,0:T(8,128)S(1)}, f32[1,1024]{1,0:T(1,128)S(1)}) custom-call(s32[1]{0:T(128)} %bitcast.place_ref.refs_0_, bf16[1024,2048]{1,0:T(8,128)(2,1)S(1)} %copy-done, f32[1,2048]{1,0:T(1,128)S(1)} %bitcast.16, f32[1,1024]{1,0:T(1,128)S(1)} %get-tuple-element.62.refs_3_, f32[1024,512]{1,0:T(8,128)S(1)} %get-tuple-element.63.refs_4_, ...), custom_call_target="tpu_custom_call" | custom-call | flops 16777216 | bytes 4194304 | tf_op jit(solution)/shard_map/gate/pallas_call | solution.py:351
  27.8 0.4 %collective-permute-start.10 = (f32[1,1024]{1,0:T(1,128)S(1)}, f32[1,1024]{1,0:T(1,128)S(1)}, u32[]{:S(2)}, u32[]{:S(2)}) collective-permute-start(f32[1,1024]{1,0:T(1,128)S(1)} %add_add_fusion.5.refs_3_), channel_id=1, source_target_pairs={{0,4},{4,0},{8,12},{12,8},{16,20},{20,16},{24,28},{28,24},{1,5},{5... | collective-permute-start | bytes 12296 | tf_op jit(solution)/shard_map/ppermute | solution.py:500
  28.2 2.8 %collective-permute-start.9 = (f32[1,1024]{1,0:T(1,128)S(1)}, f32[1,1024]{1,0:T(1,128)S(1)}, u32[]{:S(2)}, u32[]{:S(2)}) collective-permute-start(f32[1,1024]{1,0:T(1,128)S(1)} %add_add_fusion.5.refs_3_), channel_id=1, source_target_pairs={{0,6},{1,7},{2,4},{3,5},{4,2},{5,3},{6,0},{7,1},{8,14},{9,15},{10,... | collective-permute-start | bytes 12296 | tf_op jit(solution)/shard_map/ppermute | solution.py:500
  31.0 1.0 %gate.3 = (f32[1024,1024]{1,0:T(8,128)S(1)}, f32[1,1024]{1,0:T(1,128)S(1)}) custom-call(s32[1]{0:T(128)} %bitcast.place_ref.refs_0_, bf16[1024,2048]{1,0:T(8,128)(2,1)S(1)} %copy-done, f32[1,2048]{1,0:T(1,128)S(1)} %bitcast.17, f32[1,1024]{1,0:T(1,128)S(1)} %add_add_fusion.5.refs_3_, f32[1024,512]{1,0:T(8,128)S(1)} %get-tuple-element.66.refs_4_, ...), custom_call_target="tpu_custom_call" | custom-call | flops 16777216 | bytes 4194304 | tf_op jit(solution)/shard_map/gate/pallas_call | solution.py:351
  31.9 0.4 %collective-permute-done.9 = f32[1,1024]{1,0:T(1,128)S(1)} collective-permute-done((f32[1,1024]{1,0:T(1,128)S(1)}, f32[1,1024]{1,0:T(1,128)S(1)}, u32[]{:S(2)}, u32[]{:S(2)}) %collective-permute-start.9) | collective-permute-done | bytes 4128 | tf_op jit(solution)/shard_map/ppermute | solution.py:500
  32.3 2.4 %scale.1 = bf16[1024,2048]{1,0:T(8,128)(2,1)} custom-call(s32[1]{0:T(128)} %bitcast.place_ref.refs_0_, f32[1024,1024]{1,0:T(8,128)S(1)} %get-tuple-element.68.refs_1_, f32[1024,1024]{1,0:T(8,128)S(1)} %get-tuple-element.69.refs_2_, f32[1,1024]{1,0:T(1,128)S(1)} %add_add_fusion.4.refs_3_), custom_call_target="tpu_custom_call" | custom-call | flops 4194304 | bytes 4194304 | tf_op jit(solution)/shard_map/scale/pallas_call | solution.py:382
  (15 shorter events, 0.1 us)
Async XLA Ops:
  2.9 2.9 %collective-permute-start = (f32[1024,128]{1,0:T(8,128)S(1)}, f32[1024,128]{1,0:T(8,128)S(1)}, u32[]{:S(2)}, u32[]{:S(2)}) collective-permute-start(f32[1024,128]{1,0:T(8,128)S(1)} %get-tuple-element.41), channel_id=1, source_target_pairs={{0,4},{4,0},{8,12},{12,8},{16,20},{20,16},{24,28},{28,24},{1,5},{5... | collective-permute-start | bytes 1572872 | tf_op jit(solution)/shard_map/ppermute | solution.py:456
  5.8 6.9 %collective-permute-start.2 = (f32[512,128]{1,0:T(8,128)S(1)}, f32[512,128]{1,0:T(8,128)S(1)}, u32[]{:S(2)}, u32[]{:S(2)}) collective-permute-start(f32[512,128]{1,0:T(8,128)S(1)} %get-tuple-element.76.after_ref), channel_id=1, source_target_pairs={{0,8},{4,20},{8,0},{12,28},{16,24},{20,4},{24,16},{28,12},{1,9},{5... | collective-permute-start | bytes 786440 | tf_op jit(solution)/shard_map/ppermute | solution.py:435
  8.4 7.2 %collective-permute-start.1 = (f32[512,128]{1,0:T(8,128)S(1)}, f32[512,128]{1,0:T(8,128)S(1)}, u32[]{:S(2)}, u32[]{:S(2)}) collective-permute-start(f32[512,128]{1,0:T(8,128)S(1)} %get-tuple-element.75), channel_id=1, source_target_pairs={{0,8},{4,20},{8,0},{12,28},{16,24},{20,4},{24,16},{28,12},{1,9},{5... | collective-permute-start | bytes 786440 | tf_op jit(solution)/shard_map/ppermute | solution.py:435
  12.8 8.0 %collective-permute-start.4 = (f32[512,128]{1,0:T(8,128)S(1)}, f32[512,128]{1,0:T(8,128)S(1)}, u32[]{:S(2)}, u32[]{:S(2)}) collective-permute-start(f32[512,128]{1,0:T(8,128)S(1)} %add_add_fusion.2.after_ref), channel_id=1, source_target_pairs={{0,16},{4,12},{8,24},{12,4},{16,0},{20,28},{24,8},{28,20},{1,17},{... | collective-permute-start | bytes 786440 | tf_op jit(solution)/shard_map/ppermute | solution.py:441
  15.6 6.7 %collective-permute-start.3 = (f32[512,128]{1,0:T(8,128)S(1)}, f32[512,128]{1,0:T(8,128)S(1)}, u32[]{:S(2)}, u32[]{:S(2)}) collective-permute-start(f32[512,128]{1,0:T(8,128)S(1)} %add_add_fusion.3.after_ref), channel_id=1, source_target_pairs={{0,16},{4,12},{8,24},{12,4},{16,0},{20,28},{24,8},{28,20},{1,17},{... | collective-permute-start | bytes 786440 | tf_op jit(solution)/shard_map/ppermute | solution.py:441
  20.9 1.6 %collective-permute-start.6 = (f32[512,128]{1,0:T(8,128)S(1)}, f32[512,128]{1,0:T(8,128)S(1)}, u32[]{:S(2)}, u32[]{:S(2)}) collective-permute-start(f32[512,128]{1,0:T(8,128)S(1)} %get-tuple-element.73), channel_id=1, source_target_pairs={{0,4},{4,0},{8,12},{12,8},{16,20},{20,16},{24,28},{28,24},{1,5},{5... | collective-permute-start | bytes 786440 | tf_op jit(solution)/shard_map/ppermute | solution.py:488
  22.4 1.6 %collective-permute-start.5 = (f32[512,128]{1,0:T(8,128)S(1)}, f32[512,128]{1,0:T(8,128)S(1)}, u32[]{:S(2)}, u32[]{:S(2)}) collective-permute-start(f32[512,128]{1,0:T(8,128)S(1)} %get-tuple-element.72), channel_id=1, source_target_pairs={{0,4},{4,0},{8,12},{12,8},{16,20},{20,16},{24,28},{28,24},{1,5},{5... | collective-permute-start | bytes 786440 | tf_op jit(solution)/shard_map/ppermute | solution.py:488
  24.0 2.8 %copy-start = (bf16[1024,2048]{1,0:T(8,128)(2,1)S(1)}, bf16[1024,2048]{1,0:T(8,128)(2,1)}, u32[]{:S(2)}) copy-start(bf16[1024,2048]{1,0:T(8,128)(2,1)} %refs_1_.3) | copy-start | bytes 12582916
  24.0 2.8 %copy-start.1 = (f32[2048]{0:T(1024)S(1)}, f32[2048]{0:T(1024)}, u32[]{:S(2)}) copy-start(f32[2048]{0:T(1024)} %param.10) | copy-start | bytes 24580
  24.6 3.2 %collective-permute-start.7 = (f32[1,1024]{1,0:T(1,128)S(1)}, f32[1,1024]{1,0:T(1,128)S(1)}, u32[]{:S(2)}, u32[]{:S(2)}) collective-permute-start(f32[1,1024]{1,0:T(1,128)S(1)} %get-tuple-element.62.refs_3_), channel_id=1, source_target_pairs={{0,5},{1,4},{2,7},{3,6},{4,1},{5,0},{6,3},{7,2},{8,13},{9,12},{10,... | collective-permute-start | bytes 12296 | tf_op jit(solution)/shard_map/ppermute | solution.py:500
  26.5 1.4 %collective-permute-start.8 = (f32[1,1024]{1,0:T(1,128)S(1)}, f32[1,1024]{1,0:T(1,128)S(1)}, u32[]{:S(2)}, u32[]{:S(2)}) collective-permute-start(f32[1,1024]{1,0:T(1,128)S(1)} %get-tuple-element.62.refs_3_), channel_id=1, source_target_pairs={{0,4},{4,0},{8,12},{12,8},{16,20},{20,16},{24,28},{28,24},{1,5},{5... | collective-permute-start | bytes 12296 | tf_op jit(solution)/shard_map/ppermute | solution.py:500
  27.8 4.1 %collective-permute-start.10 = (f32[1,1024]{1,0:T(1,128)S(1)}, f32[1,1024]{1,0:T(1,128)S(1)}, u32[]{:S(2)}, u32[]{:S(2)}) collective-permute-start(f32[1,1024]{1,0:T(1,128)S(1)} %add_add_fusion.5.refs_3_), channel_id=1, source_target_pairs={{0,4},{4,0},{8,12},{12,8},{16,20},{20,16},{24,28},{28,24},{1,5},{5... | collective-permute-start | bytes 12296 | tf_op jit(solution)/shard_map/ppermute | solution.py:500
  28.2 4.1 %collective-permute-start.9 = (f32[1,1024]{1,0:T(1,128)S(1)}, f32[1,1024]{1,0:T(1,128)S(1)}, u32[]{:S(2)}, u32[]{:S(2)}) collective-permute-start(f32[1,1024]{1,0:T(1,128)S(1)} %add_add_fusion.5.refs_3_), channel_id=1, source_target_pairs={{0,6},{1,7},{2,4},{3,5},{4,2},{5,3},{6,0},{7,1},{8,14},{9,15},{10,... | collective-permute-start | bytes 12296 | tf_op jit(solution)/shard_map/ppermute | solution.py:500

commit v7 on v6

--- a/solution.py
+++ b/solution.py
@@ -438,9 +438,9 @@
     for x, y in zip(sums, there):
         onward.append(weight[2:3] * x + weight[3:4] * y + zero)
         zero = zero_after(onward[-1])
-    arrived = [lax.ppermute(x, "ctx", [(i, i ^ (4 if i % 2 == 0 else 2)) for i in range(8)]) for x in onward]
+    arrived = [lax.ppermute(x, "ctx", [(i, i ^ (5 if i % 2 == 0 else 3)) for i in range(8)]) for x in onward]
     zero = beside(onward[-1])
-    return [weight[4:5] * x + y + zero for x, y in zip(there, arrived)]
+    return [weight[4:5] * x for x in there], [x + zero for x in arrived]
 
 
 def on_device(blocks, features, queries, key_rows, values, gate_input, norm_gain, session_of):
@@ -474,24 +474,37 @@
         return zero
 
     if blocks == 8:
-        prefixes = two_steps(sums, weight, mine_inside, other_inside)
+        own, arrived = two_steps(sums, weight, mine_inside, other_inside)
     else:
-        zero = mine_inside(sums[0]) + other_inside(sums[0])
-        prefixes = [general_prefix(blocks, index >> 1, session_of, x) + zero for x in sums]
+        zero = other_inside(mine_inside(sums[0]))
+        own = [general_prefix(blocks, index >> 1, session_of, x) + zero for x in sums]
+        arrived = [jnp.zeros_like(x) for x in sums]
     even, odd = weight[0:1], weight[1:2]
+    others = [lax.ppermute(x + even * k, "ctx", swap(blocks, 1)) for x, k in zip(own, kept)]
 
     mixed = {True: [], False: []}
+    parts, backs = [], []
     squares = None
-    zero = jnp.zeros((1, HEAD_DIM), F32)
-    for g, prefix in enumerate(prefixes):
-        prefix = prefix + zero
-        other = lax.ppermute(prefix + even * kept[g], "ctx", swap(blocks, 1))
-        mine = prefix + odd * got[g]
-        part, squares = mix(held[True], inside[True][g], mine, squares, starts[g], False)
-        mixed[True].append(part)
-        zero = zero_after(squares)
-        part, squares = mix(held[False], inside[False][g], other, squares, starts[g], g == GROUPS - 1)
-        mixed[False].append(part)
+
+    def swap_part(g, zero):
+        parts.append(arrived[g] + zero)
+        backs.append(lax.ppermute(parts[g], "ctx", swap(blocks, 1)))
+        return zero_after(parts[g])
+
+    def mix_group(mine, zero, last=False):
+        nonlocal squares
+        g = len(mixed[mine])
+        prefix = own[g] + odd * got[g] + backs[g] if mine else others[g] + parts[g]
+        part, squares = mix(held[mine], inside[mine][g], prefix + zero, squares, starts[g], last)
+        mixed[mine].append(part)
+        return zero_after(squares)
+
+    zero = swap_part(0, jnp.zeros((1, HEAD_DIM), F32))
+    for g in range(GROUPS):
+        zero = mix_group(False, zero)
+        if g + 1 < GROUPS:
+            zero = swap_part(g + 1, zero)
+        zero = mix_group(True, zero, g == GROUPS - 1)
     power = squares
     count = features // width
 

time: 34.8 us -> 34.3 us (0.986)
  waiting for transfers between devices: 2.5 us -> 1.54 us
    ppermute x4 -> x6, waiting for transfers between devices: 1.44 us -> 0.47 us  [the longest x2 0.38 us: swap_part(): backs.append(lax.ppermute(parts[g], 'ctx', swap(blocks, 1)))]
    ppermute x4 -> x6, starting transfers between devices: 4.59 us -> 5.12 us  [the longest x2 2.99 us: two_steps(): lax.ppermute(x, 'ctx', [(i, i ^ (5 if i % 2 == 0 else 3)) for i in range(...]
    ppermute x2, starting transfers between devices: 0.73 us -> 0.37 us  [crossed(): lax.ppermute(power, 'ctx', swap(blocks, 1))]
  transfers between devices with their start and end apart: 11 -> 13, of which waited for: 5 -> 6; matrix products, arithmetic and copies ran while one was open for 1% -> 1% of each run, Pallas kernels for 37% -> 38%
where the time goes in v7:
time: 34.3 us; the launch traced here: 34.2 us
  Pallas kernels  18.7 us (55%)
  starting transfers between devices  13.1 us (38%)
  waiting for transfers between devices  1.54 us (4%)
  other arithmetic  0.45 us (1%)
  between operations  0.4 us (1%)
    ppermute x2, starting transfers between devices, crossed(): lax.ppermute(power, ('ctx', 'head'), pairs)  4.44 us
    pallas_call x1, Pallas kernels, mine_inner(): pl.pallas_call(mine_kernel, in_specs=[SCALARS, ANYWHERE, ANYWHERE] + [WHO...  4.16 us
    ppermute x2, starting transfers between devices, two_steps(): lax.ppermute(x, 'ctx', [(i, i ^ (5 if i % 2 == 0 else 3)) for i in range(...  2.99 us
    pallas_call x1, Pallas kernels, other_inner(): pl.pallas_call(other_kernel, in_specs=[ANYWHERE] + [WHOLE] * 4, out_specs...  2.91 us
    pallas_call x1, Pallas kernels, sent_states(): pl.pallas_call(sent_kernel, in_specs=[SCALARS] + [ANYWHERE] * 3, out_spec...  2.88 us
    ppermute x2, starting transfers between devices, two_steps(): lax.ppermute(x, 'ctx', [(i, i ^ (2 if i % 2 == 0 else 4)) for i in range(...  2.66 us
    pallas_call x1, Pallas kernels, scale(): pl.pallas_call(lambda *refs: scale_kernel(features, *refs), in_specs=[SCA...  2.35 us
    pallas_call x1, Pallas kernels, kept_states(): pl.pallas_call(kept_kernel, in_specs=[SCALARS] + [ANYWHERE] * 3 + [WHOLE]...  2.33 us
  transfers between devices with their start and end apart: 13, of which 6 were waited for; matrix products, arithmetic and copies ran while one was open for 1% of the time, Pallas kernels for 38%

profile of v7, /device:TPU:0, one launch (start us, length us, event | category | flops | bytes accessed | tf_op | source)
XLA Modules:
  0.0 34.2 jit_solution(7921864973628566065)
XLA Ops:
  0.0 2.9 %states.2 = (f32[1024,128]{1,0:T(8,128)S(1)}, bf16[3072,128]{1,0:T(8,128)(2,1)S(1)}, bf16[1024,1024]{1,0:T(8,128)(2,1)S(1)}, bf16[1024,1024]{1,0:T(8,128)(2,1)S(...) custom-call(s32[1]{0:T(128)} %bitcast.place_ref.refs_0_, s32[8]{0:T(128)} %session_ref.1, ...), custom_call_target="tpu_custom_call" | custom-call | flops 268435456 | bytes 6291456 | tf_op jit(solution)/shard_map/states/pallas_call | solution.py:113
  2.9 0.5 %collective-permute-start = (f32[1024,128]{1,0:T(8,128)S(1)}, f32[1024,128]{1,0:T(8,128)S(1)}, u32[]{:S(2)}, u32[]{:S(2)}) collective-permute-start(f32[1024,128]{1,0:T(8,128)S(1)} %get-tuple-element.42), channel_id=1, source_target_pairs={{0,4},{4,0},{8,12},{12,8},{16,20},{20,16},{24,28},{28,24},{1,5},{5... | collective-permute-start | bytes 1572872 | tf_op jit(solution)/shard_map/ppermute | solution.py:456
  3.4 2.3 %states.3 = (f32[512,128]{1,0:T(8,128)S(1)}, f32[512,128]{1,0:T(8,128)S(1)}, bf16[3072,128]{1,0:T(8,128)(2,1)S(1)}, bf16[512,1024]{1,0:T(8,128)(2,1)S(1)}, bf16[...) custom-call(s32[1]{0:T(128)} %bitcast.place_ref.refs_0_, bf16[1024,2048]{1,0:T(8,128)(2,1)} %key_ref.3, ...), custom_call_target="tpu_custom_call" | custom-call | flops 268435456 | bytes 2097152 | tf_op jit(solution)/shard_map/states/pallas_call | solution.py:166
  5.8 2.6 %collective-permute-start.2 = (f32[512,128]{1,0:T(8,128)S(1)}, f32[512,128]{1,0:T(8,128)S(1)}, u32[]{:S(2)}, u32[]{:S(2)}) collective-permute-start(f32[512,128]{1,0:T(8,128)S(1)} %get-tuple-element.72.after_ref), channel_id=1, source_target_pairs={{0,8},{4,20},{8,0},{12,28},{16,24},{20,4},{24,16},{28,12},{1,9},{5... | collective-permute-start | bytes 786440 | tf_op jit(solution)/shard_map/ppermute | solution.py:435
  8.4 0.1 collective-permute-start.1
  8.5 4.2 %inner.2 = (bf16[512,1024]{1,0:T(8,128)(2,1)S(1)}, bf16[1024,1024]{1,0:T(8,128)(2,1)S(1)}, f32[1024,512]{1,0:T(8,128)S(1)}, f32[1024,512]{1,0:T(8,128)S(1)}, f32[1,128]{1,0:T(1,128)S(1)}) custom-call(s32[1]{0:T(128)} %bitcast.place_ref.refs_0_, bf16[1024,2048]{1,0:T(8,128)(2,1)} %query_ref.3, f32[512,128]{1,0:T(8,128)S(1)} %get-tuple-element.72.after_ref, ...), custom_call_target="tpu_custom_call" | custom-call | flops 1610612736 | bytes 12582912 | tf_op jit(solution)/shard_map/inner/pallas_call | solution.py:261
  12.7 0.1 collective-permute-done.2
  12.7 0.1 multiply_add_fusion.1
  12.8 1.5 %collective-permute-start.5 = (f32[512,128]{1,0:T(8,128)S(1)}, f32[512,128]{1,0:T(8,128)S(1)}, u32[]{:S(2)}, u32[]{:S(2)}) collective-permute-start(f32[512,128]{1,0:T(8,128)S(1)} %get-tuple-element.76.after_ref), channel_id=1, source_target_pairs={{0,20},{4,8},{8,28},{12,0},{16,4},{20,24},{24,12},{28,16},{1,21},{... | collective-permute-start | bytes 786440 | tf_op jit(solution)/shard_map/ppermute | solution.py:441
  14.3 0.7 %collective-permute-start.4 = (f32[512,128]{1,0:T(8,128)S(1)}, f32[512,128]{1,0:T(8,128)S(1)}, u32[]{:S(2)}, u32[]{:S(2)}) collective-permute-start(f32[512,128]{1,0:T(8,128)S(1)} %get-tuple-element.75), channel_id=1, source_target_pairs={{0,4},{4,0},{8,12},{12,8},{16,20},{20,16},{24,28},{28,24},{1,5},{5... | collective-permute-start | bytes 786440 | tf_op jit(solution)/shard_map/ppermute | solution.py:483
  15.0 0.5 %collective-permute-done.1 = f32[512,128]{1,0:T(8,128)S(1)} collective-permute-done((f32[512,128]{1,0:T(8,128)S(1)}, f32[512,128]{1,0:T(8,128)S(1)}, u32[]{:S(2)}, u32[]{:S(2)}) %collective-permute-start.1) | collective-permute-done | bytes 262176 | tf_op jit(solution)/shard_map/ppermute | solution.py:435
  15.6 0.1 multiply_add_fusion
  15.6 1.5 %collective-permute-start.3 = (f32[512,128]{1,0:T(8,128)S(1)}, f32[512,128]{1,0:T(8,128)S(1)}, u32[]{:S(2)}, u32[]{:S(2)}) collective-permute-start(f32[512,128]{1,0:T(8,128)S(1)} %get-tuple-element.74.after_ref), channel_id=1, source_target_pairs={{0,20},{4,8},{8,28},{12,0},{16,4},{20,24},{24,12},{28,16},{1,21},{... | collective-permute-start | bytes 786440 | tf_op jit(solution)/shard_map/ppermute | solution.py:441
  17.1 0.8 %collective-permute-start.7 = (f32[512,128]{1,0:T(8,128)S(1)}, f32[512,128]{1,0:T(8,128)S(1)}, u32[]{:S(2)}, u32[]{:S(2)}) collective-permute-start(f32[512,128]{1,0:T(8,128)S(1)} %get-tuple-element.73), channel_id=1, source_target_pairs={{0,4},{4,0},{8,12},{12,8},{16,20},{20,16},{24,28},{28,24},{1,5},{5... | collective-permute-start | bytes 786440 | tf_op jit(solution)/shard_map/ppermute | solution.py:483
  18.0 2.9 %inner.3 = (f32[1024,512]{1,0:T(8,128)S(1)}, f32[1024,512]{1,0:T(8,128)S(1)}, f32[1,128]{1,0:T(1,128)S(1)}) custom-call(f32[512,128]{1,0:T(8,128)S(1)} %get-tuple-element.74.after_ref, bf16[1024,1024]{1,0:T(8,128)(2,1)S(1)} %get-tuple-element.51.query_ref.refs_0_, bf16[1024,1024]{1,0:T(8,128)(2,1)S(1)} %get-tuple-element.52.key_ref, ...), custom_call_target="tpu_custom_call" | custom-call | flops 1610612736 | bytes 12582912 | tf_op jit(solution)/shard_map/inner/pallas_call | solution.py:282
  21.0 0.1 collective-permute-start.8
  21.1 0.5 %mix.4 = (f32[1024,512]{1,0:T(8,128)S(1)}, f32[1024,128]{1,0:T(8,128)S(1)}) custom-call(bf16[1024,1024]{1,0:T(8,128)(2,1)S(1)} %get-tuple-element.51.query_ref.refs_0_, f32[1024,512]{1,0:T(8,128)S(1)} %get-tuple-element.56.refs_1_, f32[512,128]{1,0:T(8,128)S(1)} %add_add_fusion.3.refs_2_), custom_call_target="tpu_custom_call" | custom-call | flops 134217728 | bytes 6291456 | tf_op jit(solution)/shard_map/mix/pallas_call | solution.py:316
  21.6 0.1 collective-permute-done.3
  21.7 0.5 %collective-permute-start.6 = (f32[512,128]{1,0:T(8,128)S(1)}, f32[512,128]{1,0:T(8,128)S(1)}, u32[]{:S(2)}, u32[]{:S(2)}) collective-permute-start(f32[512,128]{1,0:T(8,128)S(1)} %add_add_fusion.4.after_ref), channel_id=1, source_target_pairs={{0,4},{4,0},{8,12},{12,8},{16,20},{20,16},{24,28},{28,24},{1,5},{5... | collective-permute-start | bytes 786440 | tf_op jit(solution)/shard_map/ppermute | solution.py:491
  22.2 0.4 %collective-permute-done.8 = f32[512,128]{1,0:T(8,128)S(1)} collective-permute-done((f32[512,128]{1,0:T(8,128)S(1)}, f32[512,128]{1,0:T(8,128)S(1)}, u32[]{:S(2)}, u32[]{:S(2)}) %collective-permute-start.8) | collective-permute-done | bytes 262176 | tf_op jit(solution)/shard_map/ppermute | solution.py:491
  22.6 0.5 %mix.5 = (f32[1024,512]{1,0:T(8,128)S(1)}, f32[1024,128]{1,0:T(8,128)S(1)}) custom-call(bf16[512,1024]{1,0:T(8,128)(2,1)S(1)} %get-tuple-element.40.first_queries.refs_0_, bf16[512,1024]{1,0:T(8,128)(2,1)S(1)} %get-tuple-element.46.refs_1_, f32[1024,512]{1,0:T(8,128)S(1)} %get-tuple-element.59.refs_2_, f32[512,128]{1,0:T(8,128)S(1)} %add_add_fusion.refs_3_, ...), custom_call_target="tpu_custom_call" | custom-call | flops 134217728 | bytes 6291456 | tf_op jit(solution)/shard_map/mix/pallas_call | solution.py:316
  23.2 0.5 %mix.6 = (f32[1024,512]{1,0:T(8,128)S(1)}, f32[1024,128]{1,0:T(8,128)S(1)}) custom-call(bf16[1024,1024]{1,0:T(8,128)(2,1)S(1)} %get-tuple-element.51.query_ref.refs_0_, f32[1024,512]{1,0:T(8,128)S(1)} %get-tuple-element.58.refs_1_, f32[512,128]{1,0:T(8,128)S(1)} %add_add_fusion.1.refs_2_, f32[1024,128]{1,0:T(8,128)S(1)} %get-tuple-element.60.after_ref.refs_3_), custom_call_target="tpu_custom_call" | custom-call | flops 134217728 | bytes 6291456 | tf_op jit(solution)/shard_map/mix/pallas_call | solution.py:316
  23.8 0.5 %mix.7 = (f32[1024,512]{1,0:T(8,128)S(1)}, f32[1,1024]{1,0:T(1,128)S(1)}) custom-call(bf16[512,1024]{1,0:T(8,128)(2,1)S(1)} %get-tuple-element.40.first_queries.refs_0_, bf16[512,1024]{1,0:T(8,128)(2,1)S(1)} %get-tuple-element.46.refs_1_, f32[1024,512]{1,0:T(8,128)S(1)} %get-tuple-element.47.refs_2_, f32[512,128]{1,0:T(8,128)S(1)} %add_add_fusion.2.refs_3_, ...), custom_call_target="tpu_custom_call" | custom-call | flops 134217728 | bytes 6291456 | tf_op jit(solution)/shard_map/mix/pallas_call | solution.py:316
  24.3 0.2 collective-permute-start.10
  24.5 1.7 %collective-permute-start.9 = (f32[1,1024]{1,0:T(1,128)S(1)}, f32[1,1024]{1,0:T(1,128)S(1)}, u32[]{:S(2)}, u32[]{:S(2)}) collective-permute-start(f32[1,1024]{1,0:T(1,128)S(1)} %get-tuple-element.62.refs_3_), channel_id=1, source_target_pairs={{0,5},{1,4},{2,7},{3,6},{4,1},{5,0},{6,3},{7,2},{8,13},{9,12},{10,... | collective-permute-start | bytes 12296 | tf_op jit(solution)/shard_map/ppermute | solution.py:513
  26.2 1.0 %gate.2 = (f32[1024,1024]{1,0:T(8,128)S(1)}, f32[1,1024]{1,0:T(1,128)S(1)}) custom-call(s32[1]{0:T(128)} %bitcast.place_ref.refs_0_, bf16[1024,2048]{1,0:T(8,128)(2,1)S(1)} %copy-done, f32[1,2048]{1,0:T(1,128)S(1)} %bitcast.20, f32[1,1024]{1,0:T(1,128)S(1)} %get-tuple-element.62.refs_3_, f32[1024,512]{1,0:T(8,128)S(1)} %get-tuple-element.63.refs_4_, ...), custom_call_target="tpu_custom_call" | custom-call | flops 16777216 | bytes 4194304 | tf_op jit(solution)/shard_map/gate/pallas_call | solution.py:351
  27.3 0.3 collective-permute-done.9
  27.6 2.8 %collective-permute-start.11 = (f32[1,1024]{1,0:T(1,128)S(1)}, f32[1,1024]{1,0:T(1,128)S(1)}, u32[]{:S(2)}, u32[]{:S(2)}) collective-permute-start(f32[1,1024]{1,0:T(1,128)S(1)} %add_add_fusion.8.refs_3_), channel_id=1, source_target_pairs={{0,6},{1,7},{2,4},{3,5},{4,2},{5,3},{6,0},{7,1},{8,14},{9,15},{10,... | collective-permute-start | bytes 12296 | tf_op jit(solution)/shard_map/ppermute | solution.py:513
  30.3 0.2 collective-permute-start.12
  30.5 1.0 %gate.3 = (f32[1024,1024]{1,0:T(8,128)S(1)}, f32[1,1024]{1,0:T(1,128)S(1)}) custom-call(s32[1]{0:T(128)} %bitcast.place_ref.refs_0_, bf16[1024,2048]{1,0:T(8,128)(2,1)S(1)} %copy-done, f32[1,2048]{1,0:T(1,128)S(1)} %bitcast.21, f32[1,1024]{1,0:T(1,128)S(1)} %add_add_fusion.8.refs_3_, f32[1024,512]{1,0:T(8,128)S(1)} %get-tuple-element.66.refs_4_, ...), custom_call_target="tpu_custom_call" | custom-call | flops 16777216 | bytes 4194304 | tf_op jit(solution)/shard_map/gate/pallas_call | solution.py:351
  31.5 0.1 collective-permute-done.11
  31.7 2.3 %scale.1 = bf16[1024,2048]{1,0:T(8,128)(2,1)} custom-call(s32[1]{0:T(128)} %bitcast.place_ref.refs_0_, f32[1024,1024]{1,0:T(8,128)S(1)} %get-tuple-element.68.refs_1_, f32[1024,1024]{1,0:T(8,128)S(1)} %get-tuple-element.69.refs_2_, f32[1,1024]{1,0:T(1,128)S(1)} %add_add_fusion.7.refs_3_), custom_call_target="tpu_custom_call" | custom-call | flops 4194304 | bytes 4194304 | tf_op jit(solution)/shard_map/scale/pallas_call | solution.py:382
  (27 shorter events, 0.4 us)
Async XLA Ops:
  2.9 2.9 %collective-permute-start = (f32[1024,128]{1,0:T(8,128)S(1)}, f32[1024,128]{1,0:T(8,128)S(1)}, u32[]{:S(2)}, u32[]{:S(2)}) collective-permute-start(f32[1024,128]{1,0:T(8,128)S(1)} %get-tuple-element.42), channel_id=1, source_target_pairs={{0,4},{4,0},{8,12},{12,8},{16,20},{20,16},{24,28},{28,24},{1,5},{5... | collective-permute-start | bytes 1572872 | tf_op jit(solution)/shard_map/ppermute | solution.py:456
  5.8 6.9 %collective-permute-start.2 = (f32[512,128]{1,0:T(8,128)S(1)}, f32[512,128]{1,0:T(8,128)S(1)}, u32[]{:S(2)}, u32[]{:S(2)}) collective-permute-start(f32[512,128]{1,0:T(8,128)S(1)} %get-tuple-element.72.after_ref), channel_id=1, source_target_pairs={{0,8},{4,20},{8,0},{12,28},{16,24},{20,4},{24,16},{28,12},{1,9},{5... | collective-permute-start | bytes 786440 | tf_op jit(solution)/shard_map/ppermute | solution.py:435
  8.4 7.2 %collective-permute-start.1 = (f32[512,128]{1,0:T(8,128)S(1)}, f32[512,128]{1,0:T(8,128)S(1)}, u32[]{:S(2)}, u32[]{:S(2)}) collective-permute-start(f32[512,128]{1,0:T(8,128)S(1)} %get-tuple-element.71), channel_id=1, source_target_pairs={{0,8},{4,20},{8,0},{12,28},{16,24},{20,4},{24,16},{28,12},{1,9},{5... | collective-permute-start | bytes 786440 | tf_op jit(solution)/shard_map/ppermute | solution.py:435
  12.8 8.1 %collective-permute-start.5 = (f32[512,128]{1,0:T(8,128)S(1)}, f32[512,128]{1,0:T(8,128)S(1)}, u32[]{:S(2)}, u32[]{:S(2)}) collective-permute-start(f32[512,128]{1,0:T(8,128)S(1)} %get-tuple-element.76.after_ref), channel_id=1, source_target_pairs={{0,20},{4,8},{8,28},{12,0},{16,4},{20,24},{24,12},{28,16},{1,21},{... | collective-permute-start | bytes 786440 | tf_op jit(solution)/shard_map/ppermute | solution.py:441
  14.3 6.7 %collective-permute-start.4 = (f32[512,128]{1,0:T(8,128)S(1)}, f32[512,128]{1,0:T(8,128)S(1)}, u32[]{:S(2)}, u32[]{:S(2)}) collective-permute-start(f32[512,128]{1,0:T(8,128)S(1)} %get-tuple-element.75), channel_id=1, source_target_pairs={{0,4},{4,0},{8,12},{12,8},{16,20},{20,16},{24,28},{28,24},{1,5},{5... | collective-permute-start | bytes 786440 | tf_op jit(solution)/shard_map/ppermute | solution.py:483
  15.6 6.0 %collective-permute-start.3 = (f32[512,128]{1,0:T(8,128)S(1)}, f32[512,128]{1,0:T(8,128)S(1)}, u32[]{:S(2)}, u32[]{:S(2)}) collective-permute-start(f32[512,128]{1,0:T(8,128)S(1)} %get-tuple-element.74.after_ref), channel_id=1, source_target_pairs={{0,20},{4,8},{8,28},{12,0},{16,4},{20,24},{24,12},{28,16},{1,21},{... | collective-permute-start | bytes 786440 | tf_op jit(solution)/shard_map/ppermute | solution.py:441
  17.1 6.0 %collective-permute-start.7 = (f32[512,128]{1,0:T(8,128)S(1)}, f32[512,128]{1,0:T(8,128)S(1)}, u32[]{:S(2)}, u32[]{:S(2)}) collective-permute-start(f32[512,128]{1,0:T(8,128)S(1)} %get-tuple-element.73), channel_id=1, source_target_pairs={{0,4},{4,0},{8,12},{12,8},{16,20},{20,16},{24,28},{28,24},{1,5},{5... | collective-permute-start | bytes 786440 | tf_op jit(solution)/shard_map/ppermute | solution.py:483
  21.0 1.6 %collective-permute-start.8 = (f32[512,128]{1,0:T(8,128)S(1)}, f32[512,128]{1,0:T(8,128)S(1)}, u32[]{:S(2)}, u32[]{:S(2)}) collective-permute-start(f32[512,128]{1,0:T(8,128)S(1)} %broadcast_add_fusion.after_ref), channel_id=1, source_target_pairs={{0,4},{4,0},{8,12},{12,8},{16,20},{20,16},{24,28},{28,24},{1,5},{5... | collective-permute-start | bytes 786440 | tf_op jit(solution)/shard_map/ppermute | solution.py:491
  21.7 2.0 %collective-permute-start.6 = (f32[512,128]{1,0:T(8,128)S(1)}, f32[512,128]{1,0:T(8,128)S(1)}, u32[]{:S(2)}, u32[]{:S(2)}) collective-permute-start(f32[512,128]{1,0:T(8,128)S(1)} %add_add_fusion.4.after_ref), channel_id=1, source_target_pairs={{0,4},{4,0},{8,12},{12,8},{16,20},{20,16},{24,28},{28,24},{1,5},{5... | collective-permute-start | bytes 786440 | tf_op jit(solution)/shard_map/ppermute | solution.py:491
  23.7 2.5 %copy-start = (bf16[1024,2048]{1,0:T(8,128)(2,1)S(1)}, bf16[1024,2048]{1,0:T(8,128)(2,1)}, u32[]{:S(2)}) copy-start(bf16[1024,2048]{1,0:T(8,128)(2,1)} %refs_1_.3) | copy-start | bytes 12582916
  23.8 2.5 %copy-start.1 = (f32[2048]{0:T(1024)S(1)}, f32[2048]{0:T(1024)}, u32[]{:S(2)}) copy-start(f32[2048]{0:T(1024)} %param.10) | copy-start | bytes 24580
  24.3 2.9 %collective-permute-start.10 = (f32[1,1024]{1,0:T(1,128)S(1)}, f32[1,1024]{1,0:T(1,128)S(1)}, u32[]{:S(2)}, u32[]{:S(2)}) collective-permute-start(f32[1,1024]{1,0:T(1,128)S(1)} %get-tuple-element.62.refs_3_), channel_id=1, source_target_pairs={{0,4},{4,0},{8,12},{12,8},{16,20},{20,16},{24,28},{28,24},{1,5},{5... | collective-permute-start | bytes 12296 | tf_op jit(solution)/shard_map/ppermute | solution.py:513
  24.5 3.0 %collective-permute-start.9 = (f32[1,1024]{1,0:T(1,128)S(1)}, f32[1,1024]{1,0:T(1,128)S(1)}, u32[]{:S(2)}, u32[]{:S(2)}) collective-permute-start(f32[1,1024]{1,0:T(1,128)S(1)} %get-tuple-element.62.refs_3_), channel_id=1, source_target_pairs={{0,5},{1,4},{2,7},{3,6},{4,1},{5,0},{6,3},{7,2},{8,13},{9,12},{10,... | collective-permute-start | bytes 12296 | tf_op jit(solution)/shard_map/ppermute | solution.py:513
  27.6 4.1 %collective-permute-start.11 = (f32[1,1024]{1,0:T(1,128)S(1)}, f32[1,1024]{1,0:T(1,128)S(1)}, u32[]{:S(2)}, u32[]{:S(2)}) collective-permute-start(f32[1,1024]{1,0:T(1,128)S(1)} %add_add_fusion.8.refs_3_), channel_id=1, source_target_pairs={{0,6},{1,7},{2,4},{3,5},{4,2},{5,3},{6,0},{7,1},{8,14},{9,15},{10,... | collective-permute-start | bytes 12296 | tf_op jit(solution)/shard_map/ppermute | solution.py:513
  30.3 1.3 %collective-permute-start.12 = (f32[1,1024]{1,0:T(1,128)S(1)}, f32[1,1024]{1,0:T(1,128)S(1)}, u32[]{:S(2)}, u32[]{:S(2)}) collective-permute-start(f32[1,1024]{1,0:T(1,128)S(1)} %add_add_fusion.8.refs_3_), channel_id=1, source_target_pairs={{0,4},{4,0},{8,12},{12,8},{16,20},{20,16},{24,28},{28,24},{1,5},{5... | collective-permute-start | bytes 12296 | tf_op jit(solution)/shard_map/ppermute | solution.py:513

commit v8 on v7

--- a/solution.py
+++ b/solution.py
@@ -211,23 +211,24 @@
         c -= chunks
 
 
-def inner_body(chunks, waits, query_refs, key_refs, value_refs, before_ref, inner_refs, zero_ref):
+def inner_body(chunks, waits, query_refs, key_refs, value_refs, before_ref, inner_refs, zero_ref, first_head=0):
     zero_ref[...] = jnp.zeros_like(zero_ref)
     rows_at = lax.broadcasted_iota(jnp.int32, (CHUNK, CHUNK), 0)
     cols_at = lax.broadcasted_iota(jnp.int32, (CHUNK, CHUNK), 1)
     causal = rows_at >= cols_at
     homes = [(ref, j) for ref in inner_refs for j in range(ref.shape[1] // HEAD_DIM)]
-    half = len(homes) * HEAD_DIM
+    heads = range(first_head, first_head + len(homes))
+    half = key_refs[0].shape[1]
     for c in range(chunks):
         if c in waits:
             waits[c].wait()
         (query_ref, q), (key_ref, k), (value_ref, v) = (chunk_in(x, c) for x in (query_refs, key_refs, value_refs))
         scores = []
-        for h in range(len(homes)):
+        for h in heads:
             full = dot_nt(query_ref[q, head(h)], key_ref[k, head(h)])
             scores.append(jnp.where(causal, full, 0.0).astype(BF16))
-        for h, (inner_ref, j) in enumerate(homes):
-            left, right = scores[h], value_ref[v, head(h)]
+        for h, score, (inner_ref, j) in zip(heads, scores, homes):
+            left, right = score, value_ref[v, head(h)]
             if c > 0:
                 at = (c - 1) * half + h * HEAD_DIM
                 left = jnp.concatenate([left, query_ref[q, head(h)]], axis=1)
@@ -270,22 +271,21 @@
     )(place, in_hbm(queries), after, *[in_vmem(x) for x in (first_queries, *keys, *vals, before)])
 
 
-def other_kernel(after_ref, query_ref, key_ref, value_ref, before_ref, *refs):
-    *inner_refs, zero_ref = refs
+def other_kernel(first_head, after_ref, query_ref, key_ref, value_ref, before_ref, inner_ref, zero_ref):
     chunks = query_ref.shape[0] // CHUNK
-    inner_body(chunks, {}, (query_ref,), (key_ref,), (value_ref,), before_ref, inner_refs, zero_ref)
-
-
-def other_inner(queries, keys, vals, before, after, sizes):
-    tokens, half = queries.shape
-    out_shape = [pltpu.VMEM((tokens, n * HEAD_DIM), F32) for n in sizes] + [pltpu.VMEM((1, HEAD_DIM), F32)]
-    return pl.pallas_call(
-        other_kernel,
+    inner_body(chunks, {}, (query_ref,), (key_ref,), (value_ref,), before_ref, (inner_ref,), zero_ref, first_head)
+
+
+def other_inner(queries, keys, vals, before, after, first_head, count):
+    tokens = queries.shape[0]
+    width = count * HEAD_DIM
+    return pl.pallas_call(
+        lambda *refs: other_kernel(first_head, *refs),
         in_specs=[ANYWHERE] + [WHOLE] * 4,
-        out_specs=[WHOLE] * len(out_shape),
-        out_shape=out_shape,
-        compiler_params=params(8),
-        cost_estimate=cost(tokens * half * 6 * CHUNK, 12 * tokens * half),
+        out_specs=[WHOLE] * 2,
+        out_shape=[pltpu.VMEM((tokens, width), F32), pltpu.VMEM((1, HEAD_DIM), F32)],
+        compiler_params=params(8),
+        cost_estimate=cost(tokens * width * 6 * CHUNK, 12 * tokens * width),
         name="inner",
     )(after, *[in_vmem(x) for x in (queries, keys, vals, before)])
 
@@ -469,8 +469,9 @@
         held[True], held[False] = (first_queries, late_queries), (other_queries,)
         return zero
 
-    def other_inside(after):
-        *inside[False], zero = other_inner(*held[False], sent_keys, sent_vals, sent_before, after, sizes)
+    def other_inside(after, g=0):
+        part, zero = other_inner(*held[False], sent_keys, sent_vals, sent_before, after, starts[g], sizes[g])
+        inside.setdefault(False, []).append(part)
         return zero
 
     if blocks == 8:
@@ -500,6 +501,8 @@
         return zero_after(squares)
 
     zero = swap_part(0, jnp.zeros((1, HEAD_DIM), F32))
+    for g in range(1, GROUPS):
+        zero = other_inside(parts[0], g) + zero
     for g in range(GROUPS):
         zero = mix_group(False, zero)
         if g + 1 < GROUPS:

time: 34.3 us -> 34.3 us (level)
  waiting for transfers between devices: 1.54 us -> 1.14 us
    pallas_call x1 -> x2, Pallas kernels: 2.91 us -> 3.01 us  [other_inner(): pl.pallas_call(lambda *refs: other_kernel(first_head, *refs), in_specs=[A...]
  transfers between devices with their start and end apart: 13 -> 13, of which waited for: 6 -> 5; matrix products, arithmetic and copies ran while one was open for 1% -> 1% of each run, Pallas kernels for 38% -> 38%
where the time goes in v8:
time: 34.3 us; the launch traced here: 34.2 us
  Pallas kernels  18.8 us (55%)
  starting transfers between devices  13.4 us (39%)
  waiting for transfers between devices  1.14 us (3%)
  other arithmetic  0.49 us (1%)
  between operations  0.41 us (1%)
    ppermute x2, starting transfers between devices, crossed(): lax.ppermute(power, ('ctx', 'head'), pairs)  4.41 us
    pallas_call x1, Pallas kernels, mine_inner(): pl.pallas_call(mine_kernel, in_specs=[SCALARS, ANYWHERE, ANYWHERE] + [WHO...  4.16 us
    pallas_call x2, Pallas kernels, other_inner(): pl.pallas_call(lambda *refs: other_kernel(first_head, *refs), in_specs=[A...  3.01 us
    ppermute x2, starting transfers between devices, two_steps(): lax.ppermute(x, 'ctx', [(i, i ^ (5 if i % 2 == 0 else 3)) for i in range(...  2.99 us
    pallas_call x1, Pallas kernels, sent_states(): pl.pallas_call(sent_kernel, in_specs=[SCALARS] + [ANYWHERE] * 3, out_spec...  2.88 us
    ppermute x2, starting transfers between devices, two_steps(): lax.ppermute(x, 'ctx', [(i, i ^ (2 if i % 2 == 0 else 4)) for i in range(...  2.66 us
    pallas_call x1, Pallas kernels, scale(): pl.pallas_call(lambda *refs: scale_kernel(features, *refs), in_specs=[SCA...  2.35 us
    pallas_call x1, Pallas kernels, kept_states(): pl.pallas_call(kept_kernel, in_specs=[SCALARS] + [ANYWHERE] * 3 + [WHOLE]...  2.33 us
  transfers between devices with their start and end apart: 13, of which 5 were waited for; matrix products, arithmetic and copies ran while one was open for 1% of the time, Pallas kernels for 38%

profile of v8, /device:TPU:0, one launch (start us, length us, event | category | flops | bytes accessed | tf_op | source)
XLA Modules:
  0.0 34.2 jit_solution(6149272787279399105)
XLA Ops:
  0.0 2.9 %states.2 = (f32[1024,128]{1,0:T(8,128)S(1)}, bf16[3072,128]{1,0:T(8,128)(2,1)S(1)}, bf16[1024,1024]{1,0:T(8,128)(2,1)S(1)}, bf16[1024,1024]{1,0:T(8,128)(2,1)S(...) custom-call(s32[1]{0:T(128)} %bitcast.place_ref.refs_0_, s32[8]{0:T(128)} %session_ref.1, ...), custom_call_target="tpu_custom_call" | custom-call | flops 268435456 | bytes 6291456 | tf_op jit(solution)/shard_map/states/pallas_call | solution.py:113
  2.9 0.5 %collective-permute-start = (f32[1024,128]{1,0:T(8,128)S(1)}, f32[1024,128]{1,0:T(8,128)S(1)}, u32[]{:S(2)}, u32[]{:S(2)}) collective-permute-start(f32[1024,128]{1,0:T(8,128)S(1)} %get-tuple-element.43), channel_id=1, source_target_pairs={{0,4},{4,0},{8,12},{12,8},{16,20},{20,16},{24,28},{28,24},{1,5},{5... | collective-permute-start | bytes 1572872 | tf_op jit(solution)/shard_map/ppermute | solution.py:456
  3.4 2.3 %states.3 = (f32[512,128]{1,0:T(8,128)S(1)}, f32[512,128]{1,0:T(8,128)S(1)}, bf16[3072,128]{1,0:T(8,128)(2,1)S(1)}, bf16[512,1024]{1,0:T(8,128)(2,1)S(1)}, bf16[...) custom-call(s32[1]{0:T(128)} %bitcast.place_ref.refs_0_, bf16[1024,2048]{1,0:T(8,128)(2,1)} %key_ref.3, ...), custom_call_target="tpu_custom_call" | custom-call | flops 268435456 | bytes 2097152 | tf_op jit(solution)/shard_map/states/pallas_call | solution.py:166
  5.8 0.1 slice_add_fusion
  5.8 2.6 %collective-permute-start.2 = (f32[512,128]{1,0:T(8,128)S(1)}, f32[512,128]{1,0:T(8,128)S(1)}, u32[]{:S(2)}, u32[]{:S(2)}) collective-permute-start(f32[512,128]{1,0:T(8,128)S(1)} %get-tuple-element.74.after_ref), channel_id=1, source_target_pairs={{0,8},{4,20},{8,0},{12,28},{16,24},{20,4},{24,16},{28,12},{1,9},{5... | collective-permute-start | bytes 786440 | tf_op jit(solution)/shard_map/ppermute | solution.py:435
  8.4 0.1 collective-permute-start.1
  8.5 4.2 %inner.3 = (bf16[512,1024]{1,0:T(8,128)(2,1)S(1)}, bf16[1024,1024]{1,0:T(8,128)(2,1)S(1)}, f32[1024,512]{1,0:T(8,128)S(1)}, f32[1024,512]{1,0:T(8,128)S(1)}, f32[1,128]{1,0:T(1,128)S(1)}) custom-call(s32[1]{0:T(128)} %bitcast.place_ref.refs_0_, bf16[1024,2048]{1,0:T(8,128)(2,1)} %query_ref.3, f32[512,128]{1,0:T(8,128)S(1)} %get-tuple-element.74.after_ref, ...), custom_call_target="tpu_custom_call" | custom-call | flops 1610612736 | bytes 12582912 | tf_op jit(solution)/shard_map/inner/pallas_call | solution.py:262
  12.7 0.1 collective-permute-done.2
  12.8 0.1 multiply_add_fusion.1
  12.8 1.5 %collective-permute-start.5 = (f32[512,128]{1,0:T(8,128)S(1)}, f32[512,128]{1,0:T(8,128)S(1)}, u32[]{:S(2)}, u32[]{:S(2)}) collective-permute-start(f32[512,128]{1,0:T(8,128)S(1)} %get-tuple-element.78.after_ref), channel_id=1, source_target_pairs={{0,20},{4,8},{8,28},{12,0},{16,4},{20,24},{24,12},{28,16},{1,21},{... | collective-permute-start | bytes 786440 | tf_op jit(solution)/shard_map/ppermute | solution.py:441
  14.3 0.7 %collective-permute-start.4 = (f32[512,128]{1,0:T(8,128)S(1)}, f32[512,128]{1,0:T(8,128)S(1)}, u32[]{:S(2)}, u32[]{:S(2)}) collective-permute-start(f32[512,128]{1,0:T(8,128)S(1)} %get-tuple-element.77), channel_id=1, source_target_pairs={{0,4},{4,0},{8,12},{12,8},{16,20},{20,16},{24,28},{28,24},{1,5},{5... | collective-permute-start | bytes 786440 | tf_op jit(solution)/shard_map/ppermute | solution.py:484
  15.0 0.5 %collective-permute-done.1 = f32[512,128]{1,0:T(8,128)S(1)} collective-permute-done((f32[512,128]{1,0:T(8,128)S(1)}, f32[512,128]{1,0:T(8,128)S(1)}, u32[]{:S(2)}, u32[]{:S(2)}) %collective-permute-start.1) | collective-permute-done | bytes 262176 | tf_op jit(solution)/shard_map/ppermute | solution.py:435
  15.6 0.1 multiply_add_fusion
  15.6 1.5 %collective-permute-start.3 = (f32[512,128]{1,0:T(8,128)S(1)}, f32[512,128]{1,0:T(8,128)S(1)}, u32[]{:S(2)}, u32[]{:S(2)}) collective-permute-start(f32[512,128]{1,0:T(8,128)S(1)} %get-tuple-element.76.refs_0_), channel_id=1, source_target_pairs={{0,20},{4,8},{8,28},{12,0},{16,4},{20,24},{24,12},{28,16},{1,21},{... | collective-permute-start | bytes 786440 | tf_op jit(solution)/shard_map/ppermute | solution.py:441
  17.2 0.8 %collective-permute-start.7 = (f32[512,128]{1,0:T(8,128)S(1)}, f32[512,128]{1,0:T(8,128)S(1)}, u32[]{:S(2)}, u32[]{:S(2)}) collective-permute-start(f32[512,128]{1,0:T(8,128)S(1)} %get-tuple-element.75), channel_id=1, source_target_pairs={{0,4},{4,0},{8,12},{12,8},{16,20},{20,16},{24,28},{28,24},{1,5},{5... | collective-permute-start | bytes 786440 | tf_op jit(solution)/shard_map/ppermute | solution.py:484
  18.0 1.5 %inner.4 = (f32[1024,512]{1,0:T(8,128)S(1)}, f32[1,128]{1,0:T(1,128)S(1)}) custom-call(f32[512,128]{1,0:T(8,128)S(1)} %get-tuple-element.76.refs_0_, bf16[1024,1024]{1,0:T(8,128)(2,1)S(1)} %get-tuple-element.52.refs_1_.refs_0_, bf16[1024,1024]{1,0:T(8,128)(2,1)S(1)} %get-tuple-element.53.refs_2_, bf16[1024,1024]{1,0:T(8,128)(2,1)S(1)} %get-tuple-element.54.refs_3_, ...), custom_call_target="tpu_custom_call" | custom-call | flops 805306368 | bytes 6291456 | tf_op jit(solution)/shard_map/inner/pallas_call | solution.py:282
  19.6 0.1 collective-permute-start.8
  19.7 1.5 %inner.5 = (f32[1024,512]{1,0:T(8,128)S(1)}, f32[1,128]{1,0:T(1,128)S(1)}) custom-call(f32[512,128]{1,0:T(8,128)S(1)} %broadcast_add_fusion.refs_0_.after_ref, bf16[1024,1024]{1,0:T(8,128)(2,1)S(1)} %get-tuple-element.52.refs_1_.refs_0_, bf16[1024,1024]{1,0:T(8,128)(2,1)S(1)} %get-tuple-element.53.refs_2_, bf16[1024,1024]{1,0:T(8,128)(2,1)S(1)} %get-tuple-element.54.refs_3_, ...), custom_call_target="tpu_custom_call" | custom-call | flops 805306368 | bytes 6291456 | tf_op jit(solution)/shard_map/inner/pallas_call | solution.py:282
  21.2 0.5 %mix.4 = (f32[1024,512]{1,0:T(8,128)S(1)}, f32[1024,128]{1,0:T(8,128)S(1)}) custom-call(bf16[1024,1024]{1,0:T(8,128)(2,1)S(1)} %get-tuple-element.52.refs_1_.refs_0_, f32[1024,512]{1,0:T(8,128)S(1)} %get-tuple-element.57.refs_1_, f32[512,128]{1,0:T(8,128)S(1)} %add_add_fusion.3.refs_2_), custom_call_target="tpu_custom_call" | custom-call | flops 134217728 | bytes 6291456 | tf_op jit(solution)/shard_map/mix/pallas_call | solution.py:316
  21.8 0.6 %collective-permute-start.6 = (f32[512,128]{1,0:T(8,128)S(1)}, f32[512,128]{1,0:T(8,128)S(1)}, u32[]{:S(2)}, u32[]{:S(2)}) collective-permute-start(f32[512,128]{1,0:T(8,128)S(1)} %add_add_fusion.4.after_ref), channel_id=1, source_target_pairs={{0,4},{4,0},{8,12},{12,8},{16,20},{20,16},{24,28},{28,24},{1,5},{5... | collective-permute-start | bytes 786440 | tf_op jit(solution)/shard_map/ppermute | solution.py:492
  22.4 0.5 %mix.5 = (f32[1024,512]{1,0:T(8,128)S(1)}, f32[1024,128]{1,0:T(8,128)S(1)}) custom-call(bf16[512,1024]{1,0:T(8,128)(2,1)S(1)} %get-tuple-element.41.first_queries.refs_0_, bf16[512,1024]{1,0:T(8,128)(2,1)S(1)} %get-tuple-element.47.refs_1_, f32[1024,512]{1,0:T(8,128)S(1)} %get-tuple-element.61.refs_2_, f32[512,128]{1,0:T(8,128)S(1)} %add_add_fusion.refs_3_, ...), custom_call_target="tpu_custom_call" | custom-call | flops 134217728 | bytes 6291456 | tf_op jit(solution)/shard_map/mix/pallas_call | solution.py:316
  22.9 0.5 %mix.6 = (f32[1024,512]{1,0:T(8,128)S(1)}, f32[1024,128]{1,0:T(8,128)S(1)}) custom-call(bf16[1024,1024]{1,0:T(8,128)(2,1)S(1)} %get-tuple-element.52.refs_1_.refs_0_, f32[1024,512]{1,0:T(8,128)S(1)} %get-tuple-element.60.refs_1_, f32[512,128]{1,0:T(8,128)S(1)} %add_add_fusion.1.refs_2_, f32[1024,128]{1,0:T(8,128)S(1)} %get-tuple-element.62.after_ref.refs_3_), custom_call_target="tpu_custom_call" | custom-call | flops 134217728 | bytes 6291456 | tf_op jit(solution)/shard_map/mix/pallas_call | solution.py:316
  23.6 0.5 %mix.7 = (f32[1024,512]{1,0:T(8,128)S(1)}, f32[1,1024]{1,0:T(1,128)S(1)}) custom-call(bf16[512,1024]{1,0:T(8,128)(2,1)S(1)} %get-tuple-element.41.first_queries.refs_0_, bf16[512,1024]{1,0:T(8,128)(2,1)S(1)} %get-tuple-element.47.refs_1_, f32[1024,512]{1,0:T(8,128)S(1)} %get-tuple-element.48.refs_2_, f32[512,128]{1,0:T(8,128)S(1)} %add_add_fusion.2.refs_3_, ...), custom_call_target="tpu_custom_call" | custom-call | flops 134217728 | bytes 6291456 | tf_op jit(solution)/shard_map/mix/pallas_call | solution.py:316
  24.1 0.4 %collective-permute-start.10 = (f32[1,1024]{1,0:T(1,128)S(1)}, f32[1,1024]{1,0:T(1,128)S(1)}, u32[]{:S(2)}, u32[]{:S(2)}) collective-permute-start(f32[1,1024]{1,0:T(1,128)S(1)} %get-tuple-element.64.refs_3_), channel_id=1, source_target_pairs={{0,4},{4,0},{8,12},{12,8},{16,20},{20,16},{24,28},{28,24},{1,5},{5... | collective-permute-start | bytes 12296 | tf_op jit(solution)/shard_map/ppermute | solution.py:516
  24.6 1.7 %collective-permute-start.9 = (f32[1,1024]{1,0:T(1,128)S(1)}, f32[1,1024]{1,0:T(1,128)S(1)}, u32[]{:S(2)}, u32[]{:S(2)}) collective-permute-start(f32[1,1024]{1,0:T(1,128)S(1)} %get-tuple-element.64.refs_3_), channel_id=1, source_target_pairs={{0,5},{1,4},{2,7},{3,6},{4,1},{5,0},{6,3},{7,2},{8,13},{9,12},{10,... | collective-permute-start | bytes 12296 | tf_op jit(solution)/shard_map/ppermute | solution.py:516
  26.2 1.0 %gate.2 = (f32[1024,1024]{1,0:T(8,128)S(1)}, f32[1,1024]{1,0:T(1,128)S(1)}) custom-call(s32[1]{0:T(128)} %bitcast.place_ref.refs_0_, bf16[1024,2048]{1,0:T(8,128)(2,1)S(1)} %copy-done, f32[1,2048]{1,0:T(1,128)S(1)} %bitcast.21, f32[1,1024]{1,0:T(1,128)S(1)} %get-tuple-element.64.refs_3_, f32[1024,512]{1,0:T(8,128)S(1)} %get-tuple-element.65.refs_4_, ...), custom_call_target="tpu_custom_call" | custom-call | flops 16777216 | bytes 4194304 | tf_op jit(solution)/shard_map/gate/pallas_call | solution.py:351
  27.3 0.3 collective-permute-done.9
  27.6 2.7 %collective-permute-start.11 = (f32[1,1024]{1,0:T(1,128)S(1)}, f32[1,1024]{1,0:T(1,128)S(1)}, u32[]{:S(2)}, u32[]{:S(2)}) collective-permute-start(f32[1,1024]{1,0:T(1,128)S(1)} %add_add_fusion.8.refs_3_), channel_id=1, source_target_pairs={{0,6},{1,7},{2,4},{3,5},{4,2},{5,3},{6,0},{7,1},{8,14},{9,15},{10,... | collective-permute-start | bytes 12296 | tf_op jit(solution)/shard_map/ppermute | solution.py:516
  30.4 0.2 collective-permute-start.12
  30.5 1.0 %gate.3 = (f32[1024,1024]{1,0:T(8,128)S(1)}, f32[1,1024]{1,0:T(1,128)S(1)}) custom-call(s32[1]{0:T(128)} %bitcast.place_ref.refs_0_, bf16[1024,2048]{1,0:T(8,128)(2,1)S(1)} %copy-done, f32[1,2048]{1,0:T(1,128)S(1)} %bitcast.22, f32[1,1024]{1,0:T(1,128)S(1)} %add_add_fusion.8.refs_3_, f32[1024,512]{1,0:T(8,128)S(1)} %get-tuple-element.68.refs_4_, ...), custom_call_target="tpu_custom_call" | custom-call | flops 16777216 | bytes 4194304 | tf_op jit(solution)/shard_map/gate/pallas_call | solution.py:351
  31.6 0.1 collective-permute-done.11
  31.7 2.3 %scale.1 = bf16[1024,2048]{1,0:T(8,128)(2,1)} custom-call(s32[1]{0:T(128)} %bitcast.place_ref.refs_0_, f32[1024,1024]{1,0:T(8,128)S(1)} %get-tuple-element.70.refs_1_, f32[1024,1024]{1,0:T(8,128)S(1)} %get-tuple-element.71.refs_2_, f32[1,1024]{1,0:T(1,128)S(1)} %add_add_fusion.7.refs_3_), custom_call_target="tpu_custom_call" | custom-call | flops 4194304 | bytes 4194304 | tf_op jit(solution)/shard_map/scale/pallas_call | solution.py:382
  (29 shorter events, 0.4 us)
Async XLA Ops:
  2.9 2.9 %collective-permute-start = (f32[1024,128]{1,0:T(8,128)S(1)}, f32[1024,128]{1,0:T(8,128)S(1)}, u32[]{:S(2)}, u32[]{:S(2)}) collective-permute-start(f32[1024,128]{1,0:T(8,128)S(1)} %get-tuple-element.43), channel_id=1, source_target_pairs={{0,4},{4,0},{8,12},{12,8},{16,20},{20,16},{24,28},{28,24},{1,5},{5... | collective-permute-start | bytes 1572872 | tf_op jit(solution)/shard_map/ppermute | solution.py:456
  5.8 6.9 %collective-permute-start.2 = (f32[512,128]{1,0:T(8,128)S(1)}, f32[512,128]{1,0:T(8,128)S(1)}, u32[]{:S(2)}, u32[]{:S(2)}) collective-permute-start(f32[512,128]{1,0:T(8,128)S(1)} %get-tuple-element.74.after_ref), channel_id=1, source_target_pairs={{0,8},{4,20},{8,0},{12,28},{16,24},{20,4},{24,16},{28,12},{1,9},{5... | collective-permute-start | bytes 786440 | tf_op jit(solution)/shard_map/ppermute | solution.py:435
  8.4 7.2 %collective-permute-start.1 = (f32[512,128]{1,0:T(8,128)S(1)}, f32[512,128]{1,0:T(8,128)S(1)}, u32[]{:S(2)}, u32[]{:S(2)}) collective-permute-start(f32[512,128]{1,0:T(8,128)S(1)} %get-tuple-element.73), channel_id=1, source_target_pairs={{0,8},{4,20},{8,0},{12,28},{16,24},{20,4},{24,16},{28,12},{1,9},{5... | collective-permute-start | bytes 786440 | tf_op jit(solution)/shard_map/ppermute | solution.py:435
  12.8 6.7 %collective-permute-start.5 = (f32[512,128]{1,0:T(8,128)S(1)}, f32[512,128]{1,0:T(8,128)S(1)}, u32[]{:S(2)}, u32[]{:S(2)}) collective-permute-start(f32[512,128]{1,0:T(8,128)S(1)} %get-tuple-element.78.after_ref), channel_id=1, source_target_pairs={{0,20},{4,8},{8,28},{12,0},{16,4},{20,24},{24,12},{28,16},{1,21},{... | collective-permute-start | bytes 786440 | tf_op jit(solution)/shard_map/ppermute | solution.py:441
  14.3 6.9 %collective-permute-start.4 = (f32[512,128]{1,0:T(8,128)S(1)}, f32[512,128]{1,0:T(8,128)S(1)}, u32[]{:S(2)}, u32[]{:S(2)}) collective-permute-start(f32[512,128]{1,0:T(8,128)S(1)} %get-tuple-element.77), channel_id=1, source_target_pairs={{0,4},{4,0},{8,12},{12,8},{16,20},{20,16},{24,28},{28,24},{1,5},{5... | collective-permute-start | bytes 786440 | tf_op jit(solution)/shard_map/ppermute | solution.py:484
  15.6 6.1 %collective-permute-start.3 = (f32[512,128]{1,0:T(8,128)S(1)}, f32[512,128]{1,0:T(8,128)S(1)}, u32[]{:S(2)}, u32[]{:S(2)}) collective-permute-start(f32[512,128]{1,0:T(8,128)S(1)} %get-tuple-element.76.refs_0_), channel_id=1, source_target_pairs={{0,20},{4,8},{8,28},{12,0},{16,4},{20,24},{24,12},{28,16},{1,21},{... | collective-permute-start | bytes 786440 | tf_op jit(solution)/shard_map/ppermute | solution.py:441
  17.2 5.7 %collective-permute-start.7 = (f32[512,128]{1,0:T(8,128)S(1)}, f32[512,128]{1,0:T(8,128)S(1)}, u32[]{:S(2)}, u32[]{:S(2)}) collective-permute-start(f32[512,128]{1,0:T(8,128)S(1)} %get-tuple-element.75), channel_id=1, source_target_pairs={{0,4},{4,0},{8,12},{12,8},{16,20},{20,16},{24,28},{28,24},{1,5},{5... | collective-permute-start | bytes 786440 | tf_op jit(solution)/shard_map/ppermute | solution.py:484
  19.6 2.8 %collective-permute-start.8 = (f32[512,128]{1,0:T(8,128)S(1)}, f32[512,128]{1,0:T(8,128)S(1)}, u32[]{:S(2)}, u32[]{:S(2)}) collective-permute-start(f32[512,128]{1,0:T(8,128)S(1)} %broadcast_add_fusion.refs_0_.after_ref), channel_id=1, source_target_pairs={{0,4},{4,0},{8,12},{12,8},{16,20},{20,16},{24,28},{28,24},{1,5},{5... | collective-permute-start | bytes 786440 | tf_op jit(solution)/shard_map/ppermute | solution.py:492
  21.8 1.7 %collective-permute-start.6 = (f32[512,128]{1,0:T(8,128)S(1)}, f32[512,128]{1,0:T(8,128)S(1)}, u32[]{:S(2)}, u32[]{:S(2)}) collective-permute-start(f32[512,128]{1,0:T(8,128)S(1)} %add_add_fusion.4.after_ref), channel_id=1, source_target_pairs={{0,4},{4,0},{8,12},{12,8},{16,20},{20,16},{24,28},{28,24},{1,5},{5... | collective-permute-start | bytes 786440 | tf_op jit(solution)/shard_map/ppermute | solution.py:492
  23.6 2.7 %copy-start = (bf16[1024,2048]{1,0:T(8,128)(2,1)S(1)}, bf16[1024,2048]{1,0:T(8,128)(2,1)}, u32[]{:S(2)}) copy-start(bf16[1024,2048]{1,0:T(8,128)(2,1)} %refs_1_.3) | copy-start | bytes 12582916
  23.6 2.7 %copy-start.1 = (f32[2048]{0:T(1024)S(1)}, f32[2048]{0:T(1024)}, u32[]{:S(2)}) copy-start(f32[2048]{0:T(1024)} %param.10) | copy-start | bytes 24580
  24.1 3.2 %collective-permute-start.10 = (f32[1,1024]{1,0:T(1,128)S(1)}, f32[1,1024]{1,0:T(1,128)S(1)}, u32[]{:S(2)}, u32[]{:S(2)}) collective-permute-start(f32[1,1024]{1,0:T(1,128)S(1)} %get-tuple-element.64.refs_3_), channel_id=1, source_target_pairs={{0,4},{4,0},{8,12},{12,8},{16,20},{20,16},{24,28},{28,24},{1,5},{5... | collective-permute-start | bytes 12296 | tf_op jit(solution)/shard_map/ppermute | solution.py:516
  24.6 3.0 %collective-permute-start.9 = (f32[1,1024]{1,0:T(1,128)S(1)}, f32[1,1024]{1,0:T(1,128)S(1)}, u32[]{:S(2)}, u32[]{:S(2)}) collective-permute-start(f32[1,1024]{1,0:T(1,128)S(1)} %get-tuple-element.64.refs_3_), channel_id=1, source_target_pairs={{0,5},{1,4},{2,7},{3,6},{4,1},{5,0},{6,3},{7,2},{8,13},{9,12},{10,... | collective-permute-start | bytes 12296 | tf_op jit(solution)/shard_map/ppermute | solution.py:516
  27.6 4.1 %collective-permute-start.11 = (f32[1,1024]{1,0:T(1,128)S(1)}, f32[1,1024]{1,0:T(1,128)S(1)}, u32[]{:S(2)}, u32[]{:S(2)}) collective-permute-start(f32[1,1024]{1,0:T(1,128)S(1)} %add_add_fusion.8.refs_3_), channel_id=1, source_target_pairs={{0,6},{1,7},{2,4},{3,5},{4,2},{5,3},{6,0},{7,1},{8,14},{9,15},{10,... | collective-permute-start | bytes 12296 | tf_op jit(solution)/shard_map/ppermute | solution.py:516
  30.4 1.3 %collective-permute-start.12 = (f32[1,1024]{1,0:T(1,128)S(1)}, f32[1,1024]{1,0:T(1,128)S(1)}, u32[]{:S(2)}, u32[]{:S(2)}) collective-permute-start(f32[1,1024]{1,0:T(1,128)S(1)} %add_add_fusion.8.refs_3_), channel_id=1, source_target_pairs={{0,4},{4,0},{8,12},{12,8},{16,20},{20,16},{24,28},{28,24},{1,5},{5... | collective-permute-start | bytes 12296 | tf_op jit(solution)/shard_map/ppermute | solution.py:516

commit v9 on v8

--- a/solution.py
+++ b/solution.py
@@ -140,7 +140,7 @@
     chunks = early + keys.shape[0] // CHUNK
     copies = []
     fetch(copies, sems, place_ref, True, ((key_ref, keys), (value_ref, vals)), range(early, chunks), early)
-    fetch(copies, sems, place_ref, True, ((query_ref, queries),), range(early))
+    fetch(copies, sems, place_ref, True, ((query_ref, queries),), range(queries.shape[0] // CHUNK))
     for c in range(early):
         add_chunk(c, first_keys, first_vals, chunk(c), state_refs, before_ref)
     for c in range(early, chunks):
@@ -161,14 +161,14 @@
         pltpu.VMEM(((chunks - 1) * half, HEAD_DIM), BF16),
         pltpu.VMEM((late, half), BF16),
         pltpu.VMEM((late, half), BF16),
-        pltpu.VMEM((tokens - late, half), BF16),
+        pltpu.VMEM((CHUNK, half), BF16),
     ]
     results = pl.pallas_call(
         kept_kernel,
         in_specs=[SCALARS] + [ANYWHERE] * 3 + [WHOLE] * 2,
         out_specs=[WHOLE] * len(out_shape),
         out_shape=out_shape,
-        scratch_shapes=[pltpu.SemaphoreType.DMA((chunks + late // CHUNK,))],
+        scratch_shapes=[pltpu.SemaphoreType.DMA((2 * late // CHUNK + 1,))],
         compiler_params=params(8),
         cost_estimate=cost(tokens * width * HEAD_DIM, tokens * width),
         name="states",
@@ -359,7 +359,7 @@
     )(place, in_vmem(gate_input), norm_gain.reshape(1, width), after, *[in_vmem(x) for x in mixed])
 
 
-def scale_kernel(features, place_ref, mine_ref, other_ref, power_ref, out_ref, mine_out, other_out, sems):
+def scale_kernel(features, place_ref, mine_ref, other_ref, power_ref, out_ref, buffer, sems):
     tokens, half = mine_ref.shape
     rows = HEAD_DIM
     copies = []
@@ -367,12 +367,12 @@
         at = slice(c * rows, (c + 1) * rows)
         power = jnp.broadcast_to(power_ref[:, at], (HEAD_DIM, rows))
         factor = lax.rsqrt(jnp.transpose(power) / features + 1e-06)
-        for j, (source, to) in enumerate(((mine_ref, mine_out), (other_ref, other_out))):
+        for mine, source in ((True, mine_ref), (False, other_ref)):
+            columns_of = half_heads(place_ref, mine, half)
             for h in range(half // HEAD_DIM):
-                to[at, head(h)] = (source[at, head(h)] * factor).astype(BF16)
-            cols = columns(place_ref, j == 0, half)
-            copies.append(pltpu.make_async_copy(to.at[at, :], out_ref.at[at, cols], sems.at[2 * c + j]))
-            copies[-1].start()
+                buffer[at, columns_of(h)] = (source[at, head(h)] * factor).astype(BF16)
+        copies.append(pltpu.make_async_copy(buffer.at[at, :], out_ref.at[at, :], sems.at[c]))
+        copies[-1].start()
     for copy in copies:
         copy.wait()
 
@@ -384,11 +384,7 @@
         in_specs=[SCALARS, WHOLE, WHOLE, WHOLE],
         out_specs=ANYWHERE,
         out_shape=pltpu.HBM((tokens, 2 * half), BF16),
-        scratch_shapes=[
-            pltpu.VMEM((tokens, half), BF16),
-            pltpu.VMEM((tokens, half), BF16),
-            pltpu.SemaphoreType.DMA((2 * tokens // HEAD_DIM,)),
-        ],
+        scratch_shapes=[pltpu.VMEM((tokens, 2 * half), BF16), pltpu.SemaphoreType.DMA((tokens // HEAD_DIM,))],
         compiler_params=params(8),
         cost_estimate=cost(4 * tokens * half, 4 * tokens * half),
         name="scale",

time: 34.3 us -> 34.3 us (level)
  Pallas kernels: 18.8 us -> 18.3 us
    pallas_call x1, Pallas kernels: 4.16 us -> 3.77 us  [mine_inner(): pl.pallas_call(mine_kernel, in_specs=[SCALARS, ANYWHERE, ANYWHERE] + [WHO...]
    ppermute x2, waiting for transfers between devices: 0.63 us -> 1.01 us  [two_steps(): lax.ppermute(x, 'ctx', [(i, i ^ (2 if i % 2 == 0 else 4)) for i in range(...]
  transfers between devices with their start and end apart: 13 -> 13, of which waited for: 5 -> 5; matrix products, arithmetic and copies ran while one was open for 1% -> 1% of each run, Pallas kernels for 38% -> 37%
where the time goes in v9:
time: 34.3 us; the launch traced here: 34.2 us
  Pallas kernels  18.3 us (53%)
  starting transfers between devices  13.5 us (39%)
  waiting for transfers between devices  1.47 us (4%)
  other arithmetic  0.49 us (1%)
  between operations  0.41 us (1%)
    ppermute x2, starting transfers between devices, crossed(): lax.ppermute(power, ('ctx', 'head'), pairs)  4.51 us
    pallas_call x1, Pallas kernels, mine_inner(): pl.pallas_call(mine_kernel, in_specs=[SCALARS, ANYWHERE, ANYWHERE] + [WHO...  3.77 us
    pallas_call x2, Pallas kernels, other_inner(): pl.pallas_call(lambda *refs: other_kernel(first_head, *refs), in_specs=[A...  2.96 us
    pallas_call x1, Pallas kernels, sent_states(): pl.pallas_call(sent_kernel, in_specs=[SCALARS] + [ANYWHERE] * 3, out_spec...  2.88 us
    ppermute x2, starting transfers between devices, two_steps(): lax.ppermute(x, 'ctx', [(i, i ^ (5 if i % 2 == 0 else 3)) for i in range(...  2.86 us
    ppermute x2, starting transfers between devices, two_steps(): lax.ppermute(x, 'ctx', [(i, i ^ (2 if i % 2 == 0 else 4)) for i in range(...  2.66 us
    pallas_call x1, Pallas kernels, kept_states(): pl.pallas_call(kept_kernel, in_specs=[SCALARS] + [ANYWHERE] * 3 + [WHOLE]...  2.31 us
    pallas_call x1, Pallas kernels, scale(): pl.pallas_call(lambda *refs: scale_kernel(features, *refs), in_specs=[SCA...  2.31 us
  transfers between devices with their start and end apart: 13, of which 5 were waited for; matrix products, arithmetic and copies ran while one was open for 1% of the time, Pallas kernels for 37%

profile of v9, /device:TPU:0, one launch (start us, length us, event | category | flops | bytes accessed | tf_op | source)
XLA Modules:
  0.0 34.2 jit_solution(11933871451939693161)
XLA Ops:
  0.0 2.9 %states.2 = (f32[1024,128]{1,0:T(8,128)S(1)}, bf16[3072,128]{1,0:T(8,128)(2,1)S(1)}, bf16[1024,1024]{1,0:T(8,128)(2,1)S(1)}, bf16[1024,1024]{1,0:T(8,128)(2,1)S(...) custom-call(s32[1]{0:T(128)} %bitcast.place_ref.refs_0_, s32[8]{0:T(128)} %session_ref.1, ...), custom_call_target="tpu_custom_call" | custom-call | flops 268435456 | bytes 6291456 | tf_op jit(solution)/shard_map/states/pallas_call | solution.py:113
  2.9 0.5 %collective-permute-start = (f32[1024,128]{1,0:T(8,128)S(1)}, f32[1024,128]{1,0:T(8,128)S(1)}, u32[]{:S(2)}, u32[]{:S(2)}) collective-permute-start(f32[1024,128]{1,0:T(8,128)S(1)} %get-tuple-element.43), channel_id=1, source_target_pairs={{0,4},{4,0},{8,12},{12,8},{16,20},{20,16},{24,28},{28,24},{1,5},{5... | collective-permute-start | bytes 1572872 | tf_op jit(solution)/shard_map/ppermute | solution.py:452
  3.4 2.3 %states.3 = (f32[512,128]{1,0:T(8,128)S(1)}, f32[512,128]{1,0:T(8,128)S(1)}, bf16[3072,128]{1,0:T(8,128)(2,1)S(1)}, bf16[512,1024]{1,0:T(8,128)(2,1)S(1)}, bf16[...) custom-call(s32[1]{0:T(128)} %bitcast.place_ref.refs_0_, bf16[1024,2048]{1,0:T(8,128)(2,1)} %key_ref.3, ...), custom_call_target="tpu_custom_call" | custom-call | flops 268435456 | bytes 2097152 | tf_op jit(solution)/shard_map/states/pallas_call | solution.py:166
  5.8 2.6 %collective-permute-start.2 = (f32[512,128]{1,0:T(8,128)S(1)}, f32[512,128]{1,0:T(8,128)S(1)}, u32[]{:S(2)}, u32[]{:S(2)}) collective-permute-start(f32[512,128]{1,0:T(8,128)S(1)} %get-tuple-element.74.after_ref), channel_id=1, source_target_pairs={{0,8},{4,20},{8,0},{12,28},{16,24},{20,4},{24,16},{28,12},{1,9},{5... | collective-permute-start | bytes 786440 | tf_op jit(solution)/shard_map/ppermute | solution.py:431
  8.4 0.1 collective-permute-start.1
  8.5 3.8 %inner.3 = (bf16[768,1024]{1,0:T(8,128)(2,1)S(1)}, bf16[1024,1024]{1,0:T(8,128)(2,1)S(1)}, f32[1024,512]{1,0:T(8,128)S(1)}, f32[1024,512]{1,0:T(8,128)S(1)}, f32[1,128]{1,0:T(1,128)S(1)}) custom-call(s32[1]{0:T(128)} %bitcast.place_ref.refs_0_, bf16[1024,2048]{1,0:T(8,128)(2,1)} %query_ref.3, f32[512,128]{1,0:T(8,128)S(1)} %get-tuple-element.74.after_ref, ...), custom_call_target="tpu_custom_call" | custom-call | flops 1610612736 | bytes 12582912 | tf_op jit(solution)/shard_map/inner/pallas_call | solution.py:262
  12.2 0.5 %collective-permute-done.2 = f32[512,128]{1,0:T(8,128)S(1)} collective-permute-done((f32[512,128]{1,0:T(8,128)S(1)}, f32[512,128]{1,0:T(8,128)S(1)}, u32[]{:S(2)}, u32[]{:S(2)}) %collective-permute-start.2) | collective-permute-done | bytes 262176 | tf_op jit(solution)/shard_map/ppermute | solution.py:431
  12.7 0.1 multiply_add_fusion.1
  12.8 1.3 %collective-permute-start.5 = (f32[512,128]{1,0:T(8,128)S(1)}, f32[512,128]{1,0:T(8,128)S(1)}, u32[]{:S(2)}, u32[]{:S(2)}) collective-permute-start(f32[512,128]{1,0:T(8,128)S(1)} %get-tuple-element.78.after_ref), channel_id=1, source_target_pairs={{0,20},{4,8},{8,28},{12,0},{16,4},{20,24},{24,12},{28,16},{1,21},{... | collective-permute-start | bytes 786440 | tf_op jit(solution)/shard_map/ppermute | solution.py:437
  14.2 0.8 %collective-permute-start.4 = (f32[512,128]{1,0:T(8,128)S(1)}, f32[512,128]{1,0:T(8,128)S(1)}, u32[]{:S(2)}, u32[]{:S(2)}) collective-permute-start(f32[512,128]{1,0:T(8,128)S(1)} %get-tuple-element.77), channel_id=1, source_target_pairs={{0,4},{4,0},{8,12},{12,8},{16,20},{20,16},{24,28},{28,24},{1,5},{5... | collective-permute-start | bytes 786440 | tf_op jit(solution)/shard_map/ppermute | solution.py:480
  15.0 0.5 %collective-permute-done.1 = f32[512,128]{1,0:T(8,128)S(1)} collective-permute-done((f32[512,128]{1,0:T(8,128)S(1)}, f32[512,128]{1,0:T(8,128)S(1)}, u32[]{:S(2)}, u32[]{:S(2)}) %collective-permute-start.1) | collective-permute-done | bytes 262176 | tf_op jit(solution)/shard_map/ppermute | solution.py:431
  15.5 0.1 multiply_add_fusion
  15.6 1.5 %collective-permute-start.3 = (f32[512,128]{1,0:T(8,128)S(1)}, f32[512,128]{1,0:T(8,128)S(1)}, u32[]{:S(2)}, u32[]{:S(2)}) collective-permute-start(f32[512,128]{1,0:T(8,128)S(1)} %get-tuple-element.76.refs_0_), channel_id=1, source_target_pairs={{0,20},{4,8},{8,28},{12,0},{16,4},{20,24},{24,12},{28,16},{1,21},{... | collective-permute-start | bytes 786440 | tf_op jit(solution)/shard_map/ppermute | solution.py:437
  17.1 0.8 %collective-permute-start.7 = (f32[512,128]{1,0:T(8,128)S(1)}, f32[512,128]{1,0:T(8,128)S(1)}, u32[]{:S(2)}, u32[]{:S(2)}) collective-permute-start(f32[512,128]{1,0:T(8,128)S(1)} %get-tuple-element.75), channel_id=1, source_target_pairs={{0,4},{4,0},{8,12},{12,8},{16,20},{20,16},{24,28},{28,24},{1,5},{5... | collective-permute-start | bytes 786440 | tf_op jit(solution)/shard_map/ppermute | solution.py:480
  18.0 1.5 %inner.4 = (f32[1024,512]{1,0:T(8,128)S(1)}, f32[1,128]{1,0:T(1,128)S(1)}) custom-call(f32[512,128]{1,0:T(8,128)S(1)} %get-tuple-element.76.refs_0_, bf16[1024,1024]{1,0:T(8,128)(2,1)S(1)} %get-tuple-element.52.refs_1_.refs_0_, bf16[1024,1024]{1,0:T(8,128)(2,1)S(1)} %get-tuple-element.53.refs_2_, bf16[1024,1024]{1,0:T(8,128)(2,1)S(1)} %get-tuple-element.54.refs_3_, ...), custom_call_target="tpu_custom_call" | custom-call | flops 805306368 | bytes 6291456 | tf_op jit(solution)/shard_map/inner/pallas_call | solution.py:282
  19.5 0.1 collective-permute-start.8
  19.6 1.5 %inner.5 = (f32[1024,512]{1,0:T(8,128)S(1)}, f32[1,128]{1,0:T(1,128)S(1)}) custom-call(f32[512,128]{1,0:T(8,128)S(1)} %broadcast_add_fusion.refs_0_.after_ref, bf16[1024,1024]{1,0:T(8,128)(2,1)S(1)} %get-tuple-element.52.refs_1_.refs_0_, bf16[1024,1024]{1,0:T(8,128)(2,1)S(1)} %get-tuple-element.53.refs_2_, bf16[1024,1024]{1,0:T(8,128)(2,1)S(1)} %get-tuple-element.54.refs_3_, ...), custom_call_target="tpu_custom_call" | custom-call | flops 805306368 | bytes 6291456 | tf_op jit(solution)/shard_map/inner/pallas_call | solution.py:282
  21.1 0.5 %mix.4 = (f32[1024,512]{1,0:T(8,128)S(1)}, f32[1024,128]{1,0:T(8,128)S(1)}) custom-call(bf16[1024,1024]{1,0:T(8,128)(2,1)S(1)} %get-tuple-element.52.refs_1_.refs_0_, f32[1024,512]{1,0:T(8,128)S(1)} %get-tuple-element.57.refs_1_, f32[512,128]{1,0:T(8,128)S(1)} %add_add_fusion.3.refs_2_), custom_call_target="tpu_custom_call" | custom-call | flops 134217728 | bytes 6291456 | tf_op jit(solution)/shard_map/mix/pallas_call | solution.py:316
  21.7 0.6 %collective-permute-start.6 = (f32[512,128]{1,0:T(8,128)S(1)}, f32[512,128]{1,0:T(8,128)S(1)}, u32[]{:S(2)}, u32[]{:S(2)}) collective-permute-start(f32[512,128]{1,0:T(8,128)S(1)} %add_add_fusion.4.after_ref), channel_id=1, source_target_pairs={{0,4},{4,0},{8,12},{12,8},{16,20},{20,16},{24,28},{28,24},{1,5},{5... | collective-permute-start | bytes 786440 | tf_op jit(solution)/shard_map/ppermute | solution.py:488
  22.3 0.5 %mix.5 = (f32[1024,512]{1,0:T(8,128)S(1)}, f32[1024,128]{1,0:T(8,128)S(1)}) custom-call(bf16[256,1024]{1,0:T(8,128)(2,1)S(1)} %get-tuple-element.41.first_queries.refs_0_, bf16[768,1024]{1,0:T(8,128)(2,1)S(1)} %get-tuple-element.47.refs_1_, f32[1024,512]{1,0:T(8,128)S(1)} %get-tuple-element.61.refs_2_, f32[512,128]{1,0:T(8,128)S(1)} %add_add_fusion.refs_3_, ...), custom_call_target="tpu_custom_call" | custom-call | flops 134217728 | bytes 6291456 | tf_op jit(solution)/shard_map/mix/pallas_call | solution.py:316
  22.9 0.5 %mix.6 = (f32[1024,512]{1,0:T(8,128)S(1)}, f32[1024,128]{1,0:T(8,128)S(1)}) custom-call(bf16[1024,1024]{1,0:T(8,128)(2,1)S(1)} %get-tuple-element.52.refs_1_.refs_0_, f32[1024,512]{1,0:T(8,128)S(1)} %get-tuple-element.60.refs_1_, f32[512,128]{1,0:T(8,128)S(1)} %add_add_fusion.1.refs_2_, f32[1024,128]{1,0:T(8,128)S(1)} %get-tuple-element.62.after_ref.refs_3_), custom_call_target="tpu_custom_call" | custom-call | flops 134217728 | bytes 6291456 | tf_op jit(solution)/shard_map/mix/pallas_call | solution.py:316
  23.3 0.1 collective-permute-done.6
  23.4 0.1 add_add_fusion.2.refs_3_
  23.5 0.6 %mix.7 = (f32[1024,512]{1,0:T(8,128)S(1)}, f32[1,1024]{1,0:T(1,128)S(1)}) custom-call(bf16[256,1024]{1,0:T(8,128)(2,1)S(1)} %get-tuple-element.41.first_queries.refs_0_, bf16[768,1024]{1,0:T(8,128)(2,1)S(1)} %get-tuple-element.47.refs_1_, f32[1024,512]{1,0:T(8,128)S(1)} %get-tuple-element.48.refs_2_, f32[512,128]{1,0:T(8,128)S(1)} %add_add_fusion.2.refs_3_, ...), custom_call_target="tpu_custom_call" | custom-call | flops 134217728 | bytes 6291456 | tf_op jit(solution)/shard_map/mix/pallas_call | solution.py:316
  24.1 0.4 %collective-permute-start.10 = (f32[1,1024]{1,0:T(1,128)S(1)}, f32[1,1024]{1,0:T(1,128)S(1)}, u32[]{:S(2)}, u32[]{:S(2)}) collective-permute-start(f32[1,1024]{1,0:T(1,128)S(1)} %get-tuple-element.64.refs_3_), channel_id=1, source_target_pairs={{0,4},{4,0},{8,12},{12,8},{16,20},{20,16},{24,28},{28,24},{1,5},{5... | collective-permute-start | bytes 12296 | tf_op jit(solution)/shard_map/ppermute | solution.py:512
  24.5 1.7 %collective-permute-start.9 = (f32[1,1024]{1,0:T(1,128)S(1)}, f32[1,1024]{1,0:T(1,128)S(1)}, u32[]{:S(2)}, u32[]{:S(2)}) collective-permute-start(f32[1,1024]{1,0:T(1,128)S(1)} %get-tuple-element.64.refs_3_), channel_id=1, source_target_pairs={{0,5},{1,4},{2,7},{3,6},{4,1},{5,0},{6,3},{7,2},{8,13},{9,12},{10,... | collective-permute-start | bytes 12296 | tf_op jit(solution)/shard_map/ppermute | solution.py:512
  26.2 1.0 %gate.2 = (f32[1024,1024]{1,0:T(8,128)S(1)}, f32[1,1024]{1,0:T(1,128)S(1)}) custom-call(s32[1]{0:T(128)} %bitcast.place_ref.refs_0_, bf16[1024,2048]{1,0:T(8,128)(2,1)S(1)} %copy-done, f32[1,2048]{1,0:T(1,128)S(1)} %bitcast.21, f32[1,1024]{1,0:T(1,128)S(1)} %get-tuple-element.64.refs_3_, f32[1024,512]{1,0:T(8,128)S(1)} %get-tuple-element.65.refs_4_, ...), custom_call_target="tpu_custom_call" | custom-call | flops 16777216 | bytes 4194304 | tf_op jit(solution)/shard_map/gate/pallas_call | solution.py:351
  27.3 0.3 collective-permute-done.9
  27.6 2.8 %collective-permute-start.11 = (f32[1,1024]{1,0:T(1,128)S(1)}, f32[1,1024]{1,0:T(1,128)S(1)}, u32[]{:S(2)}, u32[]{:S(2)}) collective-permute-start(f32[1,1024]{1,0:T(1,128)S(1)} %add_add_fusion.8.refs_3_), channel_id=1, source_target_pairs={{0,6},{1,7},{2,4},{3,5},{4,2},{5,3},{6,0},{7,1},{8,14},{9,15},{10,... | collective-permute-start | bytes 12296 | tf_op jit(solution)/shard_map/ppermute | solution.py:512
  30.3 0.2 collective-permute-start.12
  30.5 1.1 %gate.3 = (f32[1024,1024]{1,0:T(8,128)S(1)}, f32[1,1024]{1,0:T(1,128)S(1)}) custom-call(s32[1]{0:T(128)} %bitcast.place_ref.refs_0_, bf16[1024,2048]{1,0:T(8,128)(2,1)S(1)} %copy-done, f32[1,2048]{1,0:T(1,128)S(1)} %bitcast.22, f32[1,1024]{1,0:T(1,128)S(1)} %add_add_fusion.8.refs_3_, f32[1024,512]{1,0:T(8,128)S(1)} %get-tuple-element.68.refs_4_, ...), custom_call_target="tpu_custom_call" | custom-call | flops 16777216 | bytes 4194304 | tf_op jit(solution)/shard_map/gate/pallas_call | solution.py:351
  31.7 2.3 %scale.1 = bf16[1024,2048]{1,0:T(8,128)(2,1)} custom-call(s32[1]{0:T(128)} %bitcast.place_ref.refs_0_, f32[1024,1024]{1,0:T(8,128)S(1)} %get-tuple-element.70.refs_1_, f32[1024,1024]{1,0:T(8,128)S(1)} %get-tuple-element.71.refs_2_, f32[1,1024]{1,0:T(1,128)S(1)} %add_add_fusion.7.refs_3_), custom_call_target="tpu_custom_call" | custom-call | flops 4194304 | bytes 4194304 | tf_op jit(solution)/shard_map/scale/pallas_call | solution.py:382
  (29 shorter events, 0.4 us)
Async XLA Ops:
  2.9 2.8 %collective-permute-start = (f32[1024,128]{1,0:T(8,128)S(1)}, f32[1024,128]{1,0:T(8,128)S(1)}, u32[]{:S(2)}, u32[]{:S(2)}) collective-permute-start(f32[1024,128]{1,0:T(8,128)S(1)} %get-tuple-element.43), channel_id=1, source_target_pairs={{0,4},{4,0},{8,12},{12,8},{16,20},{20,16},{24,28},{28,24},{1,5},{5... | collective-permute-start | bytes 1572872 | tf_op jit(solution)/shard_map/ppermute | solution.py:452
  5.8 6.9 %collective-permute-start.2 = (f32[512,128]{1,0:T(8,128)S(1)}, f32[512,128]{1,0:T(8,128)S(1)}, u32[]{:S(2)}, u32[]{:S(2)}) collective-permute-start(f32[512,128]{1,0:T(8,128)S(1)} %get-tuple-element.74.after_ref), channel_id=1, source_target_pairs={{0,8},{4,20},{8,0},{12,28},{16,24},{20,4},{24,16},{28,12},{1,9},{5... | collective-permute-start | bytes 786440 | tf_op jit(solution)/shard_map/ppermute | solution.py:431
  8.4 7.2 %collective-permute-start.1 = (f32[512,128]{1,0:T(8,128)S(1)}, f32[512,128]{1,0:T(8,128)S(1)}, u32[]{:S(2)}, u32[]{:S(2)}) collective-permute-start(f32[512,128]{1,0:T(8,128)S(1)} %get-tuple-element.73), channel_id=1, source_target_pairs={{0,8},{4,20},{8,0},{12,28},{16,24},{20,4},{24,16},{28,12},{1,9},{5... | collective-permute-start | bytes 786440 | tf_op jit(solution)/shard_map/ppermute | solution.py:431
  12.8 6.6 %collective-permute-start.5 = (f32[512,128]{1,0:T(8,128)S(1)}, f32[512,128]{1,0:T(8,128)S(1)}, u32[]{:S(2)}, u32[]{:S(2)}) collective-permute-start(f32[512,128]{1,0:T(8,128)S(1)} %get-tuple-element.78.after_ref), channel_id=1, source_target_pairs={{0,20},{4,8},{8,28},{12,0},{16,4},{20,24},{24,12},{28,16},{1,21},{... | collective-permute-start | bytes 786440 | tf_op jit(solution)/shard_map/ppermute | solution.py:437
  14.2 6.9 %collective-permute-start.4 = (f32[512,128]{1,0:T(8,128)S(1)}, f32[512,128]{1,0:T(8,128)S(1)}, u32[]{:S(2)}, u32[]{:S(2)}) collective-permute-start(f32[512,128]{1,0:T(8,128)S(1)} %get-tuple-element.77), channel_id=1, source_target_pairs={{0,4},{4,0},{8,12},{12,8},{16,20},{20,16},{24,28},{28,24},{1,5},{5... | collective-permute-start | bytes 786440 | tf_op jit(solution)/shard_map/ppermute | solution.py:480
  15.6 6.0 %collective-permute-start.3 = (f32[512,128]{1,0:T(8,128)S(1)}, f32[512,128]{1,0:T(8,128)S(1)}, u32[]{:S(2)}, u32[]{:S(2)}) collective-permute-start(f32[512,128]{1,0:T(8,128)S(1)} %get-tuple-element.76.refs_0_), channel_id=1, source_target_pairs={{0,20},{4,8},{8,28},{12,0},{16,4},{20,24},{24,12},{28,16},{1,21},{... | collective-permute-start | bytes 786440 | tf_op jit(solution)/shard_map/ppermute | solution.py:437
  17.1 5.7 %collective-permute-start.7 = (f32[512,128]{1,0:T(8,128)S(1)}, f32[512,128]{1,0:T(8,128)S(1)}, u32[]{:S(2)}, u32[]{:S(2)}) collective-permute-start(f32[512,128]{1,0:T(8,128)S(1)} %get-tuple-element.75), channel_id=1, source_target_pairs={{0,4},{4,0},{8,12},{12,8},{16,20},{20,16},{24,28},{28,24},{1,5},{5... | collective-permute-start | bytes 786440 | tf_op jit(solution)/shard_map/ppermute | solution.py:480
  19.5 2.7 %collective-permute-start.8 = (f32[512,128]{1,0:T(8,128)S(1)}, f32[512,128]{1,0:T(8,128)S(1)}, u32[]{:S(2)}, u32[]{:S(2)}) collective-permute-start(f32[512,128]{1,0:T(8,128)S(1)} %broadcast_add_fusion.refs_0_.after_ref), channel_id=1, source_target_pairs={{0,4},{4,0},{8,12},{12,8},{16,20},{20,16},{24,28},{28,24},{1,5},{5... | collective-permute-start | bytes 786440 | tf_op jit(solution)/shard_map/ppermute | solution.py:488
  21.7 1.7 %collective-permute-start.6 = (f32[512,128]{1,0:T(8,128)S(1)}, f32[512,128]{1,0:T(8,128)S(1)}, u32[]{:S(2)}, u32[]{:S(2)}) collective-permute-start(f32[512,128]{1,0:T(8,128)S(1)} %add_add_fusion.4.after_ref), channel_id=1, source_target_pairs={{0,4},{4,0},{8,12},{12,8},{16,20},{20,16},{24,28},{28,24},{1,5},{5... | collective-permute-start | bytes 786440 | tf_op jit(solution)/shard_map/ppermute | solution.py:488
  23.5 2.7 %copy-start = (bf16[1024,2048]{1,0:T(8,128)(2,1)S(1)}, bf16[1024,2048]{1,0:T(8,128)(2,1)}, u32[]{:S(2)}) copy-start(bf16[1024,2048]{1,0:T(8,128)(2,1)} %refs_1_.3) | copy-start | bytes 12582916
  23.5 2.7 %copy-start.1 = (f32[2048]{0:T(1024)S(1)}, f32[2048]{0:T(1024)}, u32[]{:S(2)}) copy-start(f32[2048]{0:T(1024)} %param.10) | copy-start | bytes 24580
  24.1 3.2 %collective-permute-start.10 = (f32[1,1024]{1,0:T(1,128)S(1)}, f32[1,1024]{1,0:T(1,128)S(1)}, u32[]{:S(2)}, u32[]{:S(2)}) collective-permute-start(f32[1,1024]{1,0:T(1,128)S(1)} %get-tuple-element.64.refs_3_), channel_id=1, source_target_pairs={{0,4},{4,0},{8,12},{12,8},{16,20},{20,16},{24,28},{28,24},{1,5},{5... | collective-permute-start | bytes 12296 | tf_op jit(solution)/shard_map/ppermute | solution.py:512
  24.5 3.1 %collective-permute-start.9 = (f32[1,1024]{1,0:T(1,128)S(1)}, f32[1,1024]{1,0:T(1,128)S(1)}, u32[]{:S(2)}, u32[]{:S(2)}) collective-permute-start(f32[1,1024]{1,0:T(1,128)S(1)} %get-tuple-element.64.refs_3_), channel_id=1, source_target_pairs={{0,5},{1,4},{2,7},{3,6},{4,1},{5,0},{6,3},{7,2},{8,13},{9,12},{10,... | collective-permute-start | bytes 12296 | tf_op jit(solution)/shard_map/ppermute | solution.py:512
  27.6 4.1 %collective-permute-start.11 = (f32[1,1024]{1,0:T(1,128)S(1)}, f32[1,1024]{1,0:T(1,128)S(1)}, u32[]{:S(2)}, u32[]{:S(2)}) collective-permute-start(f32[1,1024]{1,0:T(1,128)S(1)} %add_add_fusion.8.refs_3_), channel_id=1, source_target_pairs={{0,6},{1,7},{2,4},{3,5},{4,2},{5,3},{6,0},{7,1},{8,14},{9,15},{10,... | collective-permute-start | bytes 12296 | tf_op jit(solution)/shard_map/ppermute | solution.py:512
  30.3 1.3 %collective-permute-start.12 = (f32[1,1024]{1,0:T(1,128)S(1)}, f32[1,1024]{1,0:T(1,128)S(1)}, u32[]{:S(2)}, u32[]{:S(2)}) collective-permute-start(f32[1,1024]{1,0:T(1,128)S(1)} %add_add_fusion.8.refs_3_), channel_id=1, source_target_pairs={{0,4},{4,0},{8,12},{12,8},{16,20},{20,16},{24,28},{28,24},{1,5},{5... | collective-permute-start | bytes 12296 | tf_op jit(solution)/shard_map/ppermute | solution.py:512

commit v10 on v9

--- a/solution.py
+++ b/solution.py
@@ -361,7 +361,7 @@
 
 def scale_kernel(features, place_ref, mine_ref, other_ref, power_ref, out_ref, buffer, sems):
     tokens, half = mine_ref.shape
-    rows = HEAD_DIM
+    rows = CHUNK
     copies = []
     for c in range(tokens // rows):
         at = slice(c * rows, (c + 1) * rows)
@@ -384,7 +384,7 @@
         in_specs=[SCALARS, WHOLE, WHOLE, WHOLE],
         out_specs=ANYWHERE,
         out_shape=pltpu.HBM((tokens, 2 * half), BF16),
-        scratch_shapes=[pltpu.VMEM((tokens, 2 * half), BF16), pltpu.SemaphoreType.DMA((tokens // HEAD_DIM,))],
+        scratch_shapes=[pltpu.VMEM((tokens, 2 * half), BF16), pltpu.SemaphoreType.DMA((tokens // CHUNK,))],
         compiler_params=params(8),
         cost_estimate=cost(4 * tokens * half, 4 * tokens * half),
         name="scale",

time: 34.3 us -> 34.4 us (level)
  no operation moved by 1% of the time
where the time goes in v10:
time: 34.4 us; the launch traced here: 34.2 us
  Pallas kernels  18.4 us (53%)
  starting transfers between devices  13.5 us (39%)
  waiting for transfers between devices  1.47 us (4%)
  other arithmetic  0.49 us (1%)
  between operations  0.41 us (1%)
    ppermute x2, starting transfers between devices, crossed(): lax.ppermute(power, ('ctx', 'head'), pairs)  4.51 us
    pallas_call x1, Pallas kernels, mine_inner(): pl.pallas_call(mine_kernel, in_specs=[SCALARS, ANYWHERE, ANYWHERE] + [WHO...  3.77 us
    pallas_call x2, Pallas kernels, other_inner(): pl.pallas_call(lambda *refs: other_kernel(first_head, *refs), in_specs=[A...  2.96 us
    pallas_call x1, Pallas kernels, sent_states(): pl.pallas_call(sent_kernel, in_specs=[SCALARS] + [ANYWHERE] * 3, out_spec...  2.88 us
    ppermute x2, starting transfers between devices, two_steps(): lax.ppermute(x, 'ctx', [(i, i ^ (5 if i % 2 == 0 else 3)) for i in range(...  2.86 us
    ppermute x2, starting transfers between devices, two_steps(): lax.ppermute(x, 'ctx', [(i, i ^ (2 if i % 2 == 0 else 4)) for i in range(...  2.66 us
    pallas_call x1, Pallas kernels, scale(): pl.pallas_call(lambda *refs: scale_kernel(features, *refs), in_specs=[SCA...  2.39 us
    pallas_call x1, Pallas kernels, kept_states(): pl.pallas_call(kept_kernel, in_specs=[SCALARS] + [ANYWHERE] * 3 + [WHOLE]...  2.31 us
  transfers between devices with their start and end apart: 13, of which 5 were waited for; matrix products, arithmetic and copies ran while one was open for 1% of the time, Pallas kernels for 37%

profile of v10, /device:TPU:0, one launch (start us, length us, event | category | flops | bytes accessed | tf_op | source)
XLA Modules:
  0.0 34.2 jit_solution(10133707880250120499)
XLA Ops:
  0.0 2.9 %states.2 = (f32[1024,128]{1,0:T(8,128)S(1)}, bf16[3072,128]{1,0:T(8,128)(2,1)S(1)}, bf16[1024,1024]{1,0:T(8,128)(2,1)S(1)}, bf16[1024,1024]{1,0:T(8,128)(2,1)S(...) custom-call(s32[1]{0:T(128)} %bitcast.place_ref.refs_0_, s32[8]{0:T(128)} %session_ref.1, ...), custom_call_target="tpu_custom_call" | custom-call | flops 268435456 | bytes 6291456 | tf_op jit(solution)/shard_map/states/pallas_call | solution.py:113
  2.9 0.5 %collective-permute-start = (f32[1024,128]{1,0:T(8,128)S(1)}, f32[1024,128]{1,0:T(8,128)S(1)}, u32[]{:S(2)}, u32[]{:S(2)}) collective-permute-start(f32[1024,128]{1,0:T(8,128)S(1)} %get-tuple-element.43), channel_id=1, source_target_pairs={{0,4},{4,0},{8,12},{12,8},{16,20},{20,16},{24,28},{28,24},{1,5},{5... | collective-permute-start | bytes 1572872 | tf_op jit(solution)/shard_map/ppermute | solution.py:452
  3.4 2.3 %states.3 = (f32[512,128]{1,0:T(8,128)S(1)}, f32[512,128]{1,0:T(8,128)S(1)}, bf16[3072,128]{1,0:T(8,128)(2,1)S(1)}, bf16[512,1024]{1,0:T(8,128)(2,1)S(1)}, bf16[...) custom-call(s32[1]{0:T(128)} %bitcast.place_ref.refs_0_, bf16[1024,2048]{1,0:T(8,128)(2,1)} %key_ref.3, ...), custom_call_target="tpu_custom_call" | custom-call | flops 268435456 | bytes 2097152 | tf_op jit(solution)/shard_map/states/pallas_call | solution.py:166
  5.8 2.6 %collective-permute-start.2 = (f32[512,128]{1,0:T(8,128)S(1)}, f32[512,128]{1,0:T(8,128)S(1)}, u32[]{:S(2)}, u32[]{:S(2)}) collective-permute-start(f32[512,128]{1,0:T(8,128)S(1)} %get-tuple-element.74.after_ref), channel_id=1, source_target_pairs={{0,8},{4,20},{8,0},{12,28},{16,24},{20,4},{24,16},{28,12},{1,9},{5... | collective-permute-start | bytes 786440 | tf_op jit(solution)/shard_map/ppermute | solution.py:431
  8.4 0.1 collective-permute-start.1
  8.5 3.8 %inner.3 = (bf16[768,1024]{1,0:T(8,128)(2,1)S(1)}, bf16[1024,1024]{1,0:T(8,128)(2,1)S(1)}, f32[1024,512]{1,0:T(8,128)S(1)}, f32[1024,512]{1,0:T(8,128)S(1)}, f32[1,128]{1,0:T(1,128)S(1)}) custom-call(s32[1]{0:T(128)} %bitcast.place_ref.refs_0_, bf16[1024,2048]{1,0:T(8,128)(2,1)} %query_ref.3, f32[512,128]{1,0:T(8,128)S(1)} %get-tuple-element.74.after_ref, ...), custom_call_target="tpu_custom_call" | custom-call | flops 1610612736 | bytes 12582912 | tf_op jit(solution)/shard_map/inner/pallas_call | solution.py:262
  12.2 0.5 %collective-permute-done.2 = f32[512,128]{1,0:T(8,128)S(1)} collective-permute-done((f32[512,128]{1,0:T(8,128)S(1)}, f32[512,128]{1,0:T(8,128)S(1)}, u32[]{:S(2)}, u32[]{:S(2)}) %collective-permute-start.2) | collective-permute-done | bytes 262176 | tf_op jit(solution)/shard_map/ppermute | solution.py:431
  12.7 0.1 multiply_add_fusion.1
  12.8 1.3 %collective-permute-start.5 = (f32[512,128]{1,0:T(8,128)S(1)}, f32[512,128]{1,0:T(8,128)S(1)}, u32[]{:S(2)}, u32[]{:S(2)}) collective-permute-start(f32[512,128]{1,0:T(8,128)S(1)} %get-tuple-element.78.after_ref), channel_id=1, source_target_pairs={{0,20},{4,8},{8,28},{12,0},{16,4},{20,24},{24,12},{28,16},{1,21},{... | collective-permute-start | bytes 786440 | tf_op jit(solution)/shard_map/ppermute | solution.py:437
  14.2 0.8 %collective-permute-start.4 = (f32[512,128]{1,0:T(8,128)S(1)}, f32[512,128]{1,0:T(8,128)S(1)}, u32[]{:S(2)}, u32[]{:S(2)}) collective-permute-start(f32[512,128]{1,0:T(8,128)S(1)} %get-tuple-element.77), channel_id=1, source_target_pairs={{0,4},{4,0},{8,12},{12,8},{16,20},{20,16},{24,28},{28,24},{1,5},{5... | collective-permute-start | bytes 786440 | tf_op jit(solution)/shard_map/ppermute | solution.py:480
  15.0 0.5 %collective-permute-done.1 = f32[512,128]{1,0:T(8,128)S(1)} collective-permute-done((f32[512,128]{1,0:T(8,128)S(1)}, f32[512,128]{1,0:T(8,128)S(1)}, u32[]{:S(2)}, u32[]{:S(2)}) %collective-permute-start.1) | collective-permute-done | bytes 262176 | tf_op jit(solution)/shard_map/ppermute | solution.py:431
  15.5 0.1 multiply_add_fusion
  15.6 1.5 %collective-permute-start.3 = (f32[512,128]{1,0:T(8,128)S(1)}, f32[512,128]{1,0:T(8,128)S(1)}, u32[]{:S(2)}, u32[]{:S(2)}) collective-permute-start(f32[512,128]{1,0:T(8,128)S(1)} %get-tuple-element.76.refs_0_), channel_id=1, source_target_pairs={{0,20},{4,8},{8,28},{12,0},{16,4},{20,24},{24,12},{28,16},{1,21},{... | collective-permute-start | bytes 786440 | tf_op jit(solution)/shard_map/ppermute | solution.py:437
  17.1 0.8 %collective-permute-start.7 = (f32[512,128]{1,0:T(8,128)S(1)}, f32[512,128]{1,0:T(8,128)S(1)}, u32[]{:S(2)}, u32[]{:S(2)}) collective-permute-start(f32[512,128]{1,0:T(8,128)S(1)} %get-tuple-element.75), channel_id=1, source_target_pairs={{0,4},{4,0},{8,12},{12,8},{16,20},{20,16},{24,28},{28,24},{1,5},{5... | collective-permute-start | bytes 786440 | tf_op jit(solution)/shard_map/ppermute | solution.py:480
  18.0 1.5 %inner.4 = (f32[1024,512]{1,0:T(8,128)S(1)}, f32[1,128]{1,0:T(1,128)S(1)}) custom-call(f32[512,128]{1,0:T(8,128)S(1)} %get-tuple-element.76.refs_0_, bf16[1024,1024]{1,0:T(8,128)(2,1)S(1)} %get-tuple-element.52.refs_1_.refs_0_, bf16[1024,1024]{1,0:T(8,128)(2,1)S(1)} %get-tuple-element.53.refs_2_, bf16[1024,1024]{1,0:T(8,128)(2,1)S(1)} %get-tuple-element.54.refs_3_, ...), custom_call_target="tpu_custom_call" | custom-call | flops 805306368 | bytes 6291456 | tf_op jit(solution)/shard_map/inner/pallas_call | solution.py:282
  19.5 0.1 collective-permute-start.8
  19.6 1.5 %inner.5 = (f32[1024,512]{1,0:T(8,128)S(1)}, f32[1,128]{1,0:T(1,128)S(1)}) custom-call(f32[512,128]{1,0:T(8,128)S(1)} %broadcast_add_fusion.refs_0_.after_ref, bf16[1024,1024]{1,0:T(8,128)(2,1)S(1)} %get-tuple-element.52.refs_1_.refs_0_, bf16[1024,1024]{1,0:T(8,128)(2,1)S(1)} %get-tuple-element.53.refs_2_, bf16[1024,1024]{1,0:T(8,128)(2,1)S(1)} %get-tuple-element.54.refs_3_, ...), custom_call_target="tpu_custom_call" | custom-call | flops 805306368 | bytes 6291456 | tf_op jit(solution)/shard_map/inner/pallas_call | solution.py:282
  21.1 0.5 %mix.4 = (f32[1024,512]{1,0:T(8,128)S(1)}, f32[1024,128]{1,0:T(8,128)S(1)}) custom-call(bf16[1024,1024]{1,0:T(8,128)(2,1)S(1)} %get-tuple-element.52.refs_1_.refs_0_, f32[1024,512]{1,0:T(8,128)S(1)} %get-tuple-element.57.refs_1_, f32[512,128]{1,0:T(8,128)S(1)} %add_add_fusion.3.refs_2_), custom_call_target="tpu_custom_call" | custom-call | flops 134217728 | bytes 6291456 | tf_op jit(solution)/shard_map/mix/pallas_call | solution.py:316
  21.7 0.6 %collective-permute-start.6 = (f32[512,128]{1,0:T(8,128)S(1)}, f32[512,128]{1,0:T(8,128)S(1)}, u32[]{:S(2)}, u32[]{:S(2)}) collective-permute-start(f32[512,128]{1,0:T(8,128)S(1)} %add_add_fusion.4.after_ref), channel_id=1, source_target_pairs={{0,4},{4,0},{8,12},{12,8},{16,20},{20,16},{24,28},{28,24},{1,5},{5... | collective-permute-start | bytes 786440 | tf_op jit(solution)/shard_map/ppermute | solution.py:488
  22.3 0.5 %mix.5 = (f32[1024,512]{1,0:T(8,128)S(1)}, f32[1024,128]{1,0:T(8,128)S(1)}) custom-call(bf16[256,1024]{1,0:T(8,128)(2,1)S(1)} %get-tuple-element.41.first_queries.refs_0_, bf16[768,1024]{1,0:T(8,128)(2,1)S(1)} %get-tuple-element.47.refs_1_, f32[1024,512]{1,0:T(8,128)S(1)} %get-tuple-element.61.refs_2_, f32[512,128]{1,0:T(8,128)S(1)} %add_add_fusion.refs_3_, ...), custom_call_target="tpu_custom_call" | custom-call | flops 134217728 | bytes 6291456 | tf_op jit(solution)/shard_map/mix/pallas_call | solution.py:316
  22.9 0.5 %mix.6 = (f32[1024,512]{1,0:T(8,128)S(1)}, f32[1024,128]{1,0:T(8,128)S(1)}) custom-call(bf16[1024,1024]{1,0:T(8,128)(2,1)S(1)} %get-tuple-element.52.refs_1_.refs_0_, f32[1024,512]{1,0:T(8,128)S(1)} %get-tuple-element.60.refs_1_, f32[512,128]{1,0:T(8,128)S(1)} %add_add_fusion.1.refs_2_, f32[1024,128]{1,0:T(8,128)S(1)} %get-tuple-element.62.after_ref.refs_3_), custom_call_target="tpu_custom_call" | custom-call | flops 134217728 | bytes 6291456 | tf_op jit(solution)/shard_map/mix/pallas_call | solution.py:316
  23.3 0.1 collective-permute-done.6
  23.4 0.1 add_add_fusion.2.refs_3_
  23.5 0.6 %mix.7 = (f32[1024,512]{1,0:T(8,128)S(1)}, f32[1,1024]{1,0:T(1,128)S(1)}) custom-call(bf16[256,1024]{1,0:T(8,128)(2,1)S(1)} %get-tuple-element.41.first_queries.refs_0_, bf16[768,1024]{1,0:T(8,128)(2,1)S(1)} %get-tuple-element.47.refs_1_, f32[1024,512]{1,0:T(8,128)S(1)} %get-tuple-element.48.refs_2_, f32[512,128]{1,0:T(8,128)S(1)} %add_add_fusion.2.refs_3_, ...), custom_call_target="tpu_custom_call" | custom-call | flops 134217728 | bytes 6291456 | tf_op jit(solution)/shard_map/mix/pallas_call | solution.py:316
  24.1 0.4 %collective-permute-start.10 = (f32[1,1024]{1,0:T(1,128)S(1)}, f32[1,1024]{1,0:T(1,128)S(1)}, u32[]{:S(2)}, u32[]{:S(2)}) collective-permute-start(f32[1,1024]{1,0:T(1,128)S(1)} %get-tuple-element.64.refs_3_), channel_id=1, source_target_pairs={{0,4},{4,0},{8,12},{12,8},{16,20},{20,16},{24,28},{28,24},{1,5},{5... | collective-permute-start | bytes 12296 | tf_op jit(solution)/shard_map/ppermute | solution.py:512
  24.5 1.7 %collective-permute-start.9 = (f32[1,1024]{1,0:T(1,128)S(1)}, f32[1,1024]{1,0:T(1,128)S(1)}, u32[]{:S(2)}, u32[]{:S(2)}) collective-permute-start(f32[1,1024]{1,0:T(1,128)S(1)} %get-tuple-element.64.refs_3_), channel_id=1, source_target_pairs={{0,5},{1,4},{2,7},{3,6},{4,1},{5,0},{6,3},{7,2},{8,13},{9,12},{10,... | collective-permute-start | bytes 12296 | tf_op jit(solution)/shard_map/ppermute | solution.py:512
  26.2 1.0 %gate.2 = (f32[1024,1024]{1,0:T(8,128)S(1)}, f32[1,1024]{1,0:T(1,128)S(1)}) custom-call(s32[1]{0:T(128)} %bitcast.place_ref.refs_0_, bf16[1024,2048]{1,0:T(8,128)(2,1)S(1)} %copy-done, f32[1,2048]{1,0:T(1,128)S(1)} %bitcast.21, f32[1,1024]{1,0:T(1,128)S(1)} %get-tuple-element.64.refs_3_, f32[1024,512]{1,0:T(8,128)S(1)} %get-tuple-element.65.refs_4_, ...), custom_call_target="tpu_custom_call" | custom-call | flops 16777216 | bytes 4194304 | tf_op jit(solution)/shard_map/gate/pallas_call | solution.py:351
  27.3 0.3 collective-permute-done.9
  27.6 2.8 %collective-permute-start.11 = (f32[1,1024]{1,0:T(1,128)S(1)}, f32[1,1024]{1,0:T(1,128)S(1)}, u32[]{:S(2)}, u32[]{:S(2)}) collective-permute-start(f32[1,1024]{1,0:T(1,128)S(1)} %add_add_fusion.8.refs_3_), channel_id=1, source_target_pairs={{0,6},{1,7},{2,4},{3,5},{4,2},{5,3},{6,0},{7,1},{8,14},{9,15},{10,... | collective-permute-start | bytes 12296 | tf_op jit(solution)/shard_map/ppermute | solution.py:512
  30.3 0.2 collective-permute-start.12
  30.5 1.1 %gate.3 = (f32[1024,1024]{1,0:T(8,128)S(1)}, f32[1,1024]{1,0:T(1,128)S(1)}) custom-call(s32[1]{0:T(128)} %bitcast.place_ref.refs_0_, bf16[1024,2048]{1,0:T(8,128)(2,1)S(1)} %copy-done, f32[1,2048]{1,0:T(1,128)S(1)} %bitcast.22, f32[1,1024]{1,0:T(1,128)S(1)} %add_add_fusion.8.refs_3_, f32[1024,512]{1,0:T(8,128)S(1)} %get-tuple-element.68.refs_4_, ...), custom_call_target="tpu_custom_call" | custom-call | flops 16777216 | bytes 4194304 | tf_op jit(solution)/shard_map/gate/pallas_call | solution.py:351
  31.7 2.4 %scale.1 = bf16[1024,2048]{1,0:T(8,128)(2,1)} custom-call(s32[1]{0:T(128)} %bitcast.place_ref.refs_0_, f32[1024,1024]{1,0:T(8,128)S(1)} %get-tuple-element.70.refs_1_, f32[1024,1024]{1,0:T(8,128)S(1)} %get-tuple-element.71.refs_2_, f32[1,1024]{1,0:T(1,128)S(1)} %add_add_fusion.7.refs_3_), custom_call_target="tpu_custom_call" | custom-call | flops 4194304 | bytes 4194304 | tf_op jit(solution)/shard_map/scale/pallas_call | solution.py:382
  (29 shorter events, 0.4 us)
Async XLA Ops:
  2.9 2.8 %collective-permute-start = (f32[1024,128]{1,0:T(8,128)S(1)}, f32[1024,128]{1,0:T(8,128)S(1)}, u32[]{:S(2)}, u32[]{:S(2)}) collective-permute-start(f32[1024,128]{1,0:T(8,128)S(1)} %get-tuple-element.43), channel_id=1, source_target_pairs={{0,4},{4,0},{8,12},{12,8},{16,20},{20,16},{24,28},{28,24},{1,5},{5... | collective-permute-start | bytes 1572872 | tf_op jit(solution)/shard_map/ppermute | solution.py:452
  5.8 6.9 %collective-permute-start.2 = (f32[512,128]{1,0:T(8,128)S(1)}, f32[512,128]{1,0:T(8,128)S(1)}, u32[]{:S(2)}, u32[]{:S(2)}) collective-permute-start(f32[512,128]{1,0:T(8,128)S(1)} %get-tuple-element.74.after_ref), channel_id=1, source_target_pairs={{0,8},{4,20},{8,0},{12,28},{16,24},{20,4},{24,16},{28,12},{1,9},{5... | collective-permute-start | bytes 786440 | tf_op jit(solution)/shard_map/ppermute | solution.py:431
  8.4 7.2 %collective-permute-start.1 = (f32[512,128]{1,0:T(8,128)S(1)}, f32[512,128]{1,0:T(8,128)S(1)}, u32[]{:S(2)}, u32[]{:S(2)}) collective-permute-start(f32[512,128]{1,0:T(8,128)S(1)} %get-tuple-element.73), channel_id=1, source_target_pairs={{0,8},{4,20},{8,0},{12,28},{16,24},{20,4},{24,16},{28,12},{1,9},{5... | collective-permute-start | bytes 786440 | tf_op jit(solution)/shard_map/ppermute | solution.py:431
  12.8 6.6 %collective-permute-start.5 = (f32[512,128]{1,0:T(8,128)S(1)}, f32[512,128]{1,0:T(8,128)S(1)}, u32[]{:S(2)}, u32[]{:S(2)}) collective-permute-start(f32[512,128]{1,0:T(8,128)S(1)} %get-tuple-element.78.after_ref), channel_id=1, source_target_pairs={{0,20},{4,8},{8,28},{12,0},{16,4},{20,24},{24,12},{28,16},{1,21},{... | collective-permute-start | bytes 786440 | tf_op jit(solution)/shard_map/ppermute | solution.py:437
  14.2 6.9 %collective-permute-start.4 = (f32[512,128]{1,0:T(8,128)S(1)}, f32[512,128]{1,0:T(8,128)S(1)}, u32[]{:S(2)}, u32[]{:S(2)}) collective-permute-start(f32[512,128]{1,0:T(8,128)S(1)} %get-tuple-element.77), channel_id=1, source_target_pairs={{0,4},{4,0},{8,12},{12,8},{16,20},{20,16},{24,28},{28,24},{1,5},{5... | collective-permute-start | bytes 786440 | tf_op jit(solution)/shard_map/ppermute | solution.py:480
  15.6 6.0 %collective-permute-start.3 = (f32[512,128]{1,0:T(8,128)S(1)}, f32[512,128]{1,0:T(8,128)S(1)}, u32[]{:S(2)}, u32[]{:S(2)}) collective-permute-start(f32[512,128]{1,0:T(8,128)S(1)} %get-tuple-element.76.refs_0_), channel_id=1, source_target_pairs={{0,20},{4,8},{8,28},{12,0},{16,4},{20,24},{24,12},{28,16},{1,21},{... | collective-permute-start | bytes 786440 | tf_op jit(solution)/shard_map/ppermute | solution.py:437
  17.1 5.7 %collective-permute-start.7 = (f32[512,128]{1,0:T(8,128)S(1)}, f32[512,128]{1,0:T(8,128)S(1)}, u32[]{:S(2)}, u32[]{:S(2)}) collective-permute-start(f32[512,128]{1,0:T(8,128)S(1)} %get-tuple-element.75), channel_id=1, source_target_pairs={{0,4},{4,0},{8,12},{12,8},{16,20},{20,16},{24,28},{28,24},{1,5},{5... | collective-permute-start | bytes 786440 | tf_op jit(solution)/shard_map/ppermute | solution.py:480
  19.5 2.7 %collective-permute-start.8 = (f32[512,128]{1,0:T(8,128)S(1)}, f32[512,128]{1,0:T(8,128)S(1)}, u32[]{:S(2)}, u32[]{:S(2)}) collective-permute-start(f32[512,128]{1,0:T(8,128)S(1)} %broadcast_add_fusion.refs_0_.after_ref), channel_id=1, source_target_pairs={{0,4},{4,0},{8,12},{12,8},{16,20},{20,16},{24,28},{28,24},{1,5},{5... | collective-permute-start | bytes 786440 | tf_op jit(solution)/shard_map/ppermute | solution.py:488
  21.7 1.7 %collective-permute-start.6 = (f32[512,128]{1,0:T(8,128)S(1)}, f32[512,128]{1,0:T(8,128)S(1)}, u32[]{:S(2)}, u32[]{:S(2)}) collective-permute-start(f32[512,128]{1,0:T(8,128)S(1)} %add_add_fusion.4.after_ref), channel_id=1, source_target_pairs={{0,4},{4,0},{8,12},{12,8},{16,20},{20,16},{24,28},{28,24},{1,5},{5... | collective-permute-start | bytes 786440 | tf_op jit(solution)/shard_map/ppermute | solution.py:488
  23.5 2.7 %copy-start = (bf16[1024,2048]{1,0:T(8,128)(2,1)S(1)}, bf16[1024,2048]{1,0:T(8,128)(2,1)}, u32[]{:S(2)}) copy-start(bf16[1024,2048]{1,0:T(8,128)(2,1)} %refs_1_.3) | copy-start | bytes 12582916
  23.5 2.7 %copy-start.1 = (f32[2048]{0:T(1024)S(1)}, f32[2048]{0:T(1024)}, u32[]{:S(2)}) copy-start(f32[2048]{0:T(1024)} %param.10) | copy-start | bytes 24580
  24.1 3.2 %collective-permute-start.10 = (f32[1,1024]{1,0:T(1,128)S(1)}, f32[1,1024]{1,0:T(1,128)S(1)}, u32[]{:S(2)}, u32[]{:S(2)}) collective-permute-start(f32[1,1024]{1,0:T(1,128)S(1)} %get-tuple-element.64.refs_3_), channel_id=1, source_target_pairs={{0,4},{4,0},{8,12},{12,8},{16,20},{20,16},{24,28},{28,24},{1,5},{5... | collective-permute-start | bytes 12296 | tf_op jit(solution)/shard_map/ppermute | solution.py:512
  24.5 3.1 %collective-permute-start.9 = (f32[1,1024]{1,0:T(1,128)S(1)}, f32[1,1024]{1,0:T(1,128)S(1)}, u32[]{:S(2)}, u32[]{:S(2)}) collective-permute-start(f32[1,1024]{1,0:T(1,128)S(1)} %get-tuple-element.64.refs_3_), channel_id=1, source_target_pairs={{0,5},{1,4},{2,7},{3,6},{4,1},{5,0},{6,3},{7,2},{8,13},{9,12},{10,... | collective-permute-start | bytes 12296 | tf_op jit(solution)/shard_map/ppermute | solution.py:512
  27.6 4.1 %collective-permute-start.11 = (f32[1,1024]{1,0:T(1,128)S(1)}, f32[1,1024]{1,0:T(1,128)S(1)}, u32[]{:S(2)}, u32[]{:S(2)}) collective-permute-start(f32[1,1024]{1,0:T(1,128)S(1)} %add_add_fusion.8.refs_3_), channel_id=1, source_target_pairs={{0,6},{1,7},{2,4},{3,5},{4,2},{5,3},{6,0},{7,1},{8,14},{9,15},{10,... | collective-permute-start | bytes 12296 | tf_op jit(solution)/shard_map/ppermute | solution.py:512
  30.3 1.3 %collective-permute-start.12 = (f32[1,1024]{1,0:T(1,128)S(1)}, f32[1,1024]{1,0:T(1,128)S(1)}, u32[]{:S(2)}, u32[]{:S(2)}) collective-permute-start(f32[1,1024]{1,0:T(1,128)S(1)} %add_add_fusion.8.refs_3_), channel_id=1, source_target_pairs={{0,4},{4,0},{8,12},{12,8},{16,20},{20,16},{24,28},{28,24},{1,5},{5... | collective-permute-start | bytes 12296 | tf_op jit(solution)/shard_map/ppermute | solution.py:512
